TPU v7x, 128 devices: a whole 4x4x4 slice. The times are simulated.
128 devices in a mesh: dp: 64 (over z, x, y), seq: 2 (over core).
Axes of the slice: x: 4, y: 4, z: 4, core: 2. Of those that a mesh axis runs over, the one named last changes fastest.
Arguments:
- hidden_in: bfloat16 [64, 512, 768], P('dp', 'seq'), may hold values from -6 to 6
- segments: int32 [64, 512], P('dp'), may hold values from 0 to 2, as said below
- projection_in: bfloat16 [2, 768, 3352], P(None, ('dp', 'seq')), may hold values from -0.21875 to 0.21875
- projection_out: bfloat16 [2, 1536, 768], P(None, ('dp', 'seq')), may hold values from -0.15625 to 0.15625
- kernel_weight: bfloat16 [2, 4, 1792], P(None, None, ('dp', 'seq')), may hold values from -3 to 3
- kernel_bias: bfloat16 [2, 1792], P(None, ('dp', 'seq')), may hold values from -3 to 3
- norm_gain: bfloat16 [2, 768], P(None, ('dp', 'seq')), may hold values from 0.099609375 to 1.8984375
- gate_gain: bfloat16 [2, 1536], P(None, ('dp', 'seq')), may hold values from 0.099609375 to 1.8984375
- head_values: float32 [2, 3, 24], replicated, may hold values from -9.3 to 1.5, as said below
- cotangent: bfloat16 [64, 512, 768], P('dp', 'seq'), may hold values from -6 to 6
Outputs:
- hidden_out: bfloat16 [64, 512, 768], P('dp', 'seq')
- input_gradient: bfloat16 [64, 512, 768], P('dp', 'seq')
- projection_in_gradient: float32 [2, 768, 3352], P(None, ('dp', 'seq'))
- projection_out_gradient: float32 [2, 1536, 768], P(None, ('dp', 'seq'))
- kernel_weight_gradient: float32 [2, 4, 1792], P(None, None, ('dp', 'seq'))
- kernel_bias_gradient: float32 [2, 1792], P(None, ('dp', 'seq'))
- norm_gain_gradient: float32 [2, 768], P(None, ('dp', 'seq'))
- gate_gain_gradient: float32 [2, 1536], P(None, ('dp', 'seq'))
- head_values_gradient: float32 [2, 3, 24], replicated
Inputs may be any that keep to these rules, and one draw needn't show every extreme that they name: Segment numbers never fall along a row and each row holds segments 0, 1 and 2; segment 1 reaches from the row's first block of 256 positions into its last. `head_values`: row 0 of a layer holds inverse softplus values of positive steps, row 1 logarithms of decay rates, row 2 skip gains.
All inputs are finite; a program needn't handle non-finite values.
Results may differ from a plain program's by a relative error of at most 0.012.
Values may be sent and summed in bfloat16 or wider, within the bound.
No kernel may reach another device: no remote copies, remote signals or barrier semaphores. Data moves between devices by JAX's collectives and lax.ppermute only.
A program may use at most 256 MiB of HBM per device.

v0:
```python
from functools import partial
import functools

import jax
import jax.numpy as jnp
from jax import lax
from jax.sharding import Mesh
from jax.sharding import PartitionSpec as P

HEADS = 24
HEAD_DIM = 64
STATE = 128
INNER = 1536
CONV_CH = 1792
DP_SEQ = ("dp_0", "dp_1", "dp_2", "seq")
DP = ("dp_0", "dp_1", "dp_2")


norm_eps = 1e-05
highest = lax.Precision.HIGHEST


def passed_along(block, axis, distance):
    devices = range(lax.axis_size(axis))
    route = [(i - distance, i) for i in devices if i - distance in devices]
    return lax.ppermute(block, axis, route)


def entering(array, axis, join, neutral):
    place = lax.axis_index(axis)
    gathered = jax.tree.map(
        lambda a, kind: lax.all_gather(a.astype(kind), axis), array, (jnp.bfloat16, jnp.bfloat16)
    )
    state = jax.tree.map(lambda a, e: jnp.zeros_like(a) + jnp.asarray(e, a.dtype), array, neutral)

    def entering_one(turn, state):
        return join(
            state,
            jax.tree.map(
                lambda a, own: lax.dynamic_index_in_dim(a, turn, 0, False).astype(own.dtype),
                gathered,
                array,
            ),
        )

    return lax.fori_loop(0, place, entering_one, state)


def carried_in(array, axis, join, neutral):
    count = lax.axis_size(axis)
    place = lax.axis_index(axis)
    ahead = count - 1 - place
    gathered = jax.tree.map(
        lambda a, kind: lax.all_gather(a.astype(kind), axis),
        array,
        jax.tree.map(lambda a: jnp.bfloat16 if a.dtype == jnp.float32 else a.dtype, array),
    )
    state = jax.tree.map(lambda a, e: jnp.zeros_like(a) + jnp.asarray(e, a.dtype), array, neutral)

    def carried_one(turn, state):
        source = count - 1 - turn
        return join(
            state,
            jax.tree.map(
                lambda a, own: lax.dynamic_index_in_dim(a, source, 0, False).astype(own.dtype),
                gathered,
                array,
            ),
        )

    return lax.fori_loop(0, ahead, carried_one, state)


def over_axes(array, axes):
    return functools.reduce(lax.psum, axes, array)


def rms_scale(values, gain):
    return values * lax.rsqrt(jnp.mean(values * values, axis=-1, keepdims=True) + norm_eps) * gain


def chain_ahead(earlier, later):
    return (earlier[0] * later[0], later[0][..., None, None] * earlier[1] + later[1])


def chain_behind(earlier, later):
    return (later[0] * earlier[0], later[1] + later[0][..., None, None] * earlier[1])


def local_mixer(projected, tail_rows, kernel_weights, kernel_offset, head_layer, segment_pad):
    row_count, block_size = (projected.shape[0], projected.shape[1])
    kernel_size = kernel_weights.shape[0]
    signal = projected[..., INNER : INNER + CONV_CH]
    extended = jnp.concatenate([tail_rows, signal], axis=1)
    segment_own = segment_pad[:, kernel_size - 1 :]
    summed = jnp.zeros_like(signal)
    for offset in range(kernel_size):
        same_segment = (segment_pad[:, offset : offset + block_size] == segment_own).astype(
            jnp.float32
        )
        summed = (
            summed
            + kernel_weights[offset]
            * extended[:, offset : offset + block_size]
            * same_segment[..., None]
        )
    active = jax.nn.silu(summed + kernel_offset)
    inputs = active[..., :INNER].reshape(row_count, block_size, HEADS, HEAD_DIM)
    writers = active[..., INNER : INNER + STATE]
    readers = active[..., INNER + STATE :]
    step_size = jax.nn.softplus(projected[..., INNER + CONV_CH :] + head_layer[0])
    cumul_rate = jnp.cumsum(-step_size * jnp.exp(head_layer[1]), axis=1)
    cumul_heads = jnp.swapaxes(cumul_rate, 1, 2)
    position = jnp.arange(block_size)
    allowed = (position[:, None] >= position[None, :])[None] & (
        segment_own[:, :, None] == segment_own[:, None, :]
    )
    allowed = allowed[:, None]
    spread = cumul_heads[:, :, :, None] - cumul_heads[:, :, None, :]
    decay_matrix = jnp.where(allowed, jnp.exp(jnp.where(allowed, spread, 0.0)), 0.0)
    affinity = jnp.einsum("rtn,rsn->rts", readers, writers, precision=highest)
    scaled = inputs * step_size[..., None]
    local_out = jnp.einsum(
        "rhts,rshp->rthp", decay_matrix * affinity[:, None], scaled, precision=highest
    )
    local_out = local_out + head_layer[2][:, None] * inputs
    segment_prev = segment_pad[:, kernel_size - 2]
    carry_in = (segment_own == segment_prev[:, None]).astype(jnp.float32)
    inflow = jnp.exp(cumul_rate) * carry_in[..., None]
    segment_last = segment_own[:, -1]
    keep_mask = (segment_own == segment_last[:, None]).astype(jnp.float32)
    outflow = jnp.exp(cumul_rate[:, -1:, :] - cumul_rate) * keep_mask[..., None]
    state_part = jnp.einsum(
        "rthp,rtn->rhpn", scaled * outflow[..., None], writers, precision=highest
    )
    decay_part = (
        jnp.exp(cumul_rate[:, -1, :]) * (segment_last == segment_prev).astype(jnp.float32)[:, None]
    )
    return (local_out, readers, inflow, state_part, decay_part)


def local_gate(local_out, readers, inflow, gate_in, incoming, gate_scale):
    total_out = (
        local_out
        + jnp.einsum("rtn,rhpn->rthp", readers, incoming, precision=highest) * inflow[..., None]
    )
    gated_out = total_out.reshape(gate_in.shape) * jax.nn.silu(gate_in)
    return rms_scale(gated_out, gate_scale)


def per_device(
    hidden_in,
    segments,
    projection_in,
    projection_out,
    kernel_weight,
    kernel_bias,
    norm_gain,
    gate_gain,
    head_values,
    cotangent,
):
    layer_count = projection_in.shape[0]
    row_count, block_size = (hidden_in.shape[0], hidden_in.shape[1])
    kernel_size = kernel_weight.shape[1]
    begin_at = lax.axis_index("seq") * block_size
    segment_full = jnp.pad(segments, ((0, 0), (kernel_size - 1, 0)), constant_values=-1)
    segment_pad = lax.dynamic_slice_in_dim(segment_full, begin_at, block_size + kernel_size - 1, 1)
    unit_factor = jnp.ones((row_count, HEADS), jnp.float32)
    empty_state = jnp.zeros((row_count, HEADS, HEAD_DIM, STATE), jnp.float32)
    mixer_local = partial(local_mixer, segment_pad=segment_pad)
    tail_start = block_size - kernel_size + 1
    saved_list = []
    current = hidden_in.astype(jnp.float32)
    for layer_index in range(layer_count):
        gathered = (
            lax.all_gather(projection_in[layer_index], DP_SEQ, axis=0, tiled=True),
            lax.all_gather(projection_out[layer_index], DP_SEQ, axis=0, tiled=True),
            lax.all_gather(kernel_weight[layer_index], DP_SEQ, axis=1, tiled=True),
            lax.all_gather(kernel_bias[layer_index], DP_SEQ, axis=0, tiled=True),
            lax.all_gather(norm_gain[layer_index], DP_SEQ, axis=0, tiled=True),
            lax.all_gather(gate_gain[layer_index], DP_SEQ, axis=0, tiled=True),
        )
        weight_in, weight_out = (gathered[0], gathered[1])
        kernel_weights, kernel_offset, norm_scale, gate_scale = tuple(
            (member.astype(jnp.float32) for member in gathered[2:])
        )
        head_layer = head_values[layer_index]
        normed, norm_back = jax.vjp(rms_scale, current, norm_scale)
        normed_low = normed.astype(jnp.bfloat16)
        projected = jnp.einsum(
            "rtd,dp->rtp", normed_low, weight_in, preferred_element_type=jnp.float32
        )
        tail_rows = passed_along(projected[:, tail_start:, INNER : INNER + CONV_CH], "seq", 1)
        mixer_out, mixer_back = jax.vjp(
            mixer_local, projected, tail_rows, kernel_weights, kernel_offset, head_layer
        )
        local_out, readers, inflow, state_part, decay_part = mixer_out
        incoming = entering(
            (decay_part, state_part), "seq", chain_ahead, (unit_factor, empty_state)
        )[1]
        gate_out, gate_back = jax.vjp(
            local_gate, local_out, readers, inflow, projected[..., :INNER], incoming, gate_scale
        )
        gate_low = gate_out.astype(jnp.bfloat16)
        current = current + jnp.einsum(
            "rte,ed->rtd", gate_low, weight_out, preferred_element_type=jnp.float32
        )
        kept_pair = None
        saved_list.append(
            (
                norm_back,
                normed_low,
                mixer_back,
                decay_part,
                incoming,
                gate_back,
                gate_low,
                kept_pair,
            )
        )
    upstream = cotangent.astype(jnp.float32)
    sums_kept = []
    head_backs = []
    for layer_index in reversed(range(layer_count)):
        norm_back, normed_low, mixer_back, decay_part, incoming, gate_back, gate_low, kept_pair = (
            saved_list[layer_index]
        )
        weight_in, weight_out = (
            lax.all_gather(projection_in[layer_index], DP_SEQ, axis=0, tiled=True),
            lax.all_gather(projection_out[layer_index], DP_SEQ, axis=0, tiled=True),
        )
        upstream_low = upstream.astype(jnp.bfloat16)
        weight_out_back = jnp.einsum(
            "rte,rtd->ed", gate_low, upstream_low, preferred_element_type=jnp.float32
        )
        gate_seed = jnp.einsum(
            "rtd,ed->rte", upstream_low, weight_out, preferred_element_type=jnp.float32
        )
        back_local, back_readers, back_inflow, back_gate_in, back_incoming, back_gate_scale = (
            gate_back(gate_seed)
        )
        later_state = carried_in(
            (decay_part, back_incoming), "seq", chain_behind, (unit_factor, empty_state)
        )[1]
        back_decay = jnp.sum(later_state * incoming, axis=(2, 3))
        back_projected, back_tail, back_kernel_weights, back_kernel_offset, back_heads = mixer_back(
            (back_local, back_readers, back_inflow, later_state, back_decay)
        )
        tail_arrived = passed_along(back_tail, "seq", -1)
        back_projected = jnp.concatenate([back_gate_in, back_projected[..., INNER:]], axis=-1)
        back_projected = back_projected.at[:, tail_start:, INNER : INNER + CONV_CH].add(
            tail_arrived
        )
        projected_low = back_projected.astype(jnp.bfloat16)
        weight_in_back = jnp.einsum(
            "rtd,rtp->dp", normed_low, projected_low, preferred_element_type=jnp.float32
        )
        back_normed = jnp.einsum(
            "rtp,dp->rtd", projected_low, weight_in, preferred_element_type=jnp.float32
        )
        back_current, back_norm_scale = norm_back(back_normed)
        upstream = upstream + back_current
        layer_sums = (
            weight_in_back,
            weight_out_back,
            back_kernel_weights,
            back_kernel_offset,
            back_norm_scale,
            back_gate_scale,
        )
        sums_kept.append(layer_sums)
        head_backs.append(back_heads)
    sums_kept = sums_kept[::-1]
    head_backs = head_backs[::-1]
    stacked = tuple(
        (jnp.stack([entry_set[slot_index] for entry_set in sums_kept]) for slot_index in range(6))
    )
    stacked = (
        lax.psum_scatter(stacked[0], DP_SEQ, scatter_dimension=1, tiled=True),
        lax.psum_scatter(stacked[1], DP_SEQ, scatter_dimension=1, tiled=True),
        lax.psum_scatter(stacked[2], DP_SEQ, scatter_dimension=2, tiled=True),
        lax.psum_scatter(stacked[3], DP_SEQ, scatter_dimension=1, tiled=True),
        lax.psum_scatter(stacked[4], DP_SEQ, scatter_dimension=1, tiled=True),
        lax.psum_scatter(stacked[5], DP_SEQ, scatter_dimension=1, tiled=True),
    )
    head_total = over_axes(jnp.stack(head_backs), DP_SEQ)
    return (
        (current.astype(jnp.bfloat16), upstream.astype(jnp.bfloat16))
        + tuple(stacked)
        + (head_total,)
    )


def solution(mesh):
    torus = Mesh(mesh.devices.reshape(4, 4, 4, mesh.shape["seq"]), ("dp_0", "dp_1", "dp_2", "seq"))
    return jax.shard_map(
        per_device,
        mesh=torus,
        in_specs=(
            P(DP, "seq", None),
            P(DP, None),
            P(None, DP_SEQ, None),
            P(None, DP_SEQ, None),
            P(None, None, DP_SEQ),
            P(None, DP_SEQ),
            P(None, DP_SEQ),
            P(None, DP_SEQ),
            P(),
            P(DP, "seq", None),
        ),
        out_specs=(
            P(DP, "seq", None),
            P(DP, "seq", None),
            P(None, DP_SEQ, None),
            P(None, DP_SEQ, None),
            P(None, None, DP_SEQ),
            P(None, DP_SEQ),
            P(None, DP_SEQ),
            P(None, DP_SEQ),
            P(),
        ),
        check_vma=False,
    )
```

profile of v0, /device:TPU:1, one launch (start us, length us, event | category | flops | bytes accessed | tf_op | source)
XLA Modules:
  0.0 1015.5 jit_solution(4127382113530880742)
XLA Ops:
  22.0 69.7 %all-reduce.51 = (bf16[768]{0:T(1024)(128)(2,1)S(1)}, bf16[1792]{0:T(1024)(128)(2,1)S(1)}, bf16[1536]{0:T(1024)(128)(2,1)S(1)}, bf16[768]{0:T(1024)(128)(2,1)S(1...) all-reduce(bf16[768]{0:T(1024)(128)(2,1)S(1)} %dynamic-update-slice, ...), channel_id=3, replica_groups=mesh['dp_0'=4,'dp_1'=4,'dp_2'=4,'seq'=2] {'dp_0','dp_1','dp_2','seq'}, use_global_device_ids=true, to_apply=%add.37 | all-reduce | flops 8192 | bytes 32768
  95.9 35.8 %all-gather = bf16[1,4,1792]{1,0,2:T(2,128)(2,1)S(1)} all-gather(bf16[1,4,14]{1,0,2:T(2,128)(2,1)S(1)} %copy.497), channel_id=2, replica_groups=mesh['dp_0'=4,'dp_1'=4,'dp_2'=4,'seq'=2] {'dp_0','dp_1','dp_2','seq'}, dimensions={2}, use_global_device_ids=true | all-gather | bytes 14448 | tf_op jit(solution)/shard_map/all_gather | solution.py:179
  132.9 37.7 %slice_reduce_fusion.7 = (f32[1792]{0:T(1024)}, f32[1792]{0:T(1024)}, f32[1792]{0:T(1024)}, f32[1792]{0:T(1024)}) fusion(f32[1,4,1792]{1,0,2:T(1,128)S(1)} %convert_element_type.264), kind=kLoop, calls=%fused_computation.224 | loop fusion | bytes 57344 | tf_op jit(solution)/shard_map/jvp()/slice | solution.py:103
  170.7 34.5 %all-gather.7 = bf16[1,4,1792]{1,0,2:T(2,128)(2,1)S(1)} all-gather(bf16[1,4,14]{1,0,2:T(2,128)(2,1)S(1)} %copy.498), channel_id=9, replica_groups=mesh['dp_0'=4,'dp_1'=4,'dp_2'=4,'seq'=2] {'dp_0','dp_1','dp_2','seq'}, dimensions={2}, use_global_device_ids=true | all-gather | bytes 14448 | tf_op jit(solution)/shard_map/all_gather | solution.py:179
  206.6 37.8 %slice_reduce_fusion.3 = (f32[1792]{0:T(1024)}, f32[1792]{0:T(1024)}, f32[1792]{0:T(1024)}, f32[1792]{0:T(1024)}) fusion(f32[1,4,1792]{1,0,2:T(1,128)S(1)} %convert_element_type.268), kind=kLoop, calls=%fused_computation.220 | loop fusion | bytes 57344 | tf_op jit(solution)/shard_map/jvp()/slice | solution.py:103
  245.7 23.4 %copy.393 = bf16[1,768,3352]{1,2,0:T(8,128)(2,1)} copy(bf16[1,768,3352]{2,0,1:T(2,128)(2,1)} %all-gather.21.cloned.1.call-done) | data formatting | bytes 10297344 | tf_op jit(solution)/shard_map/all_gather | solution.py:177
  292.5 23.3 %copy.407 = bf16[1,768,3352]{1,2,0:T(8,128)(2,1)} copy(bf16[1,768,3352]{2,0,1:T(2,128)(2,1)} %all-gather.25.cloned.1.call-done) | data formatting | bytes 10297344 | tf_op jit(solution)/shard_map/all_gather | solution.py:177
  316.9 7.7 fusion.61
  333.1 7.2 fusion.71
  365.8 8.5 fusion.60
  384.3 7.2 fusion.70
  411.4 9.3 fusion.19
  424.9 6.4 fusion.76
  431.4 4.8 multiply_reduce_fusion.4
  466.6 6.6 scatter-add.6
  473.2 5.5 fusion.133
  499.0 10.1 fusion.21
  511.4 6.4 fusion.74
  528.9 5.5 convolution_bitcast_fusion
  564.1 4.5 pad_maximum_fusion.1
  571.6 29.3 %copy.455 = f32[2,1536,768]{2,0,1:T(2,128)} copy(f32[2,1536,768]{2,1,0:T(8,128)S(1)} %pad_maximum_fusion.1) | data formatting | bytes 18874368 | tf_op jit(solution)/shard_map/stack | solution.py:277
  605.2 6.1 scatter-add.9
  611.4 5.8 fusion.125
  617.2 5.4 convolution_bitcast_fusion.1
  623.2 15.7 %pad_maximum_fusion = f32[2,768,3352]{1,2,0:T(8,128)} fusion(f32[1,768,3352]{1,2,0:T(8,128)} %convolution_bitcast_fusion, f32[1,768,3352]{1,2,0:T(8,128)} %convolution_bitcast_fusion.1), kind=kLoop, calls=%fused_computation.8 | loop fusion | flops 5148672 | bytes 41189376 | tf_op jit(solution)/shard_map/stack | solution.py:277
  638.9 32.4 %copy.454 = f32[2,768,3352]{2,0,1:T(2,128)} copy(f32[2,768,3352]{1,2,0:T(8,128)} %pad_maximum_fusion) | data formatting | bytes 41189376 | tf_op jit(solution)/shard_map/stack | solution.py:277
  679.4 6.4 psum.28
  685.8 8.6 psum.29
  694.4 6.1 psum.30
  700.5 6.9 psum.31
  710.8 48.3 %all-reduce.55.cloned.1.call-done = (f32[2,4,1792]{2,1,0:T(4,128)}, f32[2,1792]{1,0:T(2,128)}, f32[2,768]{1,0:T(2,128)}, f32[2,1536]{1,0:T(2,128)}) async-done(((f32[2,4,1792]{2,1,0:T(4,128)}, f32[2,1792]{1,0:T(2,128)}, f32[2,768]{1,0:T(2,128)}, f32[2,1536]{1,0:T(2,128)}), (f32[2,4,1792]{2,1,0:T(4,128)}, f32[2,1792]{1,0:T(2,128)}, f32[2,768]{1,0:T(2,128)}, ...) | async-done | bytes 90128
  764.3 240.8 %all-reduce.57.cloned.1.call-done = (f32[2,768,3352]{2,0,1:T(2,128)}, f32[2,1536,768]{2,0,1:T(2,128)}) async-done(((f32[2,768,3352]{2,0,1:T(2,128)}, f32[2,1536,768]{2,0,1:T(2,128)}), (f32[2,768,3352]{2,0,1:T(2,128)}, f32[2,1536,768]{2,0,1:T(2,128)})) %all-reduce.57.cloned.1.call-update) | async-done | bytes 30031888
  (618 shorter events, 234.9 us)
Async XLA Ops:
  7.2 238.5 %all-gather.21.cloned.1.call-start = ((), (), s32[]{:S(2)}) async-start(), calls=%async_computation | async-start | bytes 10699776 | tf_op jit(solution)/shard_map/all_gather | solution.py:177
  9.0 283.4 %all-gather.25.cloned.1.call-start = ((), (), s32[]{:S(2)}) async-start(), calls=%async_computation.2 | async-start | bytes 10699776 | tf_op jit(solution)/shard_map/all_gather | solution.py:177
  9.8 333.1 %all-gather.23.cloned.1.call-start = ((), (), s32[]{:S(2)}) async-start(), calls=%async_computation.1 | async-start | bytes 4755456 | tf_op jit(solution)/shard_map/all_gather | solution.py:178
  11.4 383.8 %all-gather.27.cloned.1.call-start = ((), (), s32[]{:S(2)}) async-start(), calls=%async_computation.3 | async-start | bytes 4755456 | tf_op jit(solution)/shard_map/all_gather | solution.py:178
  12.0 747.1 %all-reduce.55.cloned.1.call-start = ((), (), s32[]{:S(2)}) async-start(), calls=%async_computation.4 | async-start | bytes 180224
  16.4 252.8 %copy-start.87 = (f32[256]{0:T(256)}, f32[256]{0:T(256)S(1)}, u32[]{:S(2)}) copy-start(f32[256]{0:T(256)S(1)} %fusion.214) | copy-start | bytes 3076
  20.6 252.7 %copy-start.168 = (f32[24]{0:T(128)}, f32[24]{0:T(128)S(1)}, u32[]{:S(2)}) copy-start(f32[24]{0:T(128)S(1)} %get-tuple-element.678) | copy-start | bytes 292
  20.6 252.8 %copy-start.170 = (f32[24]{0:T(128)}, f32[24]{0:T(128)S(1)}, u32[]{:S(2)}) copy-start(f32[24]{0:T(128)S(1)} %get-tuple-element.679) | copy-start | bytes 292
  92.5 362.3 %copy-start.70 = (f32[1536]{0:T(1024)}, f32[1536]{0:T(1024)S(1)}, u32[]{:S(2)}) copy-start(f32[1536]{0:T(1024)S(1)} %convert_element_type.277) | copy-start | bytes 18436
  95.1 186.3 %copy-start.139 = (f32[1,256]{1,0:T(1,128)}, f32[1,256]{1,0:T(1,128)S(1)}, u32[]{:S(2)}) copy-start(f32[1,256]{1,0:T(1,128)S(1)} %get-tuple-element.641) | copy-start | bytes 3076
  206.6 37.8 %copy-start.149 = (s32[1,512]{1,0:T(1,128)S(1)}, s32[1,512]{1,0:T(1,128)}, u32[]{:S(2)}) copy-start(s32[1,512]{1,0:T(1,128)} %param.24) | copy-start | bytes 6148
  245.7 37.5 %copy-start.112 = (f32[1,256]{1,0:T(1,128)}, f32[1,256]{1,0:T(1,128)S(1)}, u32[]{:S(2)}) copy-start(f32[1,256]{1,0:T(1,128)S(1)} %get-tuple-element.688) | copy-start | bytes 3076
  273.4 15.1 %copy-start.3 = (f32[1,256,3352]{1,2,0:T(8,128)}, f32[1,256,3352]{1,2,0:T(8,128)S(1)}, u32[]{:S(2)}) copy-start(f32[1,256,3352]{1,2,0:T(8,128)S(1)} %convolution_bitcast_fusion.3) | copy-start | bytes 10297348
  280.2 35.6 %collective-permute-start = (f32[1,3,1792]{2,0,1:T(1,128)S(1)}, f32[1,3,1792]{2,0,1:T(1,128)}, u32[]{:S(2)}, u32[]{:S(2)}) collective-permute-start(f32[1,3,1792]{2,0,1:T(1,128)S(1)} %copy.394), channel_id=1, source_target_pairs={{0,1},{2,3},{4,5},{6,7},{8,9},{10,11},{12,13},{14,15},{16,17},{18,... | collective-permute-start | bytes 64520 | tf_op jit(solution)/shard_map/ppermute | solution.py:26
  292.4 33.6 %copy-start.74 = (f32[256,24]{0,1:T(8,128)}, f32[256,24]{0,1:T(8,128)S(1)}, u32[]{:S(2)}) copy-start(f32[256,24]{0,1:T(8,128)S(1)} %copy.401) | copy-start | bytes 73732
  292.4 24.5 %copy-start.92 = (f32[1792]{0:T(1024)S(1)}, f32[1792]{0:T(1024)}, u32[]{:S(2)}) copy-start(f32[1792]{0:T(1024)} %get-tuple-element.565) | copy-start | bytes 21508
  292.4 24.5 %copy-start.94 = (f32[1792]{0:T(1024)S(1)}, f32[1792]{0:T(1024)}, u32[]{:S(2)}) copy-start(f32[1792]{0:T(1024)} %get-tuple-element.566) | copy-start | bytes 21508
  292.4 24.5 %copy-start.96 = (f32[1792]{0:T(1024)S(1)}, f32[1792]{0:T(1024)}, u32[]{:S(2)}) copy-start(f32[1792]{0:T(1024)} %get-tuple-element.567) | copy-start | bytes 21508
  292.4 24.5 %copy-start.98 = (f32[1792]{0:T(1024)S(1)}, f32[1792]{0:T(1024)}, u32[]{:S(2)}) copy-start(f32[1792]{0:T(1024)} %get-tuple-element.568) | copy-start | bytes 21508
  292.4 24.5 %copy-start.116 = (f32[1,256]{1,0:T(1,128)S(1)}, f32[1,256]{1,0:T(1,128)}, u32[]{:S(2)}) copy-start(f32[1,256]{1,0:T(1,128)} %get-tuple-element.681) | copy-start | bytes 3076
  292.4 24.5 %copy-start.120 = (f32[1,256]{1,0:T(1,128)S(1)}, f32[1,256]{1,0:T(1,128)}, u32[]{:S(2)}) copy-start(f32[1,256]{1,0:T(1,128)} %get-tuple-element.682) | copy-start | bytes 3076
  292.4 24.5 %copy-start.124 = (f32[1,256]{1,0:T(1,128)S(1)}, f32[1,256]{1,0:T(1,128)}, u32[]{:S(2)}) copy-start(f32[1,256]{1,0:T(1,128)} %get-tuple-element.683) | copy-start | bytes 3076
  292.4 24.5 %copy-start.129 = (f32[1792]{0:T(1024)S(1)}, f32[1792]{0:T(1024)}, u32[]{:S(2)}) copy-start(f32[1792]{0:T(1024)} %convert_element_type.273) | copy-start | bytes 21508
  353.3 31.0 %copy-start.85 = (f32[256,24]{0,1:T(8,128)}, f32[256,24]{0,1:T(8,128)S(1)}, u32[]{:S(2)}) copy-start(f32[256,24]{0,1:T(8,128)S(1)} %get-tuple-element.647) | copy-start | bytes 73732
  356.9 7.6 collective-permute-start.1
  364.4 19.9 %copy-start.80 = (f32[256,24]{0,1:T(8,128)}, f32[256,24]{0,1:T(8,128)S(1)}, u32[]{:S(2)}) copy-start(f32[256,24]{0,1:T(8,128)S(1)} %copy.419) | copy-start | bytes 73732
  411.4 11.9 %copy-start.29 = (f32[1,256,1536]{1,2,0:T(8,128)S(1)}, f32[1,256,1536]{1,2,0:T(8,128)}, u32[]{:S(2)}) copy-start(f32[1,256,1536]{1,2,0:T(8,128)} %copy-done.28) | copy-start | bytes 4718596
  450.5 12.2 %collective-permute-start.2 = (f32[1,3,1792]{2,0,1:T(1,128)}, f32[1,3,1792]{2,0,1:T(1,128)S(1)}, u32[]{:S(2)}, u32[]{:S(2)}) collective-permute-start(f32[1,3,1792]{2,0,1:T(1,128)} %copy.435), channel_id=1, source_target_pairs={{1,0},{3,2},{5,4},{7,6},{9,8},{11,10},{13,12},{15,14},{17,16},{19,... | collective-permute-start | bytes 64520 | tf_op jit(solution)/shard_map/ppermute | solution.py:26
  550.4 12.2 %copy-start.169 = (f32[24]{0:T(128)S(1)}, f32[24]{0:T(128)}, u32[]{:S(2)}) copy-start(f32[24]{0:T(128)} %copy-done.168) | copy-start | bytes 292
  556.0 44.9 %collective-permute-start.3 = (f32[1,3,1792]{2,0,1:T(1,128)}, f32[1,3,1792]{2,0,1:T(1,128)}, u32[]{:S(2)}, u32[]{:S(2)}) collective-permute-start(f32[1,3,1792]{2,0,1:T(1,128)} %copy.452), channel_id=1, source_target_pairs={{1,0},{3,2},{5,4},{7,6},{9,8},{11,10},{13,12},{15,14},{17,16},{19,... | collective-permute-start | bytes 64520 | tf_op jit(solution)/shard_map/ppermute | solution.py:26
  623.2 382.0 %all-reduce.57.cloned.1.call-start = ((), (), s32[]{:S(2)}) async-start(), calls=%async_computation.5 | async-start | bytes 61341696
  672.9 35.8 %copy-start.43 = (f32[1,256,768]{2,1,0:T(8,128)S(1)}, f32[1,256,768]{2,1,0:T(8,128)}, u32[]{:S(2)}) copy-start(f32[1,256,768]{2,1,0:T(8,128)} %copy-done.41) | copy-start | bytes 2359300
  (161 other events, 671.8 us)
Sparse Core Ops, SparseCore 0:
  11.6 75.4 all-gather.20
  90.7 70.7 all-gather.24
  164.6 65.5 all-gather.22
  233.1 64.5 all-gather.26
  623.3 135.7 all-reduce.54
  765.8 239.3 all-reduce.56
where the time goes:
time: 1030 us; the launch traced here: 1020 us
  waiting for transfers between devices  290 us (28%)
  local copies, waits for them, and re-layouts  271 us (26%)
  blocking collectives  184 us (18%)
  matrix products  124 us (12%)
  other arithmetic  118 us (11%)
  between operations  18.3 us (2%)
    unnamed x8, waiting for transfers between devices  290 us
    slice x2, local copies, waits for them, and re-layouts, local_mixer(): kernel_weights[offset] * extended[:, offset:offset + block_size]  75.5 us
    all_gather x2, blocking collectives, per_device(): lax.all_gather(kernel_weight[layer_index], DP_SEQ, axis=1, tiled=True)  70.4 us
    unnamed x1, blocking collectives  69.7 us
    another operation x8, local copies, waits for them, and re-layouts, per_device(): jnp.stack([entry_set[slot_index] for entry_set in sums_kept])  64.6 us
    all_gather x2, local copies, waits for them, and re-layouts, per_device(): lax.all_gather(projection_in[layer_index], DP_SEQ, axis=0, tiled=True)  46.7 us
    dot_general x6, matrix products, local_mixer(): jnp.einsum('rhts,rshp->rthp', decay_matrix * affinity[:, None], scaled, p...  46.7 us
    psum x4, blocking collectives, over_axes(): return functools.reduce(lax.psum, axes, array)  28 us
  transfers between devices with their start and end apart: 10, of which 2 were waited for; matrix products, arithmetic and copies ran while one was open for 33% of the time, Pallas kernels for 0%

commit v1 on v0

v1 whole, which is shorter than its diff:
```python
import jax
import jax.numpy as jnp
from jax import lax
from jax.experimental import pallas as pl
from jax.experimental.pallas import tpu as pltpu
from jax.sharding import Mesh
from jax.sharding import PartitionSpec as P

HEADS = 24
HEAD_DIM = 64
STATE = 128
INNER = 1536
CONV_CH = 1792
WIDTH = 768
TOKENS = 512
HALF = 256
OWN_HEADS = 12
OWN = OWN_HEADS * HEAD_DIM
OWN_CONV = OWN + 2 * STATE
OWN_COLS = OWN + OWN_CONV + 128
NORM_EPS = 1e-05
NEGATIVE = -1e30
F32 = jnp.float32
BF16 = jnp.bfloat16
HIGHEST = lax.Precision.HIGHEST


def dot(a, b, dims=((1,), (0,)), precision=None):
    return lax.dot_general(a, b, (dims, ((), ())), precision=precision, preferred_element_type=F32)


def dot_nt(a, b, precision=None):
    return dot(a, b, ((1,), (1,)), precision)


def dot_tn(a, b, precision=None):
    return dot(a, b, ((0,), (0,)), precision)


def iota(shape, dim):
    return lax.broadcasted_iota(jnp.int32, shape, dim)


def padded_order():
    column = iota((WIDTH, 1024), 1)
    core = column >> 9
    chip = (column & 511) >> 3
    place = column & 7
    feature = jnp.where(place < 6, 12 * chip + 6 * core + place, -1)
    return jnp.where(feature == iota((WIDTH, 1024), 0), 1.0, 0.0).astype(BF16)


def head_spread():
    return jnp.where(iota((128, OWN), 0) == (iota((128, OWN), 1) >> 6), 1.0, 0.0).astype(F32)


def softplus(v):
    return jnp.maximum(v, 0.0) + jnp.log1p(jnp.exp(-jnp.abs(v)))


def tap_masks(segment_column):
    position = iota((TOKENS, 1), 0)
    wide = jnp.broadcast_to(segment_column, (TOKENS, 128))
    masks = [None]
    for back in range(1, 4):
        before = pltpu.roll(wide, back, 0)[:, :1]
        same = (before == segment_column) & (position >= back)
        masks.append(jnp.where(same, 1.0, 0.0).astype(F32))
    return masks


def convolved(signal, taps, masks):
    total = taps[3:4] * signal
    for back in range(1, 4):
        total = total + taps[3 - back : 4 - back] * (pltpu.roll(signal, back, 0) * masks[back])
    return total + taps[4:5]


def steps_of(raw, heads):
    shifted = raw + heads[0:1]
    step = softplus(shifted)
    log_decay = -step * jnp.exp(heads[1:2])
    lower = jnp.where(iota((TOKENS, TOKENS), 0) >= iota((TOKENS, TOKENS), 1), 1.0, 0.0).astype(F32)
    return shifted, step, dot(lower, log_decay, precision=HIGHEST)


def lane_masks():
    low = iota((1, 128), 1) < HEAD_DIM
    return (jnp.where(low, 1.0, 0.0).astype(BF16), jnp.where(low, 0.0, 1.0).astype(BF16))


def forward_kernel(
    u_ref, win_ref, wout_ref, segc_ref, segr_ref, taps_ref, heads_ref, gain_ref,
    zx_ref, y_ref, out_ref, square_ref, dtx_ref, affinity_ref, bias_ref,
):
    order = padded_order()
    u_padded = dot(u_ref[...], order).astype(BF16)
    zx_ref[...] = dot(u_padded[:, :512], win_ref[:, :OWN_COLS]) + dot(
        u_padded[:, 512:], win_ref[:, OWN_COLS : 2 * OWN_COLS]
    )
    taps = taps_ref[...]
    heads = heads_ref[...]
    segc = segc_ref[...]
    masks = tap_masks(segc)
    before = convolved(zx_ref[:, OWN : OWN + OWN_CONV], taps, masks)
    active = before * jax.nn.sigmoid(before)
    inputs = active[:, :OWN]
    writers = active[:, OWN : OWN + STATE].astype(BF16)
    readers = active[:, OWN + STATE :].astype(BF16)
    _, step, cumul = steps_of(zx_ref[:, OWN + OWN_CONV :], heads)
    cumul_rows = cumul.T
    spread = head_spread()
    dtx_ref[...] = (dot(step, spread, precision=HIGHEST) * inputs).astype(BF16)
    y_ref[...] = dot(heads, spread, precision=HIGHEST)[2:3] * inputs
    allowed = (iota((TOKENS, TOKENS), 0) >= iota((TOKENS, TOKENS), 1)) & (segc == segr_ref[...])
    bias_ref[...] = jnp.where(allowed, 0.0, NEGATIVE).astype(F32)
    affinity_ref[...] = dot_nt(readers, writers)
    halves = lane_masks()
    for pair in range(OWN_HEADS // 2):
        lanes = slice(128 * pair, 128 * pair + 128)
        pair_inputs = dtx_ref[:, lanes]
        for block in range(2):
            rows = slice(HALF * block, HALF * block + HALF)
            reach = HALF * (block + 1)
            total = y_ref[rows, lanes]
            for member in range(2):
                head = 2 * pair + member
                decay = jnp.exp(
                    cumul[rows, head : head + 1]
                    - cumul_rows[head : head + 1, :reach]
                    + bias_ref[rows, :reach]
                )
                mixing = (decay * affinity_ref[rows, :reach]).astype(BF16)
                total = total + dot(mixing, pair_inputs[:reach] * halves[member])
            y_ref[rows, lanes] = total
    gate = zx_ref[:, :OWN]
    gated = y_ref[...] * (gate * jax.nn.sigmoid(gate))
    out_ref[...] = dot((gated * gain_ref[0:1]).astype(BF16), wout_ref[...]).astype(out_ref.dtype)
    square_ref[...] = jnp.broadcast_to(
        jnp.sum(gated * gated, axis=1, keepdims=True), square_ref.shape
    )


def forward_mix(u, win, wout, segc, segr, taps, heads, gain, interpret=False):
    return pl.pallas_call(
        forward_kernel,
        out_shape=(
            jax.ShapeDtypeStruct((TOKENS, OWN_COLS), F32),
            jax.ShapeDtypeStruct((TOKENS, OWN), F32),
            jax.ShapeDtypeStruct((TOKENS, WIDTH), BF16),
            jax.ShapeDtypeStruct((TOKENS, 128), F32),
        ),
        scratch_shapes=[
            pltpu.VMEM((TOKENS, OWN), BF16),
            pltpu.VMEM((TOKENS, TOKENS), F32),
            pltpu.VMEM((TOKENS, TOKENS), F32),
        ],
        compiler_params=pltpu.CompilerParams(vmem_limit_bytes=58 * 2**20),
        interpret=interpret,
    )(u, win, wout, segc, segr, taps, heads, gain)


def backward_kernel(
    seed_ref, mean_ref, rho_ref, u_ref, win_ref, wout_ref, zx_ref, y_ref,
    segc_ref, segr_ref, taps_ref, heads_ref, gain_ref,
    du_ref, dwin_ref, dwout_ref, dtaps_ref, dheads_ref, dgain_ref,
    dtx_ref, affinity_ref, bias_ref, daffinity_ref, dy_ref, dzx_ref, dact_ref, rise_ref, direct_ref,
):
    seed = seed_ref[...]
    gain = gain_ref[0:1]
    rho = rho_ref[...]
    gate = zx_ref[:, :OWN]
    y = y_ref[...]
    open_gate = jax.nn.sigmoid(gate)
    passed = gate * open_gate
    scaled = y * passed * rho
    dyn = dot_nt(seed, wout_ref[...])
    dgain_ref[...] = jnp.broadcast_to(jnp.sum(dyn * scaled, axis=0, keepdims=True), dgain_ref.shape)
    dgated = rho * (dyn * gain - scaled * mean_ref[...])
    dy_ref[...] = dgated * passed
    dzx_ref[:, :OWN] = (dgated * y * (open_gate * (1.0 + gate * (1.0 - open_gate)))).astype(BF16)
    dwout_ref[...] = dot_tn((scaled * gain).astype(BF16), seed).astype(BF16)

    taps = taps_ref[...]
    heads = heads_ref[...]
    segc = segc_ref[...]
    masks = tap_masks(segc)
    signal = zx_ref[:, OWN : OWN + OWN_CONV]
    before = convolved(signal, taps, masks)
    open_act = jax.nn.sigmoid(before)
    active = before * open_act
    inputs = active[:, :OWN]
    writers = active[:, OWN : OWN + STATE].astype(BF16)
    readers = active[:, OWN + STATE :].astype(BF16)
    shifted, step, cumul = steps_of(zx_ref[:, OWN + OWN_CONV :], heads)
    cumul_rows = cumul.T
    spread = head_spread()
    step_wide = dot(step, spread, precision=HIGHEST)
    skip_wide = dot(heads, spread, precision=HIGHEST)[2:3]
    dtx_ref[...] = (step_wide * inputs).astype(BF16)
    allowed = (iota((TOKENS, TOKENS), 0) <= iota((TOKENS, TOKENS), 1)) & (segc == segr_ref[...])
    bias_ref[...] = jnp.where(allowed, 0.0, NEGATIVE).astype(F32)
    affinity_ref[...] = dot_nt(writers, readers)
    daffinity_ref[...] = jnp.zeros_like(daffinity_ref)
    rise_ref[...] = jnp.zeros_like(rise_ref)
    halves = lane_masks()
    head_lane = iota((1, 128), 1)
    fall_blocks = [jnp.zeros((HALF, 128), F32), jnp.zeros((HALF, 128), F32)]
    for pair in range(OWN_HEADS // 2):
        lanes = slice(128 * pair, 128 * pair + 128)
        pair_inputs = dtx_ref[:, lanes]
        pair_dy = dy_ref[:, lanes].astype(BF16)
        member_dy = [pair_dy * half for half in halves]
        for block in range(2):
            rows = slice(HALF * block, HALF * block + HALF)
            start = HALF * block
            dinput = jnp.zeros((HALF, 128), F32)
            for member in range(2):
                head = 2 * pair + member
                decay = jnp.exp(
                    cumul_rows[head : head + 1, start:]
                    - cumul[rows, head : head + 1]
                    + bias_ref[rows, start:]
                )
                dmixing = dot_nt(pair_inputs[rows], member_dy[member][start:]) * decay
                daffinity_ref[rows, start:] += dmixing
                affinity = affinity_ref[rows, start:]
                dinput = dinput + dot((decay * affinity).astype(BF16), member_dy[member][start:])
                dspread = dmixing * affinity
                fall = jnp.sum(dspread, axis=1, keepdims=True)
                fall_blocks[block] = fall_blocks[block] + jnp.where(head_lane == head, fall, 0.0)
                rise_ref[head : head + 1, start:] += jnp.sum(dspread, axis=0, keepdims=True)
            direct_ref[rows, lanes] = dinput
    dinputs = direct_ref[...]
    dy = dy_ref[...]
    dact_ref[:, :OWN] = step_wide * dinputs + skip_wide * dy
    daffinity = daffinity_ref[...].astype(BF16)
    dact_ref[:, OWN : OWN + STATE] = dot(daffinity, readers)
    dact_ref[:, OWN + STATE :] = dot_tn(daffinity, writers)
    dstep = dot_nt(dinputs * inputs, spread, precision=HIGHEST)
    skip_sum = jnp.broadcast_to(jnp.sum(dy * inputs, axis=0, keepdims=True), (8, OWN))
    dskip = dot_nt(skip_sum, spread, precision=HIGHEST)[0:1]
    dcumul = rise_ref[...].T - jnp.concatenate(fall_blocks, axis=0)
    upper = jnp.where(iota((TOKENS, TOKENS), 0) <= iota((TOKENS, TOKENS), 1), 1.0, 0.0).astype(F32)
    dlog = dot(upper, dcumul, precision=HIGHEST)
    rate = jnp.exp(heads[1:2])
    draw = (dstep - dlog * rate) * jax.nn.sigmoid(shifted)
    dheads_ref[...] = jnp.zeros_like(dheads_ref)
    dheads_ref[0:1] = jnp.sum(draw, axis=0, keepdims=True)
    dheads_ref[1:2] = jnp.sum(-dlog * step * rate, axis=0, keepdims=True)
    dheads_ref[2:3] = dskip
    dzx_ref[:, OWN + OWN_CONV :] = draw.astype(BF16)

    dconv = dact_ref[...] * (open_act * (1.0 + before * (1.0 - open_act)))
    dtaps_ref[...] = jnp.zeros_like(dtaps_ref)
    dtaps_ref[4:5] = jnp.sum(dconv, axis=0, keepdims=True)
    dtaps_ref[3:4] = jnp.sum(dconv * signal, axis=0, keepdims=True)
    dsignal = taps[3:4] * dconv
    for back in range(1, 4):
        masked = dconv * masks[back]
        dtaps_ref[3 - back : 4 - back] = jnp.sum(
            masked * pltpu.roll(signal, back, 0), axis=0, keepdims=True
        )
        dsignal = dsignal + taps[3 - back : 4 - back] * pltpu.roll(masked, TOKENS - back, 0)
    dzx_ref[:, OWN : OWN + OWN_CONV] = dsignal.astype(BF16)

    order = padded_order()
    dzx = dzx_ref[...]
    u_padded = dot(u_ref[...], order).astype(BF16)
    du_parts = []
    for core in range(2):
        columns = slice(OWN_COLS * core, OWN_COLS * core + OWN_COLS)
        dwin_ref[:, columns] = dot_tn(u_padded[:, 512 * core : 512 * core + 512], dzx).astype(BF16)
        du_parts.append(dot_nt(dzx, win_ref[:, columns]).astype(BF16))
    du_ref[...] = dot_nt(jnp.concatenate(du_parts, axis=1), order).astype(BF16)


def backward_mix(seed, mean, rho, u, win, wout, zx, y, segc, segr, taps, heads, gain, interpret=False):
    square = (TOKENS, TOKENS)
    return pl.pallas_call(
        backward_kernel,
        out_shape=(
            jax.ShapeDtypeStruct((TOKENS, WIDTH), BF16),
            jax.ShapeDtypeStruct((512, 2 * OWN_COLS), BF16),
            jax.ShapeDtypeStruct((OWN, WIDTH), BF16),
            jax.ShapeDtypeStruct((8, OWN_CONV), F32),
            jax.ShapeDtypeStruct((8, 128), F32),
            jax.ShapeDtypeStruct((8, OWN), F32),
        ),
        scratch_shapes=[
            pltpu.VMEM((TOKENS, OWN), BF16),
            pltpu.VMEM(square, F32),
            pltpu.VMEM(square, F32),
            pltpu.VMEM(square, F32),
            pltpu.VMEM((TOKENS, OWN), F32),
            pltpu.VMEM((TOKENS, OWN_COLS), BF16),
            pltpu.VMEM((TOKENS, OWN_CONV), F32),
            pltpu.VMEM((128, TOKENS), F32),
            pltpu.VMEM((TOKENS, OWN), F32),
        ],
        compiler_params=pltpu.CompilerParams(vmem_limit_bytes=58 * 2**20),
        interpret=interpret,
    )(seed, mean, rho, u, win, wout, zx, y, segc, segr, taps, heads, gain)


DP = ("dp_0", "dp_1", "dp_2")
DP_SEQ = DP + ("seq",)
CHIPS = 64
LAYERS = 2
GATHER_COLS = 2 * OWN_COLS + 3 * 384 + 128


def swapped(v):
    return lax.ppermute(v, "seq", [(0, 1), (1, 0)])


def part(v, index, size, axis):
    return lax.dynamic_slice_in_dim(v, index * size, size, axis)


def in_order(core, own, other, axis):
    first = jnp.where(core == 0, own, other)
    second = jnp.where(core == 0, other, own)
    return jnp.concatenate([first, second], axis=axis)


def padded(v, sizes):
    return jnp.pad(v, [(0, size - now) for now, size in zip(v.shape, sizes)])


def columns_of(win, core):
    gate = part(win, core, OWN, 2)
    inputs = part(win[:, :, INNER : 2 * INNER], core, OWN, 2)
    shared = win[:, :, 2 * INNER : INNER + CONV_CH]
    steps = part(win[:, :, INNER + CONV_CH :], core, OWN_HEADS, 2)
    steps = padded(steps, steps.shape[:2] + (128,))
    return jnp.concatenate([gate, inputs, shared, steps], axis=2)


def packed_weights(win, wout, kernel_weight, kernel_bias, norm_gain, gate_gain, core):
    win = padded(win, (LAYERS, 8, win.shape[2]))
    win_part = in_order(core, columns_of(win, core), swapped(columns_of(win, 1 - core)), 2)
    wout_part = in_order(core, part(wout, core, 384, 2), swapped(part(wout, 1 - core, 384, 2)), 1)
    wout_part = wout_part.reshape(LAYERS, 3, 8, 384).transpose(0, 2, 1, 3).reshape(LAYERS, 8, 1152)
    rows = [padded(kernel_weight, (LAYERS, 4, 16))]
    for vector in (kernel_bias, norm_gain, gate_gain):
        rows.append(padded(vector[:, None], (LAYERS, 1, 16)))
    vectors = padded(jnp.concatenate(rows, axis=1), (LAYERS, 8, 16))
    vectors = padded(in_order(core, vectors, swapped(vectors), 2), (LAYERS, 8, 128))
    return jnp.concatenate([win_part, wout_part, vectors], axis=2)


def gathered_weights(block):
    spread = jnp.broadcast_to(block[None], (CHIPS,) + block.shape)
    return lax.all_to_all(spread, DP, 0, 0, tiled=True)


def unpacked_weights(gathered, core):
    wout = gathered[:, :, 2 * OWN_COLS : 2 * OWN_COLS + 1152].reshape(CHIPS, 8, 3, 384)
    wout = wout.transpose(0, 2, 1, 3).reshape(INNER, 384)
    wout = in_order(core, part(wout, core, OWN, 0), swapped(part(wout, 1 - core, OWN, 0)), 1)
    vectors = gathered[:, :, GATHER_COLS - 128 : GATHER_COLS - 96].astype(F32)
    vectors = vectors.reshape(CHIPS, 8, 2, 16).transpose(1, 0, 2, 3)
    taps = vectors[:5, :, :, :14].reshape(5, CONV_CH)
    taps = jnp.concatenate([part(taps[:, :INNER], core, OWN, 1), taps[:, INNER:]], axis=1)
    norm = vectors[5, :, :, :6].reshape(1, WIDTH)
    gain = part(vectors[6, :, :, :12].reshape(1, INNER), core, OWN, 1)
    return (
        gathered.reshape(CHIPS * 8, GATHER_COLS),
        wout,
        padded(taps, (8, OWN_CONV)),
        norm,
        jnp.broadcast_to(gain, (8, OWN)),
    )


def over_positions(partial_sum, core):
    own = part(partial_sum, core, HALF, 0).astype(F32)
    return own + swapped(part(partial_sum, 1 - core, HALF, 0)).astype(F32)


def packed_gradients(dwin, dwout, dtaps, dheads, dnorm, dgain, core):
    dwout = in_order(core, part(dwout, core, 384, 1), swapped(part(dwout, 1 - core, 384, 1)), 0)
    dwout = dwout.reshape(CHIPS, 3, 8, 384).transpose(0, 2, 1, 3).reshape(CHIPS, 8, 1152)
    taps = jnp.zeros((5, INNER), F32)
    taps = lax.dynamic_update_slice_in_dim(taps, dtaps[:5, :OWN], core * OWN, 1)
    taps = jnp.concatenate([taps, dtaps[:5, OWN:]], axis=1)
    gain = lax.dynamic_update_slice_in_dim(jnp.zeros((1, INNER), F32), dgain[:1], core * OWN, 1)
    heads = jnp.zeros((3, HEADS), F32)
    heads = lax.dynamic_update_slice_in_dim(
        heads, dheads[:3, :OWN_HEADS], core * OWN_HEADS, 1
    ).reshape(1, 72)
    rows = [padded(taps.reshape(5, CHIPS, 2, 14), (5, CHIPS, 2, 16))]
    rows.append(padded(dnorm.reshape(1, CHIPS, 2, 6), (1, CHIPS, 2, 16)))
    rows.append(padded(gain.reshape(1, CHIPS, 2, 12), (1, CHIPS, 2, 16)))
    vectors = jnp.concatenate(rows, axis=0).reshape(7, CHIPS, 32)
    vectors = padded(vectors, (7, CHIPS, 128)).transpose(1, 0, 2)
    heads = jnp.broadcast_to(jnp.pad(heads, ((0, 0), (32, 24)))[None], (CHIPS, 1, 128))
    vectors = jnp.concatenate([vectors, heads], axis=1)
    vectors = vectors + swapped(vectors)
    high = lax.reduce_precision(vectors, 8, 7)
    return jnp.concatenate(
        [
            dwin.reshape(CHIPS, 8, 2 * OWN_COLS),
            dwout,
            high.astype(BF16),
            (vectors - high).astype(BF16),
        ],
        axis=2,
    )


def reduced_gradients(packed):
    arrived = lax.all_to_all(packed, DP, 0, 0, tiled=True)
    return jnp.sum(arrived.astype(F32), axis=0)


def unpacked_gradients(total, core):
    win = [total[:6, :OWN_COLS], total[:6, OWN_COLS : 2 * OWN_COLS]]
    own = jnp.where(core == 0, win[0], win[1])
    got = swapped(jnp.where(core == 0, win[1], win[0]))
    left = jnp.where(core == 0, own, got)
    right = jnp.where(core == 0, got, own)
    shared = slice(2 * OWN, 2 * OWN + 2 * STATE)
    steps = slice(2 * OWN + 2 * STATE, 2 * OWN + 2 * STATE + OWN_HEADS)
    dwin = jnp.concatenate(
        [
            left[:, :OWN],
            right[:, :OWN],
            left[:, OWN : 2 * OWN],
            right[:, OWN : 2 * OWN],
            left[:, shared] + right[:, shared],
            left[:, steps],
            right[:, steps],
        ],
        axis=1,
    )
    start = 2 * OWN_COLS
    wout = total[:, start : start + 1152].reshape(8, 3, 384).transpose(1, 0, 2).reshape(24, 384)
    dwout = in_order(core, part(wout, core, 12, 0), swapped(part(wout, 1 - core, 12, 0)), 1)
    vectors = total[:, start + 1152 : start + 1280] + total[:, start + 1280 : start + 1408]
    own_vectors = part(vectors[:, :32], core, 16, 1)
    return (
        dwin,
        dwout,
        own_vectors[:4, :14],
        own_vectors[4, :14],
        own_vectors[5, :6],
        own_vectors[6, :12],
        vectors[7, 32:104].reshape(3, HEADS),
    )


def mean_square_scale(values):
    return lax.rsqrt(jnp.mean(values * values, axis=1, keepdims=True) + NORM_EPS)


def layers_of(hidden, cotangent, segments, head_values, weights_of, core, send, interpret=False):
    segr = segments
    segc = segments.reshape(TOKENS, 1)
    heads_all = padded(part(head_values, core, OWN_HEADS, 2), (LAYERS, 8, 128))
    current = hidden.astype(F32)
    saved = []
    for layer in range(LAYERS):
        win, wout, taps, norm, gain = weights_of(layer)
        heads = heads_all[layer]
        sigma = mean_square_scale(current)
        u = lax.all_gather((current * sigma * norm).astype(BF16), "seq", axis=0, tiled=True)
        zx, y, out, square = forward_mix(
            u, win, wout, segc, segr, taps, heads, gain, interpret=interpret
        )
        square = square + swapped(square)
        rho = lax.rsqrt(square[:, :1] / INNER + NORM_EPS)
        branch = over_positions(out, core)
        own_rho = part(rho, core, HALF, 0)
        saved.append((current, sigma, u, zx, y, rho, own_rho, branch))
        current = current + own_rho * branch
    upstream = cotangent.astype(F32)
    sent = [None] * LAYERS
    for layer in reversed(range(LAYERS)):
        win, wout, taps, norm, gain = weights_of(layer)
        heads = heads_all[layer]
        before, sigma, u, zx, y, rho, own_rho, branch = saved[layer]
        seed = upstream.astype(BF16)
        mean = own_rho * jnp.sum(seed.astype(F32) * branch, axis=1, keepdims=True) / INNER
        seed = lax.all_gather(seed, "seq", axis=0, tiled=True)
        mean = lax.all_gather(jnp.broadcast_to(mean, (HALF, 128)), "seq", axis=0, tiled=True)
        du, dwin, dwout, dtaps, dheads, dgain = backward_mix(
            seed, mean[:, :1], rho, u, win, wout, zx, y, segc, segr, taps, heads, gain,
            interpret=interpret,
        )
        du = over_positions(du, core)
        dnorm = jnp.sum(du * (before * sigma), axis=0, keepdims=True)
        scaled = du * norm
        upstream = upstream + sigma * (
            scaled
            - before * (sigma * sigma) * jnp.mean(scaled * before, axis=1, keepdims=True)
        )
        sent[layer] = send(dwin, dwout, dtaps, dheads, dnorm, dgain)
    return current.astype(BF16), upstream.astype(BF16), sent


def per_device(
    hidden_in,
    segments,
    projection_in,
    projection_out,
    kernel_weight,
    kernel_bias,
    norm_gain,
    gate_gain,
    head_values,
    cotangent,
):
    core = lax.axis_index("seq")
    blocks = packed_weights(
        projection_in, projection_out, kernel_weight, kernel_bias, norm_gain, gate_gain, core
    )
    weights = [unpacked_weights(gathered_weights(blocks[layer]), core) for layer in range(LAYERS)]

    def send(*gradients):
        return reduced_gradients(packed_gradients(*gradients, core))

    hidden_out, input_gradient, totals = layers_of(
        hidden_in[0], cotangent[0], segments, head_values, lambda layer: weights[layer], core, send
    )
    pieces = [unpacked_gradients(total, core) for total in totals]
    stacked = tuple(jnp.stack([piece[slot] for piece in pieces]) for slot in range(7))
    return (hidden_out[None], input_gradient[None]) + stacked


def solution(mesh):
    torus = Mesh(mesh.devices.reshape(4, 4, 4, mesh.shape["seq"]), DP_SEQ)
    tokens = P(DP, "seq", None)
    weights = (
        P(None, DP_SEQ, None),
        P(None, DP_SEQ, None),
        P(None, None, DP_SEQ),
        P(None, DP_SEQ),
        P(None, DP_SEQ),
        P(None, DP_SEQ),
    )
    return jax.shard_map(
        per_device,
        mesh=torus,
        in_specs=(tokens, P(DP, None)) + weights + (P(), tokens),
        out_specs=(tokens, tokens) + weights + (P(),),
        check_vma=False,
    )
```

time: 1030 us -> 451 us (0.44)
  the two profiles are of different devices: /device:TPU:1 before, /device:TPU:35 now
where the time goes in v1:
time: 451 us; the launch traced here: 444 us
  waiting for transfers between devices  147 us (33%)
  blocking collectives  89 us (20%)
  Pallas kernels  81.7 us (18%)
  local copies, waits for them, and re-layouts  44.5 us (10%)
  starting transfers between devices  43.1 us (10%)
  other arithmetic  37.2 us (8%)
    all_to_all x2, waiting for transfers between devices, reduced_gradients(): arrived = lax.all_to_all(packed, DP, 0, 0, tiled=True)  81.9 us
    all_to_all x1, blocking collectives, gathered_weights(): return lax.all_to_all(spread, DP, 0, 0, tiled=True)  71.4 us
    all_to_all x1, waiting for transfers between devices, gathered_weights(): return lax.all_to_all(spread, DP, 0, 0, tiled=True)  62.8 us
    pallas_call x2, Pallas kernels, backward_mix(): pl.pallas_call(backward_kernel, out_shape=(jax.ShapeDtypeStruct((TOKENS,...  53.9 us
    pallas_call x2, Pallas kernels, forward_mix(): pl.pallas_call(forward_kernel, out_shape=(jax.ShapeDtypeStruct((TOKENS, O...  27.9 us
    all_to_all x2, starting transfers between devices, reduced_gradients(): arrived = lax.all_to_all(packed, DP, 0, 0, tiled=True)  24.4 us
    dynamic_slice x23, local copies, waits for them, and re-layouts, part(): return lax.dynamic_slice_in_dim(v, index * size, size, axis)  13.6 us
    ppermute x19, starting transfers between devices, swapped(): return lax.ppermute(v, 'seq', [(0, 1), (1, 0)])  10.9 us
  transfers between devices with their start and end apart: 22, of which 6 were waited for; matrix products, arithmetic and copies ran while one was open for 13% of the time, Pallas kernels for 6%

profile of v1, /device:TPU:35, one launch (start us, length us, event | category | flops | bytes accessed | tf_op | source)
XLA Modules:
  0.0 444.0 jit_solution(17207017960810546410)
XLA Ops:
  8.4 71.4 %all_to_all.20 = bf16[64,8,5120]{2,1,0:T(8,128)(2,1)} all-to-all(bf16[64,8,5120]{2,1,0:T(8,128)(2,1)S(1)} %broadcast_in_dim.87), channel_id=1, replica_groups=mesh['dp_0'=4,'dp_1'=4,'dp_2'=4,'seq'=2] {'dp_0','dp_1','dp_2'}, dimensions={0} | all-to-all | bytes 10485760 | tf_op jit(solution)/shard_map/all_to_all | solution.py:355
  79.8 3.0 broadcast_in_dim.91
  82.8 7.8 %all-to-all-start.1 = ((bf16[64,8,5120]{2,1,0:T(8,128)(2,1)}), bf16[64,8,5120]{2,1,0:T(8,128)(2,1)}, u32[]{:S(2)}, u32[]{:S(2)}) async-start(bf16[64,8,5120]{2,1,0:T(8,128)(2,1)} %broadcast_in_dim.91), calls=%async_computation.1 | async-start | bytes 10485760 | tf_op jit(solution)/shard_map/all_to_all | solution.py:355
  93.1 62.8 %all-to-all-done.1 = bf16[64,8,5120]{2,1,0:T(8,128)(2,1)} async-done(((bf16[64,8,5120]{2,1,0:T(8,128)(2,1)}), bf16[64,8,5120]{2,1,0:T(8,128)(2,1)}, u32[]{:S(2)}, u32[]{:S(2)}) %all-to-all-start.1) | async-done | bytes 5242912 | tf_op jit(solution)/shard_map/all_to_all | solution.py:355
  158.1 2.4 collective-permute-start.6
  167.9 3.2 all_gather.18.u_ref
  171.0 2.5 broadcast_select_fusion.5
  175.3 14.0 %shard_map.169 = (f32[512,1920]{1,0:T(8,128)}, f32[512,768]{1,0:T(8,128)}, bf16[512,768]{1,0:T(8,128)(2,1)}, f32[512,128]{1,0:T(8,128)}) custom-call(bf16[512,768]{1,0:T(8,128)(2,1)} %all_gather.18.u_ref, bf16[512,5120]{1,0:T(8,128)(2,1)} %bitcast.101, bf16[768,768]{1,0:T(8,128)(2,1)} %pad_maximum_fusion.2.wout_ref, s32[512,1]{1,0:T(8,128)} %copy.106.segc_ref, ...), custom_call_target="tpu_custom_call" | custom-call | tf_op jit(solution)/shard_map/pallas_call | solution.py:145
  189.6 1.8 constant_dynamic-slice_fusion.12
  196.2 2.7 all_gather.19.u_ref
  199.4 13.9 %shard_map.170 = (f32[512,1920]{1,0:T(8,128)}, f32[512,768]{1,0:T(8,128)}, bf16[512,768]{1,0:T(8,128)(2,1)}, f32[512,128]{1,0:T(8,128)}) custom-call(bf16[512,768]{1,0:T(8,128)(2,1)} %all_gather.19.u_ref, bf16[512,5120]{1,0:T(8,128)(2,1)} %bitcast.22.win_ref, bf16[768,768]{1,0:T(8,128)(2,1)} %pad_maximum_fusion.3.wout_ref, s32[512,1]{1,0:T(8,128)} %copy.106.segc_ref, ...), custom_call_target="tpu_custom_call" | custom-call | tf_op jit(solution)/shard_map/pallas_call | solution.py:145
  215.1 2.5 all-gather
  219.9 2.3 all-gather.1.mean_ref
  222.3 27.1 %shard_map.171 = (bf16[512,768]{1,0:T(8,128)(2,1)}, bf16[512,3840]{1,0:T(8,128)(2,1)}, bf16[768,768]{1,0:T(8,128)(2,1)}, f32[8,1024]{1,0:T(8,128)}, f32[8,128]{1,0:T(8,128)}, /*index=5*/f32[8,768]{1,0:T(8,128)}) custom-call(bf16[512,768]{1,0:T(8,128)(2,1)} %bitcast.111, f32[512,1]{1,0:T(8,128)} %all-gather.1.mean_ref, f32[512,1]{1,0:T(8,128)} %copy-done.7, ...), custom_call_target="tpu_custom_call" | custom-call | tf_op jit(solution)/shard_map/pallas_call | solution.py:280
  249.3 1.9 constant_dynamic-slice_fusion.7
  251.5 1.9 constant_dynamic-slice_fusion.4
  262.2 1.6 broadcast_select_fusion.1
  264.4 3.2 pad_maximum_fusion.1
  267.6 6.9 %all-to-all-start.3 = ((bf16[64,8,5248]{2,1,0:T(8,128)(2,1)}), bf16[64,8,5248]{2,1,0:T(8,128)(2,1)}, u32[]{:S(2)}, u32[]{:S(2)}) async-start(bf16[64,8,5248]{2,1,0:T(8,128)(2,1)} %pad_maximum_fusion.1), calls=%async_computation.3 | async-start | bytes 10747904 | tf_op jit(solution)/shard_map/all_to_all | solution.py:414
  274.5 2.4 multiply_reduce_fusion.1
  277.1 2.5 all-gather.2.mean_ref
  279.7 4.4 all_gather.22.seed_ref
  284.1 26.8 %shard_map.172 = (bf16[512,768]{1,0:T(8,128)(2,1)}, bf16[512,3840]{1,0:T(8,128)(2,1)}, bf16[768,768]{1,0:T(8,128)(2,1)}, f32[8,1024]{1,0:T(8,128)}, f32[8,128]{1,0:T(8,128)}, /*index=5*/f32[8,768]{1,0:T(8,128)}) custom-call(bf16[512,768]{1,0:T(8,128)(2,1)} %all_gather.22.seed_ref, f32[512,1]{1,0:T(8,128)} %all-gather.2.mean_ref, f32[512,1]{1,0:T(8,128)} %copy-done.6, ...), custom_call_target="tpu_custom_call" | custom-call | tf_op jit(solution)/shard_map/pallas_call | solution.py:280
  316.4 2.0 constant_dynamic-slice_fusion.5
  322.5 3.3 pad_maximum_fusion
  325.8 15.8 %all-to-all-done.3 = bf16[64,8,5248]{2,1,0:T(8,128)(2,1)} async-done(((bf16[64,8,5248]{2,1,0:T(8,128)(2,1)}), bf16[64,8,5248]{2,1,0:T(8,128)(2,1)}, u32[]{:S(2)}, u32[]{:S(2)}) %all-to-all-start.3) | async-done | bytes 5373984 | tf_op jit(solution)/shard_map/all_to_all | solution.py:414
  341.6 17.5 %all-to-all-start.2 = ((bf16[64,8,5248]{2,1,0:T(8,128)(2,1)}), bf16[64,8,5248]{2,1,0:T(8,128)(2,1)}, u32[]{:S(2)}, u32[]{:S(2)}) async-start(bf16[64,8,5248]{2,1,0:T(8,128)(2,1)} %pad_maximum_fusion), calls=%async_computation.2 | async-start | bytes 10747904 | tf_op jit(solution)/shard_map/all_to_all | solution.py:414
  360.2 3.3 convert_reduce_fusion
  363.5 1.6 collective-permute-start.18
  366.9 66.1 %all-to-all-done.2 = bf16[64,8,5248]{2,1,0:T(8,128)(2,1)} async-done(((bf16[64,8,5248]{2,1,0:T(8,128)(2,1)}), bf16[64,8,5248]{2,1,0:T(8,128)(2,1)}, u32[]{:S(2)}, u32[]{:S(2)}) %all-to-all-start.2) | async-done | bytes 5373984 | tf_op jit(solution)/shard_map/all_to_all | solution.py:414
  433.0 3.3 convert_reduce_fusion.1
  436.5 2.4 collective-permute-start.13
  (282 shorter events, 57.8 us)
Async XLA Ops:
  0.6 90.8 %copy-start = (f32[2,3,24]{2,0,1:T(2,128)S(1)}, f32[2,3,24]{2,0,1:T(2,128)}, u32[]{:S(2)}) copy-start(f32[2,3,24]{2,0,1:T(2,128)} %param.18) | copy-start | bytes 1732
  3.4 3.3 collective-permute-start.2
  4.8 1.9 collective-permute-start.1
  6.1 1.6 collective-permute-start
  82.8 73.1 %all-to-all-start.1 = ((bf16[64,8,5120]{2,1,0:T(8,128)(2,1)}), bf16[64,8,5120]{2,1,0:T(8,128)(2,1)}, u32[]{:S(2)}, u32[]{:S(2)}) async-start(bf16[64,8,5120]{2,1,0:T(8,128)(2,1)} %broadcast_in_dim.91), calls=%async_computation.1 | async-start | bytes 10485760 | tf_op jit(solution)/shard_map/all_to_all | solution.py:355
  92.9 74.8 %copy-start.19 = (f32[256]{0:T(256)}, f32[256]{0:T(256)S(1)}, u32[]{:S(2)}) copy-start(f32[256]{0:T(256)S(1)} %get-tuple-element.141) | copy-start | bytes 3076
  158.1 12.9 %collective-permute-start.6 = (bf16[768,384]{1,0:T(8,128)(2,1)}, bf16[768,384]{1,0:T(8,128)(2,1)}, u32[]{:S(2)}, u32[]{:S(2)}) collective-permute-start(bf16[768,384]{1,0:T(8,128)(2,1)} %constant_dynamic-slice_fusion.11), channel_id=1, source_target_pairs={{0,1},{1,0},{2,3},{3,2},{4,5},{5,4},{6,7},{7,6},{8,9},{9,8},{10,11... | collective-permute-start | bytes 1769480 | tf_op jit(solution)/shard_map/ppermute | solution.py:314
  162.7 8.3 %collective-permute-start.3 = (bf16[768,384]{1,0:T(8,128)(2,1)}, bf16[768,384]{1,0:T(8,128)(2,1)}, u32[]{:S(2)}, u32[]{:S(2)}) collective-permute-start(bf16[768,384]{1,0:T(8,128)(2,1)} %constant_dynamic-slice_fusion.16), channel_id=1, source_target_pairs={{0,1},{1,0},{2,3},{3,2},{4,5},{5,4},{6,7},{7,6},{8,9},{9,8},{10,11... | collective-permute-start | bytes 1769480 | tf_op jit(solution)/shard_map/ppermute | solution.py:314
  175.3 16.3 %slice-start.1 = ((f32[5,1792]{1,0:T(8,128)}), f32[5,256]{1,0:T(8,128)S(1)}, s32[]{:S(2)}) async-start(f32[5,1792]{1,0:T(8,128)} %copy-done.16), calls=%async_computation.5 | async-start | bytes 16384 | tf_op jit(solution)/shard_map/slice | solution.py:365
  175.3 16.3 %copy-start.17 = (f32[5,768]{1,0:T(8,128)S(1)}, f32[5,768]{1,0:T(8,128)}, u32[]{:S(2)}) copy-start(f32[5,768]{1,0:T(8,128)} %constant_dynamic-slice_fusion.10) | copy-start | bytes 46084
  175.3 17.5 %copy-start.8 = (bf16[768,384]{1,0:T(8,128)(2,1)S(1)}, bf16[768,384]{1,0:T(8,128)(2,1)}, u32[]{:S(2)}) copy-start(bf16[768,384]{1,0:T(8,128)(2,1)} %get-tuple-element.99) | copy-start | bytes 1769476
  189.2 4.7 %collective-permute-start.4 = (f32[512,128]{1,0:T(8,128)}, f32[512,128]{1,0:T(8,128)}, u32[]{:S(2)}, u32[]{:S(2)}) collective-permute-start(f32[512,128]{1,0:T(8,128)} %get-tuple-element.29), channel_id=1, source_target_pairs={{0,1},{1,0},{2,3},{3,2},{4,5},{5,4},{6,7},{7,6},{8,9},{9,8},{10,11... | collective-permute-start | bytes 786440 | tf_op jit(solution)/shard_map/ppermute | solution.py:314
  191.4 3.7 collective-permute-start.5
  195.0 82.1 %copy-start.6 = (f32[512,1]{1,0:T(8,128)}, f32[512,1]{1,0:T(8,128)S(1)}, u32[]{:S(2)}) copy-start(f32[512,1]{1,0:T(8,128)S(1)} %fusion.23.rho_ref) | copy-start | bytes 6148
  195.1 18.3 %copy-start.12 = (bf16[256,768]{1,0:T(8,128)(2,1)}, bf16[256,768]{1,0:T(8,128)(2,1)S(1)}, u32[]{:S(2)}) copy-start(bf16[256,768]{1,0:T(8,128)(2,1)S(1)} %collective-permute-done.5) | copy-start | bytes 1179652
  196.0 17.3 %copy-start.21 = (f32[256]{0:T(256)}, f32[256]{0:T(256)S(1)}, u32[]{:S(2)}) copy-start(f32[256]{0:T(256)S(1)} %get-tuple-element.143) | copy-start | bytes 3076
  199.4 15.6 %copy-start.5 = (bf16[1,256,768]{2,1,0:T(8,128)(2,1)S(1)}, bf16[1,256,768]{2,1,0:T(8,128)(2,1)}, u32[]{:S(2)}) copy-start(bf16[1,256,768]{2,1,0:T(8,128)(2,1)} %param.19) | copy-start | bytes 1179652
  213.4 4.2 collective-permute-start.7
  214.8 3.9 collective-permute-start.8
  251.2 8.8 %collective-permute-start.9 = (bf16[256,768]{1,0:T(8,128)(2,1)}, bf16[256,768]{1,0:T(8,128)(2,1)}, u32[]{:S(2)}, u32[]{:S(2)}) collective-permute-start(bf16[256,768]{1,0:T(8,128)(2,1)} %constant_dynamic-slice_fusion.7), channel_id=1, source_target_pairs={{0,1},{1,0},{2,3},{3,2},{4,5},{5,4},{6,7},{7,6},{8,9},{9,8},{10,11... | collective-permute-start | bytes 1179656 | tf_op jit(solution)/shard_map/ppermute | solution.py:314
  253.4 8.8 %collective-permute-start.14 = (bf16[768,384]{1,0:T(8,128)(2,1)}, bf16[768,384]{1,0:T(8,128)(2,1)}, u32[]{:S(2)}, u32[]{:S(2)}) collective-permute-start(bf16[768,384]{1,0:T(8,128)(2,1)} %constant_dynamic-slice_fusion.4), channel_id=1, source_target_pairs={{0,1},{1,0},{2,3},{3,2},{4,5},{5,4},{6,7},{7,6},{8,9},{9,8},{10,11... | collective-permute-start | bytes 1769480 | tf_op jit(solution)/shard_map/ppermute | solution.py:314
  262.0 2.0 collective-permute-start.15
  267.6 74.0 %all-to-all-start.3 = ((bf16[64,8,5248]{2,1,0:T(8,128)(2,1)}), bf16[64,8,5248]{2,1,0:T(8,128)(2,1)}, u32[]{:S(2)}, u32[]{:S(2)}) async-start(bf16[64,8,5248]{2,1,0:T(8,128)(2,1)} %pad_maximum_fusion.1), calls=%async_computation.3 | async-start | bytes 10747904 | tf_op jit(solution)/shard_map/all_to_all | solution.py:414
  312.0 6.7 %collective-permute-start.10 = (bf16[256,768]{1,0:T(8,128)(2,1)S(1)}, bf16[256,768]{1,0:T(8,128)(2,1)S(1)}, u32[]{:S(2)}, u32[]{:S(2)}) collective-permute-start(bf16[256,768]{1,0:T(8,128)(2,1)S(1)} %constant_dynamic-slice_fusion.6), channel_id=1, source_target_pairs={{0,1},{1,0},{2,3},{3,2},{4,5},{5,4},{6,7},{7,6},{8,9},{9,8},{10,11... | collective-permute-start | bytes 1179656 | tf_op jit(solution)/shard_map/ppermute | solution.py:314
  318.4 2.3 collective-permute-start.11
  319.7 2.8 collective-permute-start.12
  325.8 33.3 %copy-start.23 = (f32[256]{0:T(256)S(1)}, f32[256]{0:T(256)}, u32[]{:S(2)}) copy-start(f32[256]{0:T(256)} %get-tuple-element.140) | copy-start | bytes 3076
  341.6 91.4 %all-to-all-start.2 = ((bf16[64,8,5248]{2,1,0:T(8,128)(2,1)}), bf16[64,8,5248]{2,1,0:T(8,128)(2,1)}, u32[]{:S(2)}, u32[]{:S(2)}) async-start(bf16[64,8,5248]{2,1,0:T(8,128)(2,1)} %pad_maximum_fusion), calls=%async_computation.2 | async-start | bytes 10747904 | tf_op jit(solution)/shard_map/all_to_all | solution.py:414
  363.5 2.5 collective-permute-start.18
  365.4 1.3 collective-permute-start.16
  436.5 6.3 %collective-permute-start.13 = (f32[6,1920]{1,0:T(8,128)S(1)}, f32[6,1920]{1,0:T(8,128)S(1)}, u32[]{:S(2)}, u32[]{:S(2)}) collective-permute-start(f32[6,1920]{1,0:T(8,128)S(1)} %slice_select_fusion.2), channel_id=1, source_target_pairs={{0,1},{1,0},{2,3},{3,2},{4,5},{5,4},{6,7},{7,6},{8,9},{9,8},{10,11... | collective-permute-start | bytes 138248 | tf_op jit(solution)/shard_map/ppermute | solution.py:314
  439.0 3.1 collective-permute-start.17
  (18 other events, 105.1 us)

commit v2 on v1

--- a/solution.py
+++ b/solution.py
@@ -18,6 +18,9 @@
 OWN = OWN_HEADS * HEAD_DIM
 OWN_CONV = OWN + 2 * STATE
 OWN_COLS = OWN + OWN_CONV + 128
+FOLD = 1024
+WIN_COLS = OWN_COLS + FOLD
+STEP_TILE = OWN + OWN_CONV
 NORM_EPS = 1e-05
 NEGATIVE = -1e30
 F32 = jnp.float32
@@ -41,13 +44,17 @@
     return lax.broadcasted_iota(jnp.int32, shape, dim)
 
 
-def padded_order():
-    column = iota((WIDTH, 1024), 1)
-    core = column >> 9
-    chip = (column & 511) >> 3
+def padded_orders():
+    column = iota((WIDTH, 512), 1)
+    row = iota((WIDTH, 512), 0)
+    start = 12 * (column >> 3)
     place = column & 7
-    feature = jnp.where(place < 6, 12 * chip + 6 * core + place, -1)
-    return jnp.where(feature == iota((WIDTH, 1024), 0), 1.0, 0.0).astype(BF16)
+    features = (
+        start + place,
+        jnp.where(place < 4, start + place + 8, -1),
+        jnp.where(place < 4, -1, start + place + 4),
+    )
+    return [jnp.where(feature == row, 1.0, 0.0).astype(BF16) for feature in features]
 
 
 def head_spread():
@@ -93,10 +100,13 @@
     u_ref, win_ref, wout_ref, segc_ref, segr_ref, taps_ref, heads_ref, gain_ref,
     zx_ref, y_ref, out_ref, square_ref, dtx_ref, affinity_ref, bias_ref,
 ):
-    order = padded_order()
-    u_padded = dot(u_ref[...], order).astype(BF16)
-    zx_ref[...] = dot(u_padded[:, :512], win_ref[:, :OWN_COLS]) + dot(
-        u_padded[:, 512:], win_ref[:, OWN_COLS : 2 * OWN_COLS]
+    u = u_ref[...]
+    u_full, u_low, u_high = [dot(u, order).astype(BF16) for order in padded_orders()]
+    zx_ref[:, :FOLD] = dot(u_full, win_ref[:, :FOLD]) + dot(
+        u_low, win_ref[:, OWN_COLS : OWN_COLS + FOLD]
+    )
+    zx_ref[:, FOLD:] = dot(u_full, win_ref[:, FOLD:OWN_COLS]) + dot(
+        u_high, win_ref[:, OWN_COLS : 2 * OWN_COLS - FOLD]
     )
     taps = taps_ref[...]
     heads = heads_ref[...]
@@ -264,15 +274,24 @@
         dsignal = dsignal + taps[3 - back : 4 - back] * pltpu.roll(masked, TOKENS - back, 0)
     dzx_ref[:, OWN : OWN + OWN_CONV] = dsignal.astype(BF16)
 
-    order = padded_order()
+    orders = padded_orders()
     dzx = dzx_ref[...]
-    u_padded = dot(u_ref[...], order).astype(BF16)
-    du_parts = []
-    for core in range(2):
-        columns = slice(OWN_COLS * core, OWN_COLS * core + OWN_COLS)
-        dwin_ref[:, columns] = dot_tn(u_padded[:, 512 * core : 512 * core + 512], dzx).astype(BF16)
-        du_parts.append(dot_nt(dzx, win_ref[:, columns]).astype(BF16))
-    du_ref[...] = dot_nt(jnp.concatenate(du_parts, axis=1), order).astype(BF16)
+    u = u_ref[...]
+    u_full, u_low, u_high = [dot(u, order).astype(BF16) for order in orders]
+    rest = OWN_COLS - FOLD
+    dwin_ref[:, :OWN_COLS] = dot_tn(u_full, dzx).astype(BF16)
+    folded = dot_tn(u_low, dzx[:, :FOLD])
+    dwin_ref[:, OWN_COLS : OWN_COLS + rest] = (
+        folded[:, :rest] + dot_tn(u_high, dzx[:, FOLD:])
+    ).astype(BF16)
+    dwin_ref[:, OWN_COLS + rest :] = folded[:, rest:].astype(BF16)
+    du_parts = (
+        dot_nt(dzx, win_ref[:, :OWN_COLS]),
+        dot_nt(dzx[:, :FOLD], win_ref[:, OWN_COLS:WIN_COLS]),
+        dot_nt(dzx[:, FOLD:], win_ref[:, OWN_COLS : OWN_COLS + rest]),
+    )
+    du = [dot_nt(piece.astype(BF16), order) for piece, order in zip(du_parts, orders)]
+    du_ref[...] = (du[0] + du[1] + du[2]).astype(BF16)
 
 
 def backward_mix(seed, mean, rho, u, win, wout, zx, y, segc, segr, taps, heads, gain, interpret=False):
@@ -281,7 +300,7 @@
         backward_kernel,
         out_shape=(
             jax.ShapeDtypeStruct((TOKENS, WIDTH), BF16),
-            jax.ShapeDtypeStruct((512, 2 * OWN_COLS), BF16),
+            jax.ShapeDtypeStruct((512, WIN_COLS), BF16),
             jax.ShapeDtypeStruct((OWN, WIDTH), BF16),
             jax.ShapeDtypeStruct((8, OWN_CONV), F32),
             jax.ShapeDtypeStruct((8, 128), F32),
@@ -307,7 +326,8 @@
 DP_SEQ = DP + ("seq",)
 CHIPS = 64
 LAYERS = 2
-GATHER_COLS = 2 * OWN_COLS + 3 * 384 + 128
+GATHER_COLS = WIN_COLS + 3 * 384
+VECTORS = STEP_TILE + OWN_HEADS
 
 
 def swapped(v):
@@ -338,16 +358,19 @@
 
 
 def packed_weights(win, wout, kernel_weight, kernel_bias, norm_gain, gate_gain, core):
-    win = padded(win, (LAYERS, 8, win.shape[2]))
-    win_part = in_order(core, columns_of(win, core), swapped(columns_of(win, 1 - core)), 2)
+    win_rows = in_order(core, columns_of(win, core), swapped(columns_of(win, 1 - core)), 1)
+    folded = padded(win_rows[:, 8:], (LAYERS, 4, 2 * FOLD)).reshape(LAYERS, 4, 2, FOLD)
+    folded = folded.transpose(0, 2, 1, 3).reshape(LAYERS, 8, FOLD)
     wout_part = in_order(core, part(wout, core, 384, 2), swapped(part(wout, 1 - core, 384, 2)), 1)
     wout_part = wout_part.reshape(LAYERS, 3, 8, 384).transpose(0, 2, 1, 3).reshape(LAYERS, 8, 1152)
     rows = [padded(kernel_weight, (LAYERS, 4, 16))]
     for vector in (kernel_bias, norm_gain, gate_gain):
         rows.append(padded(vector[:, None], (LAYERS, 1, 16)))
     vectors = padded(jnp.concatenate(rows, axis=1), (LAYERS, 8, 16))
-    vectors = padded(in_order(core, vectors, swapped(vectors), 2), (LAYERS, 8, 128))
-    return jnp.concatenate([win_part, wout_part, vectors], axis=2)
+    vectors = in_order(core, vectors, swapped(vectors), 2)
+    steps = win_rows[:, :8, STEP_TILE:VECTORS]
+    tile = padded(jnp.concatenate([steps, vectors], axis=2), (LAYERS, 8, 128))
+    return jnp.concatenate([win_rows[:, :8, :STEP_TILE], tile, folded, wout_part], axis=2)
 
 
 def gathered_weights(block):
@@ -356,10 +379,10 @@
 
 
 def unpacked_weights(gathered, core):
-    wout = gathered[:, :, 2 * OWN_COLS : 2 * OWN_COLS + 1152].reshape(CHIPS, 8, 3, 384)
+    wout = gathered[:, :, WIN_COLS:].reshape(CHIPS, 8, 3, 384)
     wout = wout.transpose(0, 2, 1, 3).reshape(INNER, 384)
     wout = in_order(core, part(wout, core, OWN, 0), swapped(part(wout, 1 - core, OWN, 0)), 1)
-    vectors = gathered[:, :, GATHER_COLS - 128 : GATHER_COLS - 96].astype(F32)
+    vectors = gathered[:, :, VECTORS : VECTORS + 32].astype(F32)
     vectors = vectors.reshape(CHIPS, 8, 2, 16).transpose(1, 0, 2, 3)
     taps = vectors[:5, :, :, :14].reshape(5, CONV_CH)
     taps = jnp.concatenate([part(taps[:, :INNER], core, OWN, 1), taps[:, INNER:]], axis=1)
@@ -394,18 +417,16 @@
     rows.append(padded(dnorm.reshape(1, CHIPS, 2, 6), (1, CHIPS, 2, 16)))
     rows.append(padded(gain.reshape(1, CHIPS, 2, 12), (1, CHIPS, 2, 16)))
     vectors = jnp.concatenate(rows, axis=0).reshape(7, CHIPS, 32)
-    vectors = padded(vectors, (7, CHIPS, 128)).transpose(1, 0, 2)
-    heads = jnp.broadcast_to(jnp.pad(heads, ((0, 0), (32, 24)))[None], (CHIPS, 1, 128))
-    vectors = jnp.concatenate([vectors, heads], axis=1)
-    vectors = vectors + swapped(vectors)
+    vectors = padded(vectors, (8, CHIPS, 32)).transpose(1, 0, 2)
+    heads = jnp.broadcast_to(heads.reshape(1, 8, 9), (CHIPS, 8, 9))
+    vectors = jnp.concatenate([vectors, heads], axis=2)
     high = lax.reduce_precision(vectors, 8, 7)
+    dwin = dwin.reshape(CHIPS, 8, WIN_COLS)
+    tile = jnp.concatenate(
+        [dwin[:, :, STEP_TILE:VECTORS], high.astype(BF16), (vectors - high).astype(BF16)], axis=2
+    )
     return jnp.concatenate(
-        [
-            dwin.reshape(CHIPS, 8, 2 * OWN_COLS),
-            dwout,
-            high.astype(BF16),
-            (vectors - high).astype(BF16),
-        ],
+        [dwin[:, :, :STEP_TILE], padded(tile, (CHIPS, 8, 128)), dwin[:, :, OWN_COLS:], dwout],
         axis=2,
     )
 
@@ -416,9 +437,11 @@
 
 
 def unpacked_gradients(total, core):
-    win = [total[:6, :OWN_COLS], total[:6, OWN_COLS : 2 * OWN_COLS]]
-    own = jnp.where(core == 0, win[0], win[1])
-    got = swapped(jnp.where(core == 0, win[1], win[0]))
+    folded = total[:, OWN_COLS:WIN_COLS].reshape(2, 4, FOLD).transpose(1, 0, 2)
+    folded = folded.reshape(4, 2 * FOLD)[:, :OWN_COLS]
+    win = jnp.concatenate([total[:, :OWN_COLS], folded], axis=0)
+    own = part(win, core, 6, 0)
+    got = swapped(part(win, 1 - core, 6, 0))
     left = jnp.where(core == 0, own, got)
     right = jnp.where(core == 0, got, own)
     shared = slice(2 * OWN, 2 * OWN + 2 * STATE)
@@ -435,10 +458,10 @@
         ],
         axis=1,
     )
-    start = 2 * OWN_COLS
-    wout = total[:, start : start + 1152].reshape(8, 3, 384).transpose(1, 0, 2).reshape(24, 384)
+    wout = total[:, WIN_COLS:].reshape(8, 3, 384).transpose(1, 0, 2).reshape(24, 384)
     dwout = in_order(core, part(wout, core, 12, 0), swapped(part(wout, 1 - core, 12, 0)), 1)
-    vectors = total[:, start + 1152 : start + 1280] + total[:, start + 1280 : start + 1408]
+    vectors = total[:, VECTORS : VECTORS + 41] + total[:, VECTORS + 41 : VECTORS + 82]
+    vectors = vectors + swapped(vectors)
     own_vectors = part(vectors[:, :32], core, 16, 1)
     return (
         dwin,
@@ -447,7 +470,7 @@
         own_vectors[4, :14],
         own_vectors[5, :6],
         own_vectors[6, :12],
-        vectors[7, 32:104].reshape(3, HEADS),
+        vectors[:, 32:].reshape(3, HEADS),
     )
 
 
@@ -516,7 +539,10 @@
     blocks = packed_weights(
         projection_in, projection_out, kernel_weight, kernel_bias, norm_gain, gate_gain, core
     )
-    weights = [unpacked_weights(gathered_weights(blocks[layer]), core) for layer in range(LAYERS)]
+    first = gathered_weights(blocks[0])
+    first, later = lax.optimization_barrier((first, blocks[1]))
+    gathered = (first, gathered_weights(later))
+    weights = [unpacked_weights(block, core) for block in gathered]
 
     def send(*gradients):
         return reduced_gradients(packed_gradients(*gradients, core))

time: 451 us -> 418 us (0.927)
  the two profiles are of different devices: /device:TPU:35 before, /device:TPU:1 now
where the time goes in v2:
time: 418 us; the launch traced here: 410 us
  Pallas kernels  83.5 us (20%)
  waiting for transfers between devices  82.7 us (20%)
  local copies, waits for them, and re-layouts  81.8 us (20%)
  blocking collectives  78.4 us (19%)
  other arithmetic  42.3 us (10%)
  starting transfers between devices  38.8 us (9%)
    all_to_all x1, blocking collectives, gathered_weights(): return lax.all_to_all(spread, DP, 0, 0, tiled=True)  61.7 us
    pallas_call x2, Pallas kernels, backward_mix(): pl.pallas_call(backward_kernel, out_shape=(jax.ShapeDtypeStruct((TOKENS,...  55.4 us
    all_to_all x2, waiting for transfers between devices, reduced_gradients(): arrived = lax.all_to_all(packed, DP, 0, 0, tiled=True)  47.4 us
    all_to_all x1, waiting for transfers between devices, gathered_weights(): return lax.all_to_all(spread, DP, 0, 0, tiled=True)  32.9 us
    pallas_call x2, Pallas kernels, forward_mix(): pl.pallas_call(forward_kernel, out_shape=(jax.ShapeDtypeStruct((TOKENS, O...  28.2 us
    all_to_all x2, starting transfers between devices, reduced_gradients(): arrived = lax.all_to_all(packed, DP, 0, 0, tiled=True)  18 us
    unnamed x110, local copies, waits for them, and re-layouts  16.4 us
    dynamic_slice x23, local copies, waits for them, and re-layouts, part(): return lax.dynamic_slice_in_dim(v, index * size, size, axis)  14 us
  transfers between devices with their start and end apart: 22, of which 6 were waited for; matrix products, arithmetic and copies ran while one was open for 24% of the time, Pallas kernels for 7%

profile of v2, /device:TPU:1, one launch (start us, length us, event | category | flops | bytes accessed | tf_op | source)
XLA Modules:
  0.0 409.8 jit_solution(11994476638944257893)
XLA Ops:
  12.0 61.7 %all_to_all.20 = bf16[64,8,4096]{2,1,0:T(8,128)(2,1)} all-to-all(bf16[64,8,4096]{2,1,0:T(8,128)(2,1)S(1)} %broadcast_in_dim.84), channel_id=1, replica_groups=mesh['dp_0'=4,'dp_1'=4,'dp_2'=4,'seq'=2] {'dp_0','dp_1','dp_2'}, dimensions={0} | all-to-all | bytes 8388608 | tf_op jit(solution)/shard_map/all_to_all | solution.py:378
  73.7 2.5 broadcast_in_dim.87
  76.2 7.2 %all-to-all-start.1 = ((bf16[64,8,4096]{2,1,0:T(8,128)(2,1)}), bf16[64,8,4096]{2,1,0:T(8,128)(2,1)}, u32[]{:S(2)}, u32[]{:S(2)}) async-start(bf16[64,8,4096]{2,1,0:T(8,128)(2,1)} %broadcast_in_dim.87), calls=%async_computation.1 | async-start | bytes 8388608 | tf_op jit(solution)/shard_map/all_to_all | solution.py:378
  85.7 9.2 %copy.127 = bf16[64,8,4096]{0,2,1:T(8,128)(2,1)} copy(bf16[64,8,4096]{2,1,0:T(8,128)(2,1)} %all_to_all.20) | data formatting | bytes 8388608 | tf_op jit(solution)/shard_map/optimization_barrier | solution.py:543
  99.0 2.1 collective-permute-start.3
  101.3 32.9 %all-to-all-done.1 = bf16[64,8,4096]{2,1,0:T(8,128)(2,1)} async-done(((bf16[64,8,4096]{2,1,0:T(8,128)(2,1)}), bf16[64,8,4096]{2,1,0:T(8,128)(2,1)}, u32[]{:S(2)}, u32[]{:S(2)}) %all-to-all-start.1) | async-done | bytes 4194336 | tf_op jit(solution)/shard_map/all_to_all | solution.py:378
  136.4 3.6 collective-permute-start.6
  140.9 2.7 all_gather.18.u_ref
  145.5 2.6 broadcast_select_fusion.5
  149.9 14.1 %shard_map.169 = (f32[512,1920]{1,0:T(8,128)}, f32[512,768]{1,0:T(8,128)}, bf16[512,768]{1,0:T(8,128)(2,1)}, f32[512,128]{1,0:T(8,128)}) custom-call(bf16[512,768]{1,0:T(8,128)(2,1)} %all_gather.18.u_ref, bf16[512,4096]{1,0:T(8,128)(2,1)} %bitcast.108, bf16[768,768]{1,0:T(8,128)(2,1)} %pad_maximum_fusion.wout_ref, s32[512,1]{1,0:T(8,128)} %copy.132.segc_ref, ...), custom_call_target="tpu_custom_call" | custom-call | tf_op jit(solution)/shard_map/pallas_call | solution.py:155
  171.1 2.5 all_gather.19.u_ref
  174.2 14.1 %shard_map.170 = (f32[512,1920]{1,0:T(8,128)}, f32[512,768]{1,0:T(8,128)}, bf16[512,768]{1,0:T(8,128)(2,1)}, f32[512,128]{1,0:T(8,128)}) custom-call(bf16[512,768]{1,0:T(8,128)(2,1)} %all_gather.19.u_ref, bf16[512,4096]{1,0:T(8,128)(2,1)} %bitcast.25.win_ref, bf16[768,768]{1,0:T(8,128)(2,1)} %pad_maximum_fusion.1.wout_ref, s32[512,1]{1,0:T(8,128)} %copy.132.segc_ref, ...), custom_call_target="tpu_custom_call" | custom-call | tf_op jit(solution)/shard_map/pallas_call | solution.py:155
  190.0 2.5 all-gather
  194.8 2.3 all-gather.1.mean_ref
  197.1 27.8 %shard_map.171 = (bf16[512,768]{1,0:T(8,128)(2,1)}, bf16[512,2944]{1,0:T(8,128)(2,1)}, bf16[768,768]{1,0:T(8,128)(2,1)}, f32[8,1024]{1,0:T(8,128)}, f32[8,128]{1,0:T(8,128)}, /*index=5*/f32[8,768]{1,0:T(8,128)}) custom-call(bf16[512,768]{1,0:T(8,128)(2,1)} %bitcast.116, f32[512,1]{1,0:T(8,128)} %all-gather.1.mean_ref, f32[512,1]{1,0:T(8,128)} %copy-done.12, ...), custom_call_target="tpu_custom_call" | custom-call | tf_op jit(solution)/shard_map/pallas_call | solution.py:299
  230.2 2.3 slice.369
  242.8 2.1 reshape.188
  249.6 2.0 multiply_reduce_fusion
  257.7 2.3 fusion.8
  260.0 7.6 %all-to-all-start.3 = ((bf16[64,8,4096]{2,1,0:T(8,128)(2,1)}), bf16[64,8,4096]{2,1,0:T(8,128)(2,1)}, u32[]{:S(2)}, u32[]{:S(2)}) async-start(bf16[64,8,4096]{2,1,0:T(8,128)(2,1)} %fusion.8), calls=%async_computation.3 | async-start | bytes 8388608 | tf_op jit(solution)/shard_map/all_to_all | solution.py:435
  267.7 2.6 multiply_reduce_fusion.1
  270.5 2.3 all-gather.2.mean_ref
  272.8 4.4 %all_gather.22.seed_ref = bf16[512,768]{1,0:T(8,128)(2,1)} all-gather(bf16[256,768]{1,0:T(8,128)(2,1)} %get-tuple-element.94), channel_id=1, replica_groups=mesh['dp_0'=4,'dp_1'=4,'dp_2'=4,'seq'=2] {'seq'}, dimensions={0}, use_global_device_ids=true | all-gather | bytes 1179648 | tf_op jit(solution)/shard_map/all_gather | solution.py:509
  277.2 27.6 %shard_map.172 = (bf16[512,768]{1,0:T(8,128)(2,1)}, bf16[512,2944]{1,0:T(8,128)(2,1)}, bf16[768,768]{1,0:T(8,128)(2,1)}, f32[8,1024]{1,0:T(8,128)}, f32[8,128]{1,0:T(8,128)}, /*index=5*/f32[8,768]{1,0:T(8,128)}) custom-call(bf16[512,768]{1,0:T(8,128)(2,1)} %all_gather.22.seed_ref, f32[512,1]{1,0:T(8,128)} %all-gather.2.mean_ref, f32[512,1]{1,0:T(8,128)} %copy-done.10, ...), custom_call_target="tpu_custom_call" | custom-call | tf_op jit(solution)/shard_map/pallas_call | solution.py:299
  310.0 2.3 slice.355
  321.4 2.1 reshape.180
  326.0 2.0 constant_dynamic-slice_fusion.5
  332.2 2.3 fusion.5
  334.6 10.4 %all-to-all-start.2 = ((bf16[64,8,4096]{2,1,0:T(8,128)(2,1)}), bf16[64,8,4096]{2,1,0:T(8,128)(2,1)}, u32[]{:S(2)}, u32[]{:S(2)}) async-start(bf16[64,8,4096]{2,1,0:T(8,128)(2,1)} %fusion.5), calls=%async_computation.2 | async-start | bytes 8388608 | tf_op jit(solution)/shard_map/all_to_all | solution.py:435
  346.1 2.8 convert_reduce_fusion
  351.5 47.4 %all-to-all-done.2 = bf16[64,8,4096]{2,1,0:T(8,128)(2,1)} async-done(((bf16[64,8,4096]{2,1,0:T(8,128)(2,1)}), bf16[64,8,4096]{2,1,0:T(8,128)(2,1)}, u32[]{:S(2)}, u32[]{:S(2)}) %all-to-all-start.2) | async-done | bytes 4194336 | tf_op jit(solution)/shard_map/all_to_all | solution.py:435
  398.8 2.8 convert_reduce_fusion.1
  (339 shorter events, 94.9 us)
Async XLA Ops:
  0.6 83.6 %copy-start = (f32[2,3,24]{2,0,1:T(2,128)S(1)}, f32[2,3,24]{2,0,1:T(2,128)}, u32[]{:S(2)}) copy-start(f32[2,3,24]{2,0,1:T(2,128)} %param.18) | copy-start | bytes 1732
  4.0 7.3 %collective-permute-start = (bf16[2,6,1920]{2,1,0:T(8,128)(2,1)S(1)}, bf16[2,6,1920]{2,1,0:T(8,128)(2,1)S(1)}, u32[]{:S(2)}, u32[]{:S(2)}) collective-permute-start(bf16[2,6,1920]{2,1,0:T(8,128)(2,1)S(1)} %fusion.45), channel_id=1, source_target_pairs={{0,1},{1,0},{2,3},{3,2},{4,5},{5,4},{6,7},{7,6},{8,9},{9,8},{10,11... | collective-permute-start | bytes 138248 | tf_op jit(solution)/shard_map/ppermute | solution.py:334
  8.2 1.4 collective-permute-start.1
  9.0 1.4 collective-permute-start.2
  76.2 58.0 %all-to-all-start.1 = ((bf16[64,8,4096]{2,1,0:T(8,128)(2,1)}), bf16[64,8,4096]{2,1,0:T(8,128)(2,1)}, u32[]{:S(2)}, u32[]{:S(2)}) async-start(bf16[64,8,4096]{2,1,0:T(8,128)(2,1)} %broadcast_in_dim.87), calls=%async_computation.1 | async-start | bytes 8388608 | tf_op jit(solution)/shard_map/all_to_all | solution.py:378
  85.7 15.4 %copy-start.33 = (f32[256]{0:T(256)}, f32[256]{0:T(256)S(1)}, u32[]{:S(2)}) copy-start(f32[256]{0:T(256)S(1)} %get-tuple-element.145) | copy-start | bytes 3076
  99.0 46.5 %collective-permute-start.3 = (bf16[768,384]{1,0:T(8,128)(2,1)}, bf16[768,384]{1,0:T(8,128)(2,1)}, u32[]{:S(2)}, u32[]{:S(2)}) collective-permute-start(bf16[768,384]{1,0:T(8,128)(2,1)} %constant_dynamic-slice_fusion.16), channel_id=1, source_target_pairs={{0,1},{1,0},{2,3},{3,2},{4,5},{5,4},{6,7},{7,6},{8,9},{9,8},{10,11... | collective-permute-start | bytes 1769480 | tf_op jit(solution)/shard_map/ppermute | solution.py:334
  136.4 9.1 %collective-permute-start.6 = (bf16[768,384]{1,0:T(8,128)(2,1)}, bf16[768,384]{1,0:T(8,128)(2,1)}, u32[]{:S(2)}, u32[]{:S(2)}) collective-permute-start(bf16[768,384]{1,0:T(8,128)(2,1)} %constant_dynamic-slice_fusion.11), channel_id=1, source_target_pairs={{0,1},{1,0},{2,3},{3,2},{4,5},{5,4},{6,7},{7,6},{8,9},{9,8},{10,11... | collective-permute-start | bytes 1769480 | tf_op jit(solution)/shard_map/ppermute | solution.py:334
  149.9 16.1 %slice-start = ((f32[5,1792]{1,0:T(8,128)}), f32[5,256]{1,0:T(8,128)S(1)}, s32[]{:S(2)}) async-start(f32[5,1792]{1,0:T(8,128)} %copy-done.23), calls=%async_computation.4 | async-start | bytes 16384 | tf_op jit(solution)/shard_map/slice | solution.py:388
  149.9 17.3 %copy-start.9 = (bf16[768,384]{1,0:T(8,128)(2,1)S(1)}, bf16[768,384]{1,0:T(8,128)(2,1)}, u32[]{:S(2)}) copy-start(bf16[768,384]{1,0:T(8,128)(2,1)} %get-tuple-element.103) | copy-start | bytes 1769476
  164.0 4.4 %collective-permute-start.4 = (f32[512,128]{1,0:T(8,128)}, f32[512,128]{1,0:T(8,128)}, u32[]{:S(2)}, u32[]{:S(2)}) collective-permute-start(f32[512,128]{1,0:T(8,128)} %get-tuple-element.32), channel_id=1, source_target_pairs={{0,1},{1,0},{2,3},{3,2},{4,5},{5,4},{6,7},{7,6},{8,9},{9,8},{10,11... | collective-permute-start | bytes 786440 | tf_op jit(solution)/shard_map/ppermute | solution.py:334
  165.2 4.8 %collective-permute-start.5 = (bf16[256,768]{1,0:T(8,128)(2,1)S(1)}, bf16[256,768]{1,0:T(8,128)(2,1)S(1)}, u32[]{:S(2)}, u32[]{:S(2)}) collective-permute-start(bf16[256,768]{1,0:T(8,128)(2,1)S(1)} %constant_dynamic-slice_fusion.12), channel_id=1, source_target_pairs={{0,1},{1,0},{2,3},{3,2},{4,5},{5,4},{6,7},{7,6},{8,9},{9,8},{10,11... | collective-permute-start | bytes 1179656 | tf_op jit(solution)/shard_map/ppermute | solution.py:334
  170.0 18.3 %copy-start.18 = (bf16[256,768]{1,0:T(8,128)(2,1)}, bf16[256,768]{1,0:T(8,128)(2,1)S(1)}, u32[]{:S(2)}) copy-start(bf16[256,768]{1,0:T(8,128)(2,1)S(1)} %collective-permute-done.5) | copy-start | bytes 1179652
  174.2 15.8 %copy-start.5 = (bf16[1,256,768]{2,1,0:T(8,128)(2,1)S(1)}, bf16[1,256,768]{2,1,0:T(8,128)(2,1)}, u32[]{:S(2)}) copy-start(bf16[1,256,768]{2,1,0:T(8,128)(2,1)} %param.19) | copy-start | bytes 1179652
  188.3 4.2 %collective-permute-start.7 = (f32[512,128]{1,0:T(8,128)}, f32[512,128]{1,0:T(8,128)S(1)}, u32[]{:S(2)}, u32[]{:S(2)}) collective-permute-start(f32[512,128]{1,0:T(8,128)} %get-tuple-element.35), channel_id=1, source_target_pairs={{0,1},{1,0},{2,3},{3,2},{4,5},{5,4},{6,7},{7,6},{8,9},{9,8},{10,11... | collective-permute-start | bytes 786440 | tf_op jit(solution)/shard_map/ppermute | solution.py:334
  189.6 4.0 collective-permute-start.8
  226.9 22.7 %collective-permute-start.9 = (bf16[256,768]{1,0:T(8,128)(2,1)}, bf16[256,768]{1,0:T(8,128)(2,1)}, u32[]{:S(2)}, u32[]{:S(2)}) collective-permute-start(bf16[256,768]{1,0:T(8,128)(2,1)} %constant_dynamic-slice_fusion.7), channel_id=1, source_target_pairs={{0,1},{1,0},{2,3},{3,2},{4,5},{5,4},{6,7},{7,6},{8,9},{9,8},{10,11... | collective-permute-start | bytes 1179656 | tf_op jit(solution)/shard_map/ppermute | solution.py:334
  249.3 6.7 %collective-permute-start.13 = (bf16[768,384]{1,0:T(8,128)(2,1)}, bf16[768,384]{1,0:T(8,128)(2,1)}, u32[]{:S(2)}, u32[]{:S(2)}) collective-permute-start(bf16[768,384]{1,0:T(8,128)(2,1)} %constant_dynamic-slice_fusion.4), channel_id=1, source_target_pairs={{0,1},{1,0},{2,3},{3,2},{4,5},{5,4},{6,7},{7,6},{8,9},{9,8},{10,11... | collective-permute-start | bytes 1769480 | tf_op jit(solution)/shard_map/ppermute | solution.py:334
  260.0 74.5 %all-to-all-start.3 = ((bf16[64,8,4096]{2,1,0:T(8,128)(2,1)}), bf16[64,8,4096]{2,1,0:T(8,128)(2,1)}, u32[]{:S(2)}, u32[]{:S(2)}) async-start(bf16[64,8,4096]{2,1,0:T(8,128)(2,1)} %fusion.8), calls=%async_computation.3 | async-start | bytes 8388608 | tf_op jit(solution)/shard_map/all_to_all | solution.py:435
  306.7 21.8 %collective-permute-start.10 = (bf16[256,768]{1,0:T(8,128)(2,1)}, bf16[256,768]{1,0:T(8,128)(2,1)S(1)}, u32[]{:S(2)}, u32[]{:S(2)}) collective-permute-start(bf16[256,768]{1,0:T(8,128)(2,1)} %constant_dynamic-slice_fusion.6), channel_id=1, source_target_pairs={{0,1},{1,0},{2,3},{3,2},{4,5},{5,4},{6,7},{7,6},{8,9},{9,8},{10,11... | collective-permute-start | bytes 1179656 | tf_op jit(solution)/shard_map/ppermute | solution.py:334
  312.3 16.2 %copy-start.16 = (bf16[512,768]{1,0:T(8,128)(2,1)S(1)}, bf16[512,768]{1,0:T(8,128)(2,1)}, u32[]{:S(2)}) copy-start(bf16[512,768]{1,0:T(8,128)(2,1)} %get-tuple-element.42) | copy-start | bytes 2359300
  328.0 2.6 collective-permute-start.11
  334.5 10.4 %copy-start.34 = (f32[256]{0:T(256)S(1)}, f32[256]{0:T(256)}, u32[]{:S(2)}) copy-start(f32[256]{0:T(256)} %copy-done.33) | copy-start | bytes 3076
  334.5 10.5 %copy-start.37 = (f32[256]{0:T(256)S(1)}, f32[256]{0:T(256)}, u32[]{:S(2)}) copy-start(f32[256]{0:T(256)} %get-tuple-element.144) | copy-start | bytes 3076
  334.6 64.3 %all-to-all-start.2 = ((bf16[64,8,4096]{2,1,0:T(8,128)(2,1)}), bf16[64,8,4096]{2,1,0:T(8,128)(2,1)}, u32[]{:S(2)}, u32[]{:S(2)}) async-start(bf16[64,8,4096]{2,1,0:T(8,128)(2,1)} %fusion.5), calls=%async_computation.2 | async-start | bytes 8388608 | tf_op jit(solution)/shard_map/all_to_all | solution.py:435
  349.0 2.2 collective-permute-start.14
  349.7 1.2 collective-permute-start.18
  349.8 1.5 collective-permute-start.16
  398.8 10.6 %copy-start.1 = (f32[2,3,24]{2,0,1:T(2,128)S(1)}, f32[2,3,24]{2,0,1:T(2,128)}, u32[]{:S(2)}) copy-start(f32[2,3,24]{2,0,1:T(2,128)} %param.18) | copy-start | bytes 1732
  401.8 6.6 %collective-permute-start.12 = (f32[6,1920]{1,0:T(8,128)S(1)}, f32[6,1920]{1,0:T(8,128)S(1)}, u32[]{:S(2)}, u32[]{:S(2)}) collective-permute-start(f32[6,1920]{1,0:T(8,128)S(1)} %fusion.48), channel_id=1, source_target_pairs={{0,1},{1,0},{2,3},{3,2},{4,5},{5,4},{6,7},{7,6},{8,9},{9,8},{10,11... | collective-permute-start | bytes 138248 | tf_op jit(solution)/shard_map/ppermute | solution.py:334
  403.3 1.2 collective-permute-start.17
  403.4 4.3 %collective-permute-start.15 = (f32[12,384]{1,0:T(8,128)S(1)}, f32[12,384]{1,0:T(8,128)S(1)}, u32[]{:S(2)}, u32[]{:S(2)}) collective-permute-start(f32[12,384]{1,0:T(8,128)S(1)} %constant_dynamic-slice_fusion.3), channel_id=1, source_target_pairs={{0,1},{1,0},{2,3},{3,2},{4,5},{5,4},{6,7},{7,6},{8,9},{9,8},{10,11... | collective-permute-start | bytes 55304 | tf_op jit(solution)/shard_map/ppermute | solution.py:334
  (33 other events, 157.6 us)

commit v3 on v2

v3 whole, which is shorter than its diff:
```python
import functools

import jax
import jax.numpy as jnp
from jax import lax
from jax.experimental import pallas as pl
from jax.experimental.pallas import tpu as pltpu
from jax.sharding import Mesh
from jax.sharding import PartitionSpec as P

HEADS = 24
HEAD_DIM = 64
STATE = 128
INNER = 1536
CONV_CH = 1792
WIDTH = 768
TOKENS = 512
CHIPS = 64
HALF = 256
OWN_HEADS = 12
OWN = OWN_HEADS * HEAD_DIM
OWN_CONV = OWN + 2 * STATE
REST = OWN_CONV + 128
GATE_FOLD = OWN // 2
REST_FOLD = 640
GATE_COLS = OWN + GATE_FOLD
REST_COLS = REST + REST_FOLD
WIN_COLS = GATE_COLS + REST_COLS
OUT_COLS = 3 * (WIDTH // 2)
LAYER_COLS = WIN_COLS + OUT_COLS
VECTORS = OWN_HEADS
REMAINDERS = 64
VECTOR_COLS = 40
NORM_EPS = 1e-05
NEGATIVE = -1e30
F32 = jnp.float32
BF16 = jnp.bfloat16
HIGHEST = lax.Precision.HIGHEST


def dot(a, b, dims=((1,), (0,)), precision=None):
    return lax.dot_general(a, b, (dims, ((), ())), precision=precision, preferred_element_type=F32)


def dot_nt(a, b, precision=None):
    return dot(a, b, ((1,), (1,)), precision)


def dot_tn(a, b, precision=None):
    return dot(a, b, ((0,), (0,)), precision)


def iota(shape, dim):
    return lax.broadcasted_iota(jnp.int32, shape, dim)


def padded_orders():
    column = iota((WIDTH, 512), 1)
    row = iota((WIDTH, 512), 0)
    start = 12 * (column >> 3)
    place = column & 7
    features = (
        start + place,
        jnp.where(place < 4, start + place + 8, -1),
        jnp.where(place < 4, -1, start + place + 4),
    )
    return [jnp.where(feature == row, 1.0, 0.0).astype(BF16) for feature in features]


def head_spread():
    return jnp.where(iota((128, OWN), 0) == (iota((128, OWN), 1) >> 6), 1.0, 0.0).astype(F32)


def softplus(v):
    return jnp.maximum(v, 0.0) + jnp.log1p(jnp.exp(-jnp.abs(v)))


def tap_masks(segment_column):
    position = iota((TOKENS, 1), 0)
    wide = jnp.broadcast_to(segment_column, (TOKENS, 128))
    masks = [None]
    for back in range(1, 4):
        before = pltpu.roll(wide, back, 0)[:, :1]
        same = (before == segment_column) & (position >= back)
        masks.append(jnp.where(same, 1.0, 0.0).astype(F32))
    return masks


def convolved(signal, taps, masks):
    total = taps[3:4] * signal
    for back in range(1, 4):
        total = total + taps[3 - back : 4 - back] * (pltpu.roll(signal, back, 0) * masks[back])
    return total + taps[4:5]


def steps_of(raw, heads):
    shifted = raw + heads[0:1]
    step = softplus(shifted)
    log_decay = -step * jnp.exp(heads[1:2])
    lower = jnp.where(iota((TOKENS, TOKENS), 0) >= iota((TOKENS, TOKENS), 1), 1.0, 0.0).astype(F32)
    return shifted, step, dot(lower, log_decay, precision=HIGHEST)


def lane_masks():
    low = iota((1, 128), 1) < HEAD_DIM
    return (jnp.where(low, 1.0, 0.0).astype(BF16), jnp.where(low, 0.0, 1.0).astype(BF16))


def reordered(scaled):
    return [dot(scaled, order).astype(BF16) for order in padded_orders()]


def projected(parts, full, folded, fold):
    u_full, u_low, u_high = parts
    rest = full.shape[1] - fold
    left = dot(u_full, full[:, :fold]) + dot(u_low, folded)
    right = dot(u_full, full[:, fold:]) + dot(u_high, folded[:, :rest])
    return left, right


def weight_gradient(parts, grad, fold):
    u_full, u_low, u_high = parts
    rest = grad.shape[1] - fold
    folded = dot_tn(u_low, grad[:, :fold])
    high = dot_tn(u_high, grad[:, fold:])
    if rest < fold:
        high = jnp.concatenate([high, jnp.zeros((high.shape[0], fold - rest), F32)], axis=1)
    return dot_tn(u_full, grad), folded + high


def input_gradients(grad, full, folded, fold):
    rest = grad.shape[1] - fold
    return (
        dot_nt(grad, full),
        dot_nt(grad[:, :fold], folded),
        dot_nt(grad[:, fold:], folded[:, :rest]),
    )


def column_picks(maps, kind, columns):
    chips = maps[2 * kind : 2 * kind + 1, :columns]
    places = maps[2 * kind + 1 : 2 * kind + 2, :columns]
    rows = iota((512, 1), 0) >> 3
    keep = jnp.where(rows == chips, 1.0, 0.0).astype(F32)
    pick = jnp.where(iota((128, columns), 0) == places + VECTORS, 1.0, 0.0).astype(F32)
    return keep, pick


def vectors_from(tile, maps, kind, columns):
    keep, pick = column_picks(maps, kind, columns)
    spread = dot(tile, pick.astype(BF16)) * keep
    return jnp.sum(spread.reshape(CHIPS, 8, columns), axis=0)


def vectors_into(values, maps, kind):
    columns = values.shape[1]
    keep, pick = column_picks(maps, kind, columns)
    tiled = jnp.broadcast_to(values[None], (CHIPS, 8, columns)).reshape(512, columns)
    return dot_nt(tiled * keep, pick, precision=HIGHEST)


def only_row(values, row):
    return jnp.where(iota((8, 1), 0) == row, values, 0.0)


def fetched(source, target, semaphore, layer, columns):
    start = layer * LAYER_COLS
    return pltpu.make_async_copy(source.at[:, start : start + columns], target, semaphore)


def forward_kernel(
    layer, xhat_ref, weights_ref, wout_ref, segc_ref, segr_ref, heads_ref, maps_ref,
    gate_ref, rest_ref, y_ref, out_ref, square_ref, taps_ref, norm_ref, gain_ref,
    win_ref, dtx_ref, affinity_ref, bias_ref, semaphore,
):
    copy = fetched(weights_ref, win_ref, semaphore, layer, WIN_COLS)
    copy.start()
    segc = segc_ref[...]
    masks = tap_masks(segc)
    allowed = (iota((TOKENS, TOKENS), 0) >= iota((TOKENS, TOKENS), 1)) & (segc == segr_ref[...])
    bias_ref[...] = jnp.where(allowed, 0.0, NEGATIVE).astype(F32)
    copy.wait()
    maps = maps_ref[...]
    tile = win_ref[:, GATE_COLS + OWN_CONV : GATE_COLS + REST]
    taps = vectors_from(tile, maps, 0, OWN_CONV)
    norm = vectors_from(tile, maps, 1, WIDTH)[5:6]
    gain = vectors_from(tile, maps, 2, OWN)[6:7]
    taps_ref[...] = taps
    norm_ref[...] = jnp.broadcast_to(norm, norm_ref.shape)
    gain_ref[...] = jnp.broadcast_to(gain, gain_ref.shape)
    parts = reordered((xhat_ref[...].astype(F32) * norm).astype(BF16))
    rest_ref[:, :REST_FOLD], rest_ref[:, REST_FOLD:] = projected(
        parts, win_ref[:, GATE_COLS : GATE_COLS + REST], win_ref[:, GATE_COLS + REST :], REST_FOLD
    )
    gate_ref[:, :GATE_FOLD], gate_ref[:, GATE_FOLD:] = projected(
        parts, win_ref[:, :OWN], win_ref[:, OWN:GATE_COLS], GATE_FOLD
    )
    heads = heads_ref[...]
    before = convolved(rest_ref[:, :OWN_CONV], taps, masks)
    active = before * jax.nn.sigmoid(before)
    inputs = active[:, :OWN]
    writers = active[:, OWN : OWN + STATE].astype(BF16)
    readers = active[:, OWN + STATE :].astype(BF16)
    _, step, cumul = steps_of(rest_ref[:, OWN_CONV:], heads)
    cumul_rows = cumul.T
    spread = head_spread()
    dtx_ref[...] = (dot(step, spread, precision=HIGHEST) * inputs).astype(BF16)
    y_ref[...] = dot(heads, spread, precision=HIGHEST)[2:3] * inputs
    affinity_ref[...] = dot_nt(readers, writers)
    halves = lane_masks()
    for pair in range(OWN_HEADS // 2):
        lanes = slice(128 * pair, 128 * pair + 128)
        pair_inputs = dtx_ref[:, lanes]
        for block in range(2):
            rows = slice(HALF * block, HALF * block + HALF)
            reach = HALF * (block + 1)
            total = y_ref[rows, lanes]
            for member in range(2):
                head = 2 * pair + member
                decay = jnp.exp(
                    cumul[rows, head : head + 1]
                    - cumul_rows[head : head + 1, :reach]
                    + bias_ref[rows, :reach]
                )
                mixing = (decay * affinity_ref[rows, :reach]).astype(BF16)
                total = total + dot(mixing, pair_inputs[:reach] * halves[member])
            y_ref[rows, lanes] = total
    gate = gate_ref[...]
    gated = y_ref[...] * (gate * jax.nn.sigmoid(gate))
    out_ref[...] = dot((gated * gain).astype(BF16), wout_ref[...]).astype(out_ref.dtype)
    square_ref[...] = jnp.broadcast_to(
        jnp.sum(gated * gated, axis=1, keepdims=True), square_ref.shape
    )


def vmem(count):
    return [pl.BlockSpec(memory_space=pltpu.VMEM)] * count


def forward_mix(layer, xhat, weights, wout, segc, segr, heads, maps, interpret=False):
    return pl.pallas_call(
        functools.partial(forward_kernel, layer),
        in_specs=vmem(1) + [pl.BlockSpec(memory_space=pl.ANY)] + vmem(5),
        out_shape=(
            jax.ShapeDtypeStruct((TOKENS, OWN), F32),
            jax.ShapeDtypeStruct((TOKENS, REST), F32),
            jax.ShapeDtypeStruct((TOKENS, OWN), F32),
            jax.ShapeDtypeStruct((TOKENS, WIDTH), BF16),
            jax.ShapeDtypeStruct((TOKENS, 128), F32),
            jax.ShapeDtypeStruct((8, OWN_CONV), F32),
            jax.ShapeDtypeStruct((8, WIDTH), F32),
            jax.ShapeDtypeStruct((8, OWN), F32),
        ),
        scratch_shapes=[
            pltpu.VMEM((512, WIN_COLS), BF16),
            pltpu.VMEM((TOKENS, OWN), BF16),
            pltpu.VMEM((TOKENS, TOKENS), F32),
            pltpu.VMEM((TOKENS, TOKENS), F32),
            pltpu.SemaphoreType.DMA,
        ],
        compiler_params=pltpu.CompilerParams(vmem_limit_bytes=58 * 2**20),
        interpret=interpret,
    )(xhat, weights, wout, segc, segr, heads, maps)


def gate_kernel(
    seed_ref, rho_ref, xhat_ref, norm_ref, wout_ref, gate_ref, y_ref, gain_ref,
    dgate_ref, dy_ref, dwin_ref, dwout_ref, dgain_ref,
):
    seed = seed_ref[:, :WIDTH]
    mean = seed_ref[:, WIDTH : WIDTH + 128].astype(F32)
    mean = mean[:, 0:1] + mean[:, 1:2]
    gain = gain_ref[0:1]
    rho = rho_ref[...]
    gate = gate_ref[...]
    y = y_ref[...]
    open_gate = jax.nn.sigmoid(gate)
    passed = gate * open_gate
    scaled = y * passed * rho
    dyn = dot_nt(seed, wout_ref[...])
    dwout_ref[...] = dot_tn((scaled * gain).astype(BF16), seed).astype(BF16)
    dgain_ref[...] = jnp.broadcast_to(jnp.sum(dyn * scaled, axis=0, keepdims=True), dgain_ref.shape)
    dgated = rho * (dyn * gain - scaled * mean)
    dy_ref[...] = dgated * passed
    dgate = (dgated * y * (open_gate * (1.0 + gate * (1.0 - open_gate)))).astype(BF16)
    dgate_ref[...] = dgate
    parts = reordered((xhat_ref[...].astype(F32) * norm_ref[0:1]).astype(BF16))
    full, folded = weight_gradient(parts, dgate, GATE_FOLD)
    dwin_ref[:, :OWN] = full.astype(BF16)
    dwin_ref[:, OWN:] = folded.astype(BF16)


def gate_back(seed, rho, xhat, norm, wout, gate, y, gain, interpret=False):
    return pl.pallas_call(
        gate_kernel,
        out_shape=(
            jax.ShapeDtypeStruct((TOKENS, OWN), BF16),
            jax.ShapeDtypeStruct((TOKENS, OWN), F32),
            jax.ShapeDtypeStruct((512, GATE_COLS), BF16),
            jax.ShapeDtypeStruct((OWN, WIDTH), BF16),
            jax.ShapeDtypeStruct((8, OWN), F32),
        ),
        compiler_params=pltpu.CompilerParams(vmem_limit_bytes=58 * 2**20),
        interpret=interpret,
    )(seed, rho, xhat, norm, wout, gate, y, gain)


def backward_kernel(
    layer, dgate_ref, dy_ref, xhat_ref, norm_ref, weights_ref, rest_ref,
    segc_ref, segr_ref, taps_ref, heads_ref, dgain_ref, maps_ref,
    dscaled_ref, dwin_ref,
    win_ref, dtx_ref, affinity_ref, bias_ref, daffinity_ref, drest_ref, dact_ref, rise_ref,
    direct_ref, dtaps_ref, semaphore,
):
    copy = fetched(weights_ref, win_ref, semaphore, layer, WIN_COLS)
    copy.start()
    taps = taps_ref[...]
    heads = heads_ref[...]
    segc = segc_ref[...]
    masks = tap_masks(segc)
    signal = rest_ref[:, :OWN_CONV]
    before = convolved(signal, taps, masks)
    open_act = jax.nn.sigmoid(before)
    active = before * open_act
    inputs = active[:, :OWN]
    writers = active[:, OWN : OWN + STATE].astype(BF16)
    readers = active[:, OWN + STATE :].astype(BF16)
    shifted, step, cumul = steps_of(rest_ref[:, OWN_CONV:], heads)
    cumul_rows = cumul.T
    spread = head_spread()
    step_wide = dot(step, spread, precision=HIGHEST)
    skip_wide = dot(heads, spread, precision=HIGHEST)[2:3]
    dtx_ref[...] = (step_wide * inputs).astype(BF16)
    allowed = (iota((TOKENS, TOKENS), 0) <= iota((TOKENS, TOKENS), 1)) & (segc == segr_ref[...])
    bias_ref[...] = jnp.where(allowed, 0.0, NEGATIVE).astype(F32)
    affinity_ref[...] = dot_nt(writers, readers)
    daffinity_ref[...] = jnp.zeros_like(daffinity_ref)
    rise_ref[...] = jnp.zeros_like(rise_ref)
    halves = lane_masks()
    head_lane = iota((1, 128), 1)
    fall_blocks = [jnp.zeros((HALF, 128), F32), jnp.zeros((HALF, 128), F32)]
    for pair in range(OWN_HEADS // 2):
        lanes = slice(128 * pair, 128 * pair + 128)
        pair_inputs = dtx_ref[:, lanes]
        pair_dy = dy_ref[:, lanes].astype(BF16)
        member_dy = [pair_dy * half for half in halves]
        for block in range(2):
            rows = slice(HALF * block, HALF * block + HALF)
            start = HALF * block
            dinput = jnp.zeros((HALF, 128), F32)
            for member in range(2):
                head = 2 * pair + member
                decay = jnp.exp(
                    cumul_rows[head : head + 1, start:]
                    - cumul[rows, head : head + 1]
                    + bias_ref[rows, start:]
                )
                dmixing = dot_nt(pair_inputs[rows], member_dy[member][start:]) * decay
                daffinity_ref[rows, start:] += dmixing
                affinity = affinity_ref[rows, start:]
                dinput = dinput + dot((decay * affinity).astype(BF16), member_dy[member][start:])
                dspread = dmixing * affinity
                fall = jnp.sum(dspread, axis=1, keepdims=True)
                fall_blocks[block] = fall_blocks[block] + jnp.where(head_lane == head, fall, 0.0)
                rise_ref[head : head + 1, start:] += jnp.sum(dspread, axis=0, keepdims=True)
            direct_ref[rows, lanes] = dinput
    dinputs = direct_ref[...]
    dy = dy_ref[...]
    dact_ref[:, :OWN] = step_wide * dinputs + skip_wide * dy
    daffinity = daffinity_ref[...].astype(BF16)
    dact_ref[:, OWN : OWN + STATE] = dot(daffinity, readers)
    dact_ref[:, OWN + STATE :] = dot_tn(daffinity, writers)
    dstep = dot_nt(dinputs * inputs, spread, precision=HIGHEST)
    skip_sum = jnp.broadcast_to(jnp.sum(dy * inputs, axis=0, keepdims=True), (8, OWN))
    dskip = dot_nt(skip_sum, spread, precision=HIGHEST)[0:1]
    dcumul = rise_ref[...].T - jnp.concatenate(fall_blocks, axis=0)
    upper = jnp.where(iota((TOKENS, TOKENS), 0) <= iota((TOKENS, TOKENS), 1), 1.0, 0.0).astype(F32)
    dlog = dot(upper, dcumul, precision=HIGHEST)
    rate = jnp.exp(heads[1:2])
    draw = (dstep - dlog * rate) * jax.nn.sigmoid(shifted)
    head_rows = (
        jnp.sum(draw, axis=0, keepdims=True),
        jnp.sum(-dlog * step * rate, axis=0, keepdims=True),
        dskip,
    )
    drest_ref[:, OWN_CONV:] = draw.astype(BF16)

    dconv = dact_ref[...] * (open_act * (1.0 + before * (1.0 - open_act)))
    dtaps_ref[...] = jnp.zeros_like(dtaps_ref)
    dtaps_ref[4:5] = jnp.sum(dconv, axis=0, keepdims=True)
    dtaps_ref[3:4] = jnp.sum(dconv * signal, axis=0, keepdims=True)
    dsignal = taps[3:4] * dconv
    for back in range(1, 4):
        masked = dconv * masks[back]
        dtaps_ref[3 - back : 4 - back] = jnp.sum(
            masked * pltpu.roll(signal, back, 0), axis=0, keepdims=True
        )
        dsignal = dsignal + taps[3 - back : 4 - back] * pltpu.roll(masked, TOKENS - back, 0)
    drest_ref[:, :OWN_CONV] = dsignal.astype(BF16)

    norm = norm_ref[0:1]
    xhat = xhat_ref[...].astype(F32)
    orders = padded_orders()
    u = (xhat * norm).astype(BF16)
    parts = [dot(u, order).astype(BF16) for order in orders]
    drest = drest_ref[...]
    copy.wait()
    from_rest = input_gradients(
        drest, win_ref[:, GATE_COLS : GATE_COLS + REST], win_ref[:, GATE_COLS + REST :], REST_FOLD
    )
    from_gate = input_gradients(
        dgate_ref[...], win_ref[:, :OWN], win_ref[:, OWN:GATE_COLS], GATE_FOLD
    )
    du = jnp.zeros((TOKENS, WIDTH), F32)
    for one, other, order in zip(from_rest, from_gate, orders):
        du = du + dot_nt((one + other).astype(BF16), order)
    dscaled_ref[...] = (du * norm).astype(BF16)

    full, folded = weight_gradient(parts, drest, REST_FOLD)
    dwin_ref[:, :OWN_CONV] = full[:, :OWN_CONV].astype(BF16)
    dwin_ref[:, REST:] = folded.astype(BF16)
    maps = maps_ref[...]
    dnorm = jnp.sum(du * xhat, axis=0, keepdims=True)
    vectors = (
        vectors_into(dtaps_ref[...], maps, 0)
        + vectors_into(only_row(dnorm, 5), maps, 1)
        + vectors_into(only_row(dgain_ref[...], 6), maps, 2)
    )
    last_row = jnp.zeros((8, 128), F32)
    for place, row in enumerate(head_rows):
        shift = VECTORS + OWN_HEADS * place
        last_row = last_row + pltpu.roll(jnp.broadcast_to(row, (8, 128)), shift, 1)
    vectors = vectors + jnp.where((iota((512, 1), 0) & 7) == 7, last_row[0:1], 0.0)
    high = vectors.astype(BF16).astype(F32)
    low = pltpu.roll(vectors - high, REMAINDERS - VECTORS, 1)
    dwin_ref[:, OWN_CONV:REST] = (full[:, OWN_CONV:] + high + low).astype(BF16)


def backward_mix(
    layer, dgate, dy, xhat, norm, weights, rest, segc, segr, taps, heads, dgain, maps,
    interpret=False,
):
    square = (TOKENS, TOKENS)
    return pl.pallas_call(
        functools.partial(backward_kernel, layer),
        in_specs=vmem(4) + [pl.BlockSpec(memory_space=pl.ANY)] + vmem(7),
        out_shape=(
            jax.ShapeDtypeStruct((TOKENS, WIDTH), BF16),
            jax.ShapeDtypeStruct((512, REST_COLS), BF16),
        ),
        scratch_shapes=[
            pltpu.VMEM((512, WIN_COLS), BF16),
            pltpu.VMEM((TOKENS, OWN), BF16),
            pltpu.VMEM(square, F32),
            pltpu.VMEM(square, F32),
            pltpu.VMEM(square, F32),
            pltpu.VMEM((TOKENS, REST), BF16),
            pltpu.VMEM((TOKENS, OWN_CONV), F32),
            pltpu.VMEM((128, TOKENS), F32),
            pltpu.VMEM((TOKENS, OWN), F32),
            pltpu.VMEM((8, OWN_CONV), F32),
            pltpu.SemaphoreType.DMA,
        ],
        compiler_params=pltpu.CompilerParams(vmem_limit_bytes=58 * 2**20),
        interpret=interpret,
    )(dgate, dy, xhat, norm, weights, rest, segc, segr, taps, heads, dgain, maps)


DP = ("dp_0", "dp_1", "dp_2")
DP_SEQ = DP + ("seq",)
LAYERS = 2


def swapped(v):
    return lax.ppermute(v, "seq", [(0, 1), (1, 0)])


def part(v, index, size, axis):
    return lax.dynamic_slice_in_dim(v, index * size, size, axis)


def in_order(core, own, other, axis):
    first = jnp.where(core == 0, own, other)
    second = jnp.where(core == 0, other, own)
    return jnp.concatenate([first, second], axis=axis)


def padded(v, sizes):
    return jnp.pad(v, [(0, size - now) for now, size in zip(v.shape, sizes)])


def folded_rows(rows, fold):
    tail = padded(rows[:, 8:], (LAYERS, 4, 2 * fold)).reshape(LAYERS, 4, 2, fold)
    return tail.transpose(0, 2, 1, 3).reshape(LAYERS, 8, fold)


def packed_weights(win, wout, kernel_weight, kernel_bias, norm_gain, gate_gain, core):
    win = in_order(core, win, swapped(win), 1)
    wout = in_order(core, wout, swapped(wout), 1)
    rows = [kernel_weight, kernel_bias[:, None]]
    rows += [padded(vector[:, None], (LAYERS, 1, 14)) for vector in (norm_gain, gate_gain)]
    vectors = padded(jnp.concatenate(rows, axis=1), (LAYERS, 8, 14))
    others = swapped(vectors)
    first = jnp.where(core == 0, vectors, others)
    second = jnp.where(core == 0, others, vectors)
    joined = []
    for start, stop, size in ((0, 5, 14), (5, 6, 6), (6, 8, 12)):
        both = [first[:, start:stop, :size], second[:, start:stop, :size]]
        both = jnp.concatenate(both, axis=2)
        joined.append(padded(both, both.shape[:2] + (128 - OWN_HEADS,)))
    vectors = jnp.concatenate(joined, axis=1)
    gate = part(win[:, :, :INNER], core, OWN, 2)
    steps = part(win[:, :, INNER + CONV_CH :], core, OWN_HEADS, 2)
    tail = padded(steps[:, 8:], (LAYERS, 4, 128))
    tile = jnp.concatenate([steps[:, :8], vectors], axis=2)
    rest = jnp.concatenate(
        [
            part(win[:, :, INNER : 2 * INNER], core, OWN, 2),
            win[:, :, 2 * INNER : INNER + CONV_CH],
            jnp.concatenate([tile, tail], axis=1),
        ],
        axis=2,
    )
    wout = part(wout, core, WIDTH // 2, 2)
    wout = wout.reshape(LAYERS, 3, 8, WIDTH // 2).transpose(0, 2, 1, 3)
    block = jnp.concatenate(
        [
            gate[:, :8],
            folded_rows(gate, GATE_FOLD),
            rest[:, :8],
            folded_rows(rest, REST_FOLD),
            wout.reshape(LAYERS, 8, OUT_COLS),
        ],
        axis=2,
    )
    return block.transpose(1, 0, 2).reshape(8, LAYERS * LAYER_COLS)


def output_weights(gathered, core):
    wout = gathered.reshape(CHIPS, 8, LAYERS, LAYER_COLS)[:, :, :, WIN_COLS:]
    wout = wout.reshape(CHIPS, 8, LAYERS, 3, WIDTH // 2).transpose(2, 0, 3, 1, 4)
    wout = wout.reshape(LAYERS, INNER, WIDTH // 2)
    return in_order(core, part(wout, core, OWN, 1), swapped(part(wout, 1 - core, OWN, 1)), 2)


def vector_maps(core):
    column = jnp.arange(OWN_CONV)
    channel = jnp.where(column < OWN, column + core * OWN, column - OWN + INNER)
    feature = column + core * OWN
    rows = [channel // 28, channel % 28, column // 12, column % 12, feature // 24, feature % 24]
    return padded(jnp.stack(rows).astype(jnp.int32), (8, OWN_CONV))


def over_positions(partial_sum, core):
    own = part(partial_sum, core, HALF, 0).astype(F32)
    return own + swapped(part(partial_sum, 1 - core, HALF, 0)).astype(F32)


def reduced(packed):
    arrived = lax.all_to_all(packed, DP, 0, 0, tiled=True)
    return jnp.sum(arrived.astype(F32), axis=0)


def reduced_output(dwout, core):
    half = WIDTH // 2
    dwout = in_order(core, part(dwout, core, half, 1), swapped(part(dwout, 1 - core, half, 1)), 0)
    dwout = dwout.reshape(CHIPS, 3, 8, half).transpose(0, 2, 1, 3)
    return reduced(dwout.reshape(CHIPS, 8, OUT_COLS))


def reduced_input(dwin):
    return reduced(dwin.reshape(CHIPS, 8, dwin.shape[1]))


def unfolded(total, columns, fold):
    tail = total[:, columns:].reshape(2, 4, fold).transpose(1, 0, 2).reshape(4, 2 * fold)
    return jnp.concatenate([total[:, :columns], tail[:, :columns]], axis=0)


def unpacked_gradients(gate_total, out_total, rest_total, core):
    win = jnp.concatenate(
        [unfolded(gate_total, OWN, GATE_FOLD), unfolded(rest_total, REST, REST_FOLD)], axis=1
    )
    own = part(win, core, 6, 0)
    got = swapped(part(win, 1 - core, 6, 0))
    left = jnp.where(core == 0, own, got)
    right = jnp.where(core == 0, got, own)
    shared = slice(2 * OWN, 2 * OWN + 2 * STATE)
    steps = slice(2 * OWN + 2 * STATE, 2 * OWN + 2 * STATE + OWN_HEADS)
    dwin = jnp.concatenate(
        [
            left[:, :OWN],
            right[:, :OWN],
            left[:, OWN : 2 * OWN],
            right[:, OWN : 2 * OWN],
            left[:, shared] + right[:, shared],
            left[:, steps],
            right[:, steps],
        ],
        axis=1,
    )
    half = WIDTH // 2
    wout = out_total.reshape(8, 3, half).transpose(1, 0, 2).reshape(24, half)
    dwout = in_order(core, part(wout, core, 12, 0), swapped(part(wout, 1 - core, 12, 0)), 1)
    tile = rest_total[:, OWN_CONV:REST]
    vectors = tile[:, VECTORS : VECTORS + VECTOR_COLS] + tile[:, REMAINDERS : REMAINDERS + VECTOR_COLS]
    others = swapped(vectors)
    heads = in_order(core, vectors[7, :36].reshape(3, 12), others[7, :36].reshape(3, 12), 1)
    vectors = vectors + others
    taps = part(vectors[:5, :28], core, 14, 1)
    return (
        dwin,
        dwout,
        taps[:4],
        taps[4],
        part(vectors[5, :12], core, 6, 0),
        part(vectors[6, :24], core, 12, 0),
        heads,
    )


def mean_square_scale(values):
    return lax.rsqrt(jnp.mean(values * values, axis=1, keepdims=True) + NORM_EPS)


def layers_of(
    hidden, cotangent, segments, head_values, weights, wouts, core, send_gate, send_rest,
    interpret=False,
):
    segr = segments
    segc = segments.reshape(TOKENS, 1)
    heads_all = padded(part(head_values, core, OWN_HEADS, 2), (LAYERS, 8, 128))
    maps = vector_maps(core)
    current = hidden.astype(F32)
    saved = []
    for layer in range(LAYERS):
        sigma = mean_square_scale(current)
        xhat = lax.all_gather((current * sigma).astype(BF16), "seq", axis=0, tiled=True)
        gate, rest, y, out, square, taps, norm, gain = forward_mix(
            layer, xhat, weights, wouts[layer], segc, segr, heads_all[layer], maps,
            interpret=interpret,
        )
        square = square + swapped(square)
        rho = lax.rsqrt(square[:, :1] / INNER + NORM_EPS)
        branch = over_positions(out, core)
        own_rho = part(rho, core, HALF, 0)
        saved.append((current, sigma, xhat, gate, rest, y, rho, own_rho, branch, taps, norm, gain))
        current = current + own_rho * branch
    upstream = cotangent.astype(F32)
    sent = [None] * LAYERS
    for layer in reversed(range(LAYERS)):
        before, sigma, xhat, gate, rest, y, rho, own_rho, branch, taps, norm, gain = saved[layer]
        seed = upstream.astype(BF16)
        mean = own_rho * jnp.sum(seed.astype(F32) * branch, axis=1, keepdims=True) / INNER
        high = lax.reduce_precision(mean, 8, 7)
        means = jnp.concatenate([high, mean - high], axis=1).astype(BF16)
        seed = jnp.concatenate([seed, padded(means, (HALF, 128))], axis=1)
        seed = lax.all_gather(seed, "seq", axis=0, tiled=True)
        dgate, dy, dwin_gate, dwout, dgain = gate_back(
            seed, rho, xhat, norm, wouts[layer], gate, y, gain, interpret=interpret
        )
        early = send_gate(dwin_gate, dwout)
        dscaled, dwin_rest = backward_mix(
            layer, dgate, dy, xhat, norm, weights, rest, segc, segr, taps, heads_all[layer],
            dgain, maps, interpret=interpret,
        )
        sent[layer] = early + (send_rest(dwin_rest),)
        scaled = over_positions(dscaled, core)
        upstream = upstream + sigma * (
            scaled
            - before * (sigma * sigma) * jnp.mean(scaled * before, axis=1, keepdims=True)
        )
    return current.astype(BF16), upstream.astype(BF16), sent


def per_device(
    hidden_in,
    segments,
    projection_in,
    projection_out,
    kernel_weight,
    kernel_bias,
    norm_gain,
    gate_gain,
    head_values,
    cotangent,
):
    core = lax.axis_index("seq")
    block = packed_weights(
        projection_in, projection_out, kernel_weight, kernel_bias, norm_gain, gate_gain, core
    )
    weights = lax.all_gather(block, DP, axis=0, tiled=True)
    wouts = output_weights(weights, core)

    def send_gate(dwin, dwout):
        return reduced_input(dwin), reduced_output(dwout, core)

    hidden_out, input_gradient, totals = layers_of(
        hidden_in[0], cotangent[0], segments, head_values, weights, wouts, core, send_gate,
        reduced_input,
    )
    pieces = [unpacked_gradients(*total, core) for total in totals]
    stacked = tuple(jnp.stack([piece[slot] for piece in pieces]) for slot in range(7))
    return (hidden_out[None], input_gradient[None]) + stacked


def solution(mesh):
    torus = Mesh(mesh.devices.reshape(4, 4, 4, mesh.shape["seq"]), DP_SEQ)
    tokens = P(DP, "seq", None)
    weights = (
        P(None, DP_SEQ, None),
        P(None, DP_SEQ, None),
        P(None, None, DP_SEQ),
        P(None, DP_SEQ),
        P(None, DP_SEQ),
        P(None, DP_SEQ),
    )
    return jax.shard_map(
        per_device,
        mesh=torus,
        in_specs=(tokens, P(DP, None)) + weights + (P(), tokens),
        out_specs=(tokens, tokens) + weights + (P(),),
        check_vma=False,
    )
```

time: 418 us -> 401 us (0.959)
  blocking collectives: 78.4 us -> 10.7 us
  waiting for transfers between devices: 82.7 us -> 148 us
  local copies, waits for them, and re-layouts: 81.8 us -> 25.6 us
  starting transfers between devices: 38.8 us -> 63.2 us
  Pallas kernels: 83.5 us -> 105 us
  other arithmetic: 42.3 us -> 27.6 us
  between operations: 2.29 us -> 15.2 us
    all_gather x0 -> x1, waiting for transfers between devices: none -> 81 us  [per_device(): weights = lax.all_gather(block, DP, axis=0, tiled=True)]
    all_to_all x1 -> x0, blocking collectives: 61.7 us -> none  [gathered_weights(): return lax.all_to_all(spread, DP, 0, 0, tiled=True)]
    pallas_call x4 -> x6, Pallas kernels: 83.5 us -> 105 us  [the longest x2 58.6 us: backward_mix(): pl.pallas_call(functools.partial(backward_kernel, layer), in_specs=vmem(4...]
    all_to_all x3 -> x6, waiting for transfers between devices: 80.2 us -> 62.2 us  [reduced(): arrived = lax.all_to_all(packed, DP, 0, 0, tiled=True)]
    all_to_all x3 -> x6, starting transfers between devices: 25.2 us -> 41.7 us  [reduced(): arrived = lax.all_to_all(packed, DP, 0, 0, tiled=True)]
    slice x51 -> x28, local copies, waits for them, and re-layouts: 16.5 us -> 2.03 us  [the longest x1 1.84 us: output_weights(): wout = gathered.reshape(CHIPS, 8, LAYERS, LAYER_COLS)[:, :, :, WIN_COLS:]]
    optimization_barrier x1 -> x0, local copies, waits for them, and re-layouts: 9.17 us -> none  [per_device(): first, later = lax.optimization_barrier((first, blocks[1]))]
    concatenate x16 -> x11, other arithmetic: 10.5 us -> 2.31 us  [the longest x2 1.07 us: layers_of(): seed = jnp.concatenate([seed, padded(means, (HALF, 128))], axis=1)]
  transfers between devices with their start and end apart: 22 -> 25, of which waited for: 6 -> 14; matrix products, arithmetic and copies ran while one was open for 24% -> 9% of each run, Pallas kernels for 7% -> 9%
where the time goes in v3:
time: 401 us; the launch traced here: 396 us
  waiting for transfers between devices  148 us (37%)
  Pallas kernels  105 us (26%)
  starting transfers between devices  63.2 us (16%)
  other arithmetic  27.6 us (7%)
  local copies, waits for them, and re-layouts  25.6 us (6%)
  between operations  15.2 us (4%)
  blocking collectives  10.7 us (3%)
    all_gather x1, waiting for transfers between devices, per_device(): weights = lax.all_gather(block, DP, axis=0, tiled=True)  81 us
    all_to_all x6, waiting for transfers between devices, reduced(): arrived = lax.all_to_all(packed, DP, 0, 0, tiled=True)  62.2 us
    pallas_call x2, Pallas kernels, backward_mix(): pl.pallas_call(functools.partial(backward_kernel, layer), in_specs=vmem(4...  58.6 us
    all_to_all x6, starting transfers between devices, reduced(): arrived = lax.all_to_all(packed, DP, 0, 0, tiled=True)  41.7 us
    pallas_call x2, Pallas kernels, forward_mix(): pl.pallas_call(functools.partial(forward_kernel, layer), in_specs=vmem(1)...  30 us
    ppermute x18, starting transfers between devices, swapped(): return lax.ppermute(v, 'seq', [(0, 1), (1, 0)])  21.5 us
    pallas_call x2, Pallas kernels, gate_back(): pl.pallas_call(gate_kernel, out_shape=(jax.ShapeDtypeStruct((TOKENS, OWN)...  16.6 us
    dynamic_slice x20, local copies, waits for them, and re-layouts, part(): return lax.dynamic_slice_in_dim(v, index * size, size, axis)  10.1 us
  transfers between devices with their start and end apart: 25, of which 14 were waited for; matrix products, arithmetic and copies ran while one was open for 9% of the time, Pallas kernels for 9%

profile of v3, /device:TPU:1, one launch (start us, length us, event | category | flops | bytes accessed | tf_op | source)
XLA Modules:
  0.0 395.9 jit_solution(15828894285007232652)
XLA Ops:
  17.6 81.0 %all-gather.2.cloned.1.call-done.weights_ref = bf16[512,8192]{1,0:T(8,128)(2,1)} async-done(((bf16[8,8192]{1,0:T(8,128)(2,1)}), bf16[512,8192]{1,0:T(8,128)(2,1)}) %all-gather.2.cloned.1.call-update) | async-done | bytes 8388624 | tf_op jit(solution)/shard_map/all_gather | solution.py:692
  98.6 1.8 slice.296
  105.2 2.7 all_gather.15.xhat_ref
  107.9 1.7 broadcast_select_fusion
  111.3 15.0 %shard_map.169 = (f32[512,768]{1,0:T(8,128)}, f32[512,1152]{1,0:T(8,128)}, f32[512,768]{1,0:T(8,128)}, bf16[512,768]{1,0:T(8,128)(2,1)}, f32[512,128]{1,0:T(8,12...) custom-call(bf16[512,768]{1,0:T(8,128)(2,1)} %all_gather.15.xhat_ref, ...), custom_call_target="tpu_custom_call" | custom-call | tf_op jit(solution)/shard_map/pallas_call | solution.py:241
  130.3 2.5 all_gather.17.xhat_ref
  132.8 15.0 %shard_map.170 = (f32[512,768]{1,0:T(8,128)}, f32[512,1152]{1,0:T(8,128)}, f32[512,768]{1,0:T(8,128)}, bf16[512,768]{1,0:T(8,128)(2,1)}, f32[512,128]{1,0:T(8,12...) custom-call(bf16[512,768]{1,0:T(8,128)(2,1)} %all_gather.17.xhat_ref, ...), custom_call_target="tpu_custom_call" | custom-call | tf_op jit(solution)/shard_map/pallas_call | solution.py:241
  152.4 2.8 all_gather.18.seed_ref
  155.2 8.3 %shard_map.171 = (bf16[512,768]{1,0:T(8,128)(2,1)}, f32[512,768]{1,0:T(8,128)}, bf16[512,1152]{1,0:T(8,128)(2,1)}, bf16[768,768]{1,0:T(8,128)(2,1)}, f32[8,768]{1,0:T(8,128)}) custom-call(bf16[512,896]{1,0:T(8,128)(2,1)} %all_gather.18.seed_ref, f32[512,1]{1,0:T(8,128)} %copy-done.10, bf16[512,768]{1,0:T(8,128)(2,1)} %all_gather.17.xhat_ref, ...), custom_call_target="tpu_custom_call" | custom-call | tf_op jit(solution)/shard_map/pallas_call | solution.py:294
  163.5 29.4 %shard_map.172 = (bf16[512,768]{1,0:T(8,128)(2,1)}, bf16[512,1792]{1,0:T(8,128)(2,1)}) custom-call(bf16[512,768]{1,0:T(8,128)(2,1)} %get-tuple-element.47.dgate_ref, f32[512,768]{1,0:T(8,128)} %get-tuple-element.48.dy_ref, bf16[512,768]{1,0:T(8,128)(2,1)} %all_gather.17.xhat_ref, f32[8,768]{1,0:T(8,128)} %get-tuple-element.43.norm_ref, ...), custom_call_target="tpu_custom_call" | custom-call | tf_op jit(solution)/shard_map/pallas_call | solution.py:444
  192.9 1.8 constant_dynamic-slice_fusion.14
  194.9 8.3 %all-to-all-start.2 = ((bf16[64,8,1152]{2,1,0:T(8,128)(2,1)}), bf16[64,8,1152]{2,1,0:T(8,128)(2,1)S(1)}, u32[]{:S(2)}, u32[]{:S(2)}) async-start(bf16[64,8,1152]{2,1,0:T(8,128)(2,1)} %bitcast.116), calls=%async_computation.2 | async-start | bytes 2359296 | tf_op jit(solution)/shard_map/all_to_all | solution.py:560
  204.8 2.4 multiply_reduce_fusion
  208.6 2.8 all_gather.19.seed_ref
  211.4 8.3 %shard_map.173 = (bf16[512,768]{1,0:T(8,128)(2,1)}, f32[512,768]{1,0:T(8,128)}, bf16[512,1152]{1,0:T(8,128)(2,1)}, bf16[768,768]{1,0:T(8,128)(2,1)}, f32[8,768]{1,0:T(8,128)}) custom-call(bf16[512,896]{1,0:T(8,128)(2,1)} %all_gather.19.seed_ref, f32[512,1]{1,0:T(8,128)} %copy-done.9, bf16[512,768]{1,0:T(8,128)(2,1)} %all_gather.15.xhat_ref, ...), custom_call_target="tpu_custom_call" | custom-call | tf_op jit(solution)/shard_map/pallas_call | solution.py:294
  219.6 2.7 all-to-all-done.2
  223.4 7.3 %all-to-all-start = ((bf16[64,8,1152]{2,1,0:T(8,128)(2,1)}), bf16[64,8,1152]{2,1,0:T(8,128)(2,1)S(1)}, u32[]{:S(2)}, u32[]{:S(2)}) async-start(bf16[64,8,1152]{2,1,0:T(8,128)(2,1)} %bitcast.117), calls=%async_computation | async-start | bytes 2359296 | tf_op jit(solution)/shard_map/all_to_all | solution.py:560
  235.8 13.9 %all-to-all-done = bf16[64,8,1152]{2,1,0:T(8,128)(2,1)S(1)} async-done(((bf16[64,8,1152]{2,1,0:T(8,128)(2,1)}), bf16[64,8,1152]{2,1,0:T(8,128)(2,1)S(1)}, u32[]{:S(2)}, u32[]{:S(2)}) %all-to-all-start) | async-done | bytes 1179680 | tf_op jit(solution)/shard_map/all_to_all | solution.py:560
  250.7 5.3 %all-to-all-start.5 = ((bf16[64,8,1152]{2,1,0:T(8,128)(2,1)}), bf16[64,8,1152]{2,1,0:T(8,128)(2,1)S(1)}, u32[]{:S(2)}, u32[]{:S(2)}) async-start(bf16[64,8,1152]{2,1,0:T(8,128)(2,1)} %bitcast.112), calls=%async_computation.5 | async-start | bytes 2359296 | tf_op jit(solution)/shard_map/all_to_all | solution.py:560
  256.0 29.2 %shard_map.174 = (bf16[512,768]{1,0:T(8,128)(2,1)}, bf16[512,1792]{1,0:T(8,128)(2,1)}) custom-call(bf16[512,768]{1,0:T(8,128)(2,1)} %get-tuple-element.57.dgate_ref, f32[512,768]{1,0:T(8,128)} %get-tuple-element.58.dy_ref, bf16[512,768]{1,0:T(8,128)(2,1)} %all_gather.15.xhat_ref, f32[8,768]{1,0:T(8,128)} %get-tuple-element.53.norm_ref, ...), custom_call_target="tpu_custom_call" | custom-call | tf_op jit(solution)/shard_map/pallas_call | solution.py:444
  286.4 2.4 collective-permute-start.9
  288.8 2.0 constant_dynamic-slice_fusion.10
  292.0 10.1 %all-to-all-start.3 = ((bf16[64,8,1792]{2,1,0:T(8,128)(2,1)}), bf16[64,8,1792]{2,1,0:T(8,128)(2,1)S(1)}, u32[]{:S(2)}, u32[]{:S(2)}) async-start(bf16[64,8,1792]{2,1,0:T(8,128)(2,1)} %bitcast.115), calls=%async_computation.3 | async-start | bytes 3670016 | tf_op jit(solution)/shard_map/all_to_all | solution.py:560
  302.1 2.4 fusion.13
  311.1 16.4 %all-to-all-done.3 = bf16[64,8,1792]{2,1,0:T(8,128)(2,1)S(1)} async-done(((bf16[64,8,1792]{2,1,0:T(8,128)(2,1)}), bf16[64,8,1792]{2,1,0:T(8,128)(2,1)S(1)}, u32[]{:S(2)}, u32[]{:S(2)}) %all-to-all-start.3) | async-done | bytes 1835040 | tf_op jit(solution)/shard_map/all_to_all | solution.py:560
  327.5 5.8 %all-to-all-start.4 = ((bf16[64,8,1152]{2,1,0:T(8,128)(2,1)}), bf16[64,8,1152]{2,1,0:T(8,128)(2,1)S(1)}, u32[]{:S(2)}, u32[]{:S(2)}) async-start(bf16[64,8,1152]{2,1,0:T(8,128)(2,1)} %bitcast.111), calls=%async_computation.4 | async-start | bytes 2359296 | tf_op jit(solution)/shard_map/all_to_all | solution.py:560
  333.7 2.7 collective-permute-start.17
  337.8 12.6 %all-to-all-done.4 = bf16[64,8,1152]{2,1,0:T(8,128)(2,1)S(1)} async-done(((bf16[64,8,1152]{2,1,0:T(8,128)(2,1)}), bf16[64,8,1152]{2,1,0:T(8,128)(2,1)S(1)}, u32[]{:S(2)}, u32[]{:S(2)}) %all-to-all-start.4) | async-done | bytes 1179680 | tf_op jit(solution)/shard_map/all_to_all | solution.py:560
  350.4 4.9 %all-to-all-start.1 = ((bf16[64,8,1792]{2,1,0:T(8,128)(2,1)}), bf16[64,8,1792]{2,1,0:T(8,128)(2,1)S(1)}, u32[]{:S(2)}, u32[]{:S(2)}) async-start(bf16[64,8,1792]{2,1,0:T(8,128)(2,1)} %bitcast.114), calls=%async_computation.1 | async-start | bytes 3670016 | tf_op jit(solution)/shard_map/all_to_all | solution.py:560
  355.5 4.0 %collective-permute-start.13 = (f32[12,384]{1,0:T(8,128)S(1)}, f32[12,384]{1,0:T(8,128)S(1)}, u32[]{:S(2)}, u32[]{:S(2)}) collective-permute-start(f32[12,384]{1,0:T(8,128)S(1)} %constant_dynamic-slice_fusion.9), channel_id=1, source_target_pairs={{0,1},{1,0},{2,3},{3,2},{4,5},{5,4},{6,7},{7,6},{8,9},{9,8},{10,11... | collective-permute-start | bytes 55304 | tf_op jit(solution)/shard_map/ppermute | solution.py:475
  361.2 16.6 %all-to-all-done.1 = bf16[64,8,1792]{2,1,0:T(8,128)(2,1)S(1)} async-done(((bf16[64,8,1792]{2,1,0:T(8,128)(2,1)}), bf16[64,8,1792]{2,1,0:T(8,128)(2,1)S(1)}, u32[]{:S(2)}, u32[]{:S(2)}) %all-to-all-start.1) | async-done | bytes 1835040 | tf_op jit(solution)/shard_map/all_to_all | solution.py:560
  378.2 5.4 %collective-permute-start.16 = (f32[8,40]{1,0:T(8,128)S(1)}, f32[8,40]{1,0:T(8,128)S(1)}, u32[]{:S(2)}, u32[]{:S(2)}) collective-permute-start(f32[8,40]{1,0:T(8,128)S(1)} %slice_add_fusion.5), channel_id=1, source_target_pairs={{0,1},{1,0},{2,3},{3,2},{4,5},{5,4},{6,7},{7,6},{8,9},{9,8},{10,11... | collective-permute-start | bytes 3848 | tf_op jit(solution)/shard_map/ppermute | solution.py:475
  (248 shorter events, 53.4 us)
Async XLA Ops:
  7.2 95.4 %copy-start = (f32[2,3,24]{2,0,1:T(2,128)S(1)}, f32[2,3,24]{2,0,1:T(2,128)}, u32[]{:S(2)}) copy-start(f32[2,3,24]{2,0,1:T(2,128)} %param.18) | copy-start | bytes 1732
  7.2 91.4 %all-gather.2.cloned.1.call-start = ((), (), s32[]{:S(2)}) async-start(), calls=%async_computation.6 | async-start | bytes 8519680 | tf_op jit(solution)/shard_map/all_gather | solution.py:692
  8.1 7.3 %collective-permute-start = (bf16[2,6,3352]{2,1,0:T(8,128)(2,1)S(1)}, bf16[2,6,3352]{2,1,0:T(8,128)(2,1)S(1)}, u32[]{:S(2)}, u32[]{:S(2)}) collective-permute-start(bf16[2,6,3352]{2,1,0:T(8,128)(2,1)S(1)} %copy.121), channel_id=1, source_target_pairs={{0,1},{1,0},{2,3},{3,2},{4,5},{5,4},{6,7},{7,6},{8,9},{9,8},{10,11... | collective-permute-start | bytes 241352 | tf_op jit(solution)/shard_map/ppermute | solution.py:475
  12.3 1.4 collective-permute-start.1
  13.2 1.4 collective-permute-start.2
  100.7 4.1 %copy-start.2 = (bf16[1,256,768]{2,1,0:T(8,128)(2,1)S(1)}, bf16[1,256,768]{2,1,0:T(8,128)(2,1)}, u32[]{:S(2)}) copy-start(bf16[1,256,768]{2,1,0:T(8,128)(2,1)} %param.10) | copy-start | bytes 1179652
  101.9 6.0 %collective-permute-start.3 = (bf16[2,768,384]{2,1,0:T(8,128)(2,1)}, bf16[2,768,384]{2,1,0:T(8,128)(2,1)}, u32[]{:S(2)}, u32[]{:S(2)}) collective-permute-start(bf16[2,768,384]{2,1,0:T(8,128)(2,1)} %constant_dynamic-slice_fusion.18), channel_id=1, source_target_pairs={{0,1},{1,0},{2,3},{3,2},{4,5},{5,4},{6,7},{7,6},{8,9},{9,8},{10,11... | collective-permute-start | bytes 3538952 | tf_op jit(solution)/shard_map/ppermute | solution.py:475
  126.3 2.2 collective-permute-start.4
  127.5 2.3 collective-permute-start.5
  129.5 78.0 %copy-start.9 = (f32[512,1]{1,0:T(8,128)}, f32[512,1]{1,0:T(8,128)S(1)}, u32[]{:S(2)}) copy-start(f32[512,1]{1,0:T(8,128)S(1)} %fusion.19.rho_ref) | copy-start | bytes 6148
  147.8 1.8 collective-permute-start.6
  149.2 1.8 collective-permute-start.7
  194.6 8.6 %collective-permute-start.8 = (bf16[256,768]{1,0:T(8,128)(2,1)}, bf16[256,768]{1,0:T(8,128)(2,1)}, u32[]{:S(2)}, u32[]{:S(2)}) collective-permute-start(bf16[256,768]{1,0:T(8,128)(2,1)} %constant_dynamic-slice_fusion.14), channel_id=1, source_target_pairs={{0,1},{1,0},{2,3},{3,2},{4,5},{5,4},{6,7},{7,6},{8,9},{9,8},{10,11... | collective-permute-start | bytes 1179656 | tf_op jit(solution)/shard_map/ppermute | solution.py:475
  194.9 27.5 %all-to-all-start.2 = ((bf16[64,8,1152]{2,1,0:T(8,128)(2,1)}), bf16[64,8,1152]{2,1,0:T(8,128)(2,1)S(1)}, u32[]{:S(2)}, u32[]{:S(2)}) async-start(bf16[64,8,1152]{2,1,0:T(8,128)(2,1)} %bitcast.116), calls=%async_computation.2 | async-start | bytes 2359296 | tf_op jit(solution)/shard_map/all_to_all | solution.py:560
  223.4 26.3 %all-to-all-start = ((bf16[64,8,1152]{2,1,0:T(8,128)(2,1)}), bf16[64,8,1152]{2,1,0:T(8,128)(2,1)S(1)}, u32[]{:S(2)}, u32[]{:S(2)}) async-start(bf16[64,8,1152]{2,1,0:T(8,128)(2,1)} %bitcast.117), calls=%async_computation | async-start | bytes 2359296 | tf_op jit(solution)/shard_map/all_to_all | solution.py:560
  232.0 2.4 collective-permute-start.14
  250.7 40.3 %all-to-all-start.5 = ((bf16[64,8,1152]{2,1,0:T(8,128)(2,1)}), bf16[64,8,1152]{2,1,0:T(8,128)(2,1)S(1)}, u32[]{:S(2)}, u32[]{:S(2)}) async-start(bf16[64,8,1152]{2,1,0:T(8,128)(2,1)} %bitcast.112), calls=%async_computation.5 | async-start | bytes 2359296 | tf_op jit(solution)/shard_map/all_to_all | solution.py:560
  285.3 5.5 %copy-start.14 = (bf16[512,768]{1,0:T(8,128)(2,1)S(1)}, bf16[512,768]{1,0:T(8,128)(2,1)}, u32[]{:S(2)}) copy-start(bf16[512,768]{1,0:T(8,128)(2,1)} %get-tuple-element.62) | copy-start | bytes 2359300
  286.4 4.4 %collective-permute-start.9 = (bf16[256,768]{1,0:T(8,128)(2,1)S(1)}, bf16[256,768]{1,0:T(8,128)(2,1)S(1)}, u32[]{:S(2)}, u32[]{:S(2)}) collective-permute-start(bf16[256,768]{1,0:T(8,128)(2,1)S(1)} %constant_dynamic-slice_fusion.13), channel_id=1, source_target_pairs={{0,1},{1,0},{2,3},{3,2},{4,5},{5,4},{6,7},{7,6},{8,9},{9,8},{10,11... | collective-permute-start | bytes 1179656 | tf_op jit(solution)/shard_map/ppermute | solution.py:475
  290.8 13.8 %collective-permute-start.12 = (bf16[768,384]{1,0:T(8,128)(2,1)}, bf16[768,384]{1,0:T(8,128)(2,1)}, u32[]{:S(2)}, u32[]{:S(2)}) collective-permute-start(bf16[768,384]{1,0:T(8,128)(2,1)} %constant_dynamic-slice_fusion.10), channel_id=1, source_target_pairs={{0,1},{1,0},{2,3},{3,2},{4,5},{5,4},{6,7},{7,6},{8,9},{9,8},{10,11... | collective-permute-start | bytes 1769480 | tf_op jit(solution)/shard_map/ppermute | solution.py:475
  292.0 35.4 %all-to-all-start.3 = ((bf16[64,8,1792]{2,1,0:T(8,128)(2,1)}), bf16[64,8,1792]{2,1,0:T(8,128)(2,1)S(1)}, u32[]{:S(2)}, u32[]{:S(2)}) async-start(bf16[64,8,1792]{2,1,0:T(8,128)(2,1)} %bitcast.115), calls=%async_computation.3 | async-start | bytes 3670016 | tf_op jit(solution)/shard_map/all_to_all | solution.py:560
  309.4 1.7 collective-permute-start.15
  310.4 17.0 %copy-start.20 = (f32[8,1152]{1,0:T(8,128)}, f32[8,1152]{1,0:T(8,128)S(1)}, u32[]{:S(2)}) copy-start(f32[8,1152]{1,0:T(8,128)S(1)} %convert_reduce_fusion.5) | copy-start | bytes 110596
  327.5 22.9 %all-to-all-start.4 = ((bf16[64,8,1152]{2,1,0:T(8,128)(2,1)}), bf16[64,8,1152]{2,1,0:T(8,128)(2,1)S(1)}, u32[]{:S(2)}, u32[]{:S(2)}) async-start(bf16[64,8,1152]{2,1,0:T(8,128)(2,1)} %bitcast.111), calls=%async_computation.4 | async-start | bytes 2359296 | tf_op jit(solution)/shard_map/all_to_all | solution.py:560
  333.7 3.5 collective-permute-start.17
  336.4 18.9 %collective-permute-start.11 = (f32[6,1920]{1,0:T(8,128)S(1)}, f32[6,1920]{1,0:T(8,128)S(1)}, u32[]{:S(2)}, u32[]{:S(2)}) collective-permute-start(f32[6,1920]{1,0:T(8,128)S(1)} %constant_dynamic-slice_fusion.11), channel_id=1, source_target_pairs={{0,1},{1,0},{2,3},{3,2},{4,5},{5,4},{6,7},{7,6},{8,9},{9,8},{10,11... | collective-permute-start | bytes 138248 | tf_op jit(solution)/shard_map/ppermute | solution.py:475
  350.4 27.3 %all-to-all-start.1 = ((bf16[64,8,1792]{2,1,0:T(8,128)(2,1)}), bf16[64,8,1792]{2,1,0:T(8,128)(2,1)S(1)}, u32[]{:S(2)}, u32[]{:S(2)}) async-start(bf16[64,8,1792]{2,1,0:T(8,128)(2,1)} %bitcast.114), calls=%async_computation.1 | async-start | bytes 3670016 | tf_op jit(solution)/shard_map/all_to_all | solution.py:560
  355.5 4.9 %collective-permute-start.13 = (f32[12,384]{1,0:T(8,128)S(1)}, f32[12,384]{1,0:T(8,128)S(1)}, u32[]{:S(2)}, u32[]{:S(2)}) collective-permute-start(f32[12,384]{1,0:T(8,128)S(1)} %constant_dynamic-slice_fusion.9), channel_id=1, source_target_pairs={{0,1},{1,0},{2,3},{3,2},{4,5},{5,4},{6,7},{7,6},{8,9},{9,8},{10,11... | collective-permute-start | bytes 55304 | tf_op jit(solution)/shard_map/ppermute | solution.py:475
  360.5 23.1 %slice-start.1 = ((f32[8,1152]{1,0:T(8,128)}), f32[8,768]{1,0:T(8,128)S(1)}, s32[]{:S(2)}) async-start(f32[8,1152]{1,0:T(8,128)} %copy-done.20), calls=%async_computation.8 | async-start | bytes 49152 | tf_op jit(solution)/shard_map/slice | solution.py:577
  377.7 11.1 %copy-start.1 = (f32[2,3,24]{2,0,1:T(2,128)S(1)}, f32[2,3,24]{2,0,1:T(2,128)}, u32[]{:S(2)}) copy-start(f32[2,3,24]{2,0,1:T(2,128)} %param.18) | copy-start | bytes 1732
  378.2 6.3 %collective-permute-start.16 = (f32[8,40]{1,0:T(8,128)S(1)}, f32[8,40]{1,0:T(8,128)S(1)}, u32[]{:S(2)}, u32[]{:S(2)}) collective-permute-start(f32[8,40]{1,0:T(8,128)S(1)} %slice_add_fusion.5), channel_id=1, source_target_pairs={{0,1},{1,0},{2,3},{3,2},{4,5},{5,4},{6,7},{7,6},{8,9},{9,8},{10,11... | collective-permute-start | bytes 3848 | tf_op jit(solution)/shard_map/ppermute | solution.py:475
  383.7 4.3 %collective-permute-start.10 = (f32[6,1920]{1,0:T(8,128)S(1)}, f32[6,1920]{1,0:T(8,128)S(1)}, u32[]{:S(2)}, u32[]{:S(2)}) collective-permute-start(f32[6,1920]{1,0:T(8,128)S(1)} %constant_dynamic-slice_fusion.12), channel_id=1, source_target_pairs={{0,1},{1,0},{2,3},{3,2},{4,5},{5,4},{6,7},{7,6},{8,9},{9,8},{10,11... | collective-permute-start | bytes 138248 | tf_op jit(solution)/shard_map/ppermute | solution.py:475
  (17 other events, 36.7 us)
Sparse Core Ops, SparseCore 0:
  17.7 80.8 all-gather.1

commit v4 on v3

--- a/solution.py
+++ b/solution.py
@@ -233,6 +233,11 @@
     )
 
 
+def cost(microseconds):
+    flops, bytes_accessed = int(1.1e9 * microseconds), int(3.6e6 * microseconds)
+    return pl.CostEstimate(flops=flops, bytes_accessed=bytes_accessed, transcendentals=0)
+
+
 def vmem(count):
     return [pl.BlockSpec(memory_space=pltpu.VMEM)] * count
 
@@ -259,12 +264,13 @@
             pltpu.SemaphoreType.DMA,
         ],
         compiler_params=pltpu.CompilerParams(vmem_limit_bytes=58 * 2**20),
+        cost_estimate=cost(15),
         interpret=interpret,
     )(xhat, weights, wout, segc, segr, heads, maps)
 
 
 def gate_kernel(
-    seed_ref, rho_ref, xhat_ref, norm_ref, wout_ref, gate_ref, y_ref, gain_ref,
+    seed_ref, rho_ref, xhat_ref, norm_ref, wout_ref, gate_ref, y_ref, gain_ref, after_ref,
     dgate_ref, dy_ref, dwin_ref, dwout_ref, dgain_ref,
 ):
     seed = seed_ref[:, :WIDTH]
@@ -290,7 +296,7 @@
     dwin_ref[:, OWN:] = folded.astype(BF16)
 
 
-def gate_back(seed, rho, xhat, norm, wout, gate, y, gain, interpret=False):
+def gate_back(seed, rho, xhat, norm, wout, gate, y, gain, after, interpret=False):
     return pl.pallas_call(
         gate_kernel,
         out_shape=(
@@ -301,13 +307,14 @@
             jax.ShapeDtypeStruct((8, OWN), F32),
         ),
         compiler_params=pltpu.CompilerParams(vmem_limit_bytes=58 * 2**20),
+        cost_estimate=cost(8),
         interpret=interpret,
-    )(seed, rho, xhat, norm, wout, gate, y, gain)
+    )(seed, rho, xhat, norm, wout, gate, y, gain, after)
 
 
 def backward_kernel(
     layer, dgate_ref, dy_ref, xhat_ref, norm_ref, weights_ref, rest_ref,
-    segc_ref, segr_ref, taps_ref, heads_ref, dgain_ref, maps_ref,
+    segc_ref, segr_ref, taps_ref, heads_ref, dgain_ref, maps_ref, after_ref,
     dscaled_ref, dwin_ref,
     win_ref, dtx_ref, affinity_ref, bias_ref, daffinity_ref, drest_ref, dact_ref, rise_ref,
     direct_ref, dtaps_ref, semaphore,
@@ -438,12 +445,12 @@
 
 def backward_mix(
     layer, dgate, dy, xhat, norm, weights, rest, segc, segr, taps, heads, dgain, maps,
-    interpret=False,
+    after, interpret=False,
 ):
     square = (TOKENS, TOKENS)
     return pl.pallas_call(
         functools.partial(backward_kernel, layer),
-        in_specs=vmem(4) + [pl.BlockSpec(memory_space=pl.ANY)] + vmem(7),
+        in_specs=vmem(4) + [pl.BlockSpec(memory_space=pl.ANY)] + vmem(8),
         out_shape=(
             jax.ShapeDtypeStruct((TOKENS, WIDTH), BF16),
             jax.ShapeDtypeStruct((512, REST_COLS), BF16),
@@ -462,8 +469,9 @@
             pltpu.SemaphoreType.DMA,
         ],
         compiler_params=pltpu.CompilerParams(vmem_limit_bytes=58 * 2**20),
+        cost_estimate=cost(30),
         interpret=interpret,
-    )(dgate, dy, xhat, norm, weights, rest, segc, segr, taps, heads, dgain, maps)
+    )(dgate, dy, xhat, norm, weights, rest, segc, segr, taps, heads, dgain, maps, after)
 
 
 DP = ("dp_0", "dp_1", "dp_2")
@@ -556,65 +564,84 @@
     return own + swapped(part(partial_sum, 1 - core, HALF, 0)).astype(F32)
 
 
-def reduced(packed):
+def reduced(packed, earlier):
+    if earlier is not None:
+        packed, earlier = lax.optimization_barrier((packed, earlier))
     arrived = lax.all_to_all(packed, DP, 0, 0, tiled=True)
-    return jnp.sum(arrived.astype(F32), axis=0)
-
-
-def reduced_output(dwout, core):
+    total = jnp.sum(arrived.astype(F32), axis=0)
+    if earlier is not None:
+        total = jnp.where(jnp.isnan(earlier), earlier, total)
+    return total, arrived[0, :1, :1].astype(F32)
+
+
+def reduced_gate(dwin, dwout, core, earlier):
     half = WIDTH // 2
     dwout = in_order(core, part(dwout, core, half, 1), swapped(part(dwout, 1 - core, half, 1)), 0)
     dwout = dwout.reshape(CHIPS, 3, 8, half).transpose(0, 2, 1, 3)
-    return reduced(dwout.reshape(CHIPS, 8, OUT_COLS))
-
-
-def reduced_input(dwin):
-    return reduced(dwin.reshape(CHIPS, 8, dwin.shape[1]))
+    dwin = dwin.reshape(CHIPS, 8, GATE_COLS)
+    packed = jnp.concatenate([dwin, dwout.reshape(CHIPS, 8, OUT_COLS)], axis=2)
+    return reduced(packed, earlier)
+
+
+def reduced_rest(dwin, earlier):
+    return reduced(dwin.reshape(CHIPS, 8, REST_COLS), earlier)
 
 
 def unfolded(total, columns, fold):
-    tail = total[:, columns:].reshape(2, 4, fold).transpose(1, 0, 2).reshape(4, 2 * fold)
-    return jnp.concatenate([total[:, :columns], tail[:, :columns]], axis=0)
-
-
-def unpacked_gradients(gate_total, out_total, rest_total, core):
+    tail = total[:, :, columns:].reshape(LAYERS, 2, 4, fold).transpose(0, 2, 1, 3)
+    tail = tail.reshape(LAYERS, 4, 2 * fold)[:, :, :columns]
+    return jnp.concatenate([total[:, :, :columns], tail], axis=1)
+
+
+def unpacked_gradients(early_total, rest_total, core):
     win = jnp.concatenate(
-        [unfolded(gate_total, OWN, GATE_FOLD), unfolded(rest_total, REST, REST_FOLD)], axis=1
-    )
-    own = part(win, core, 6, 0)
-    got = swapped(part(win, 1 - core, 6, 0))
+        [
+            unfolded(early_total[:, :, :GATE_COLS], OWN, GATE_FOLD),
+            unfolded(rest_total, REST, REST_FOLD),
+        ],
+        axis=2,
+    )
+    own = part(win, core, 6, 1)
+    got = swapped(part(win, 1 - core, 6, 1))
     left = jnp.where(core == 0, own, got)
     right = jnp.where(core == 0, got, own)
     shared = slice(2 * OWN, 2 * OWN + 2 * STATE)
     steps = slice(2 * OWN + 2 * STATE, 2 * OWN + 2 * STATE + OWN_HEADS)
     dwin = jnp.concatenate(
         [
-            left[:, :OWN],
-            right[:, :OWN],
-            left[:, OWN : 2 * OWN],
-            right[:, OWN : 2 * OWN],
-            left[:, shared] + right[:, shared],
-            left[:, steps],
-            right[:, steps],
+            left[:, :, :OWN],
+            right[:, :, :OWN],
+            left[:, :, OWN : 2 * OWN],
+            right[:, :, OWN : 2 * OWN],
+            left[:, :, shared] + right[:, :, shared],
+            left[:, :, steps],
+            right[:, :, steps],
         ],
-        axis=1,
+        axis=2,
     )
     half = WIDTH // 2
-    wout = out_total.reshape(8, 3, half).transpose(1, 0, 2).reshape(24, half)
-    dwout = in_order(core, part(wout, core, 12, 0), swapped(part(wout, 1 - core, 12, 0)), 1)
-    tile = rest_total[:, OWN_CONV:REST]
-    vectors = tile[:, VECTORS : VECTORS + VECTOR_COLS] + tile[:, REMAINDERS : REMAINDERS + VECTOR_COLS]
+    wout = early_total[:, :, GATE_COLS:].reshape(LAYERS, 8, 3, half).transpose(0, 2, 1, 3)
+    wout = wout.reshape(LAYERS, 24, half)
+    dwout = in_order(core, part(wout, core, 12, 1), swapped(part(wout, 1 - core, 12, 1)), 2)
+    tile = rest_total[:, :, OWN_CONV:REST]
+    vectors = tile[:, :, VECTORS : VECTORS + VECTOR_COLS]
+    vectors = vectors + tile[:, :, REMAINDERS : REMAINDERS + VECTOR_COLS]
     others = swapped(vectors)
-    heads = in_order(core, vectors[7, :36].reshape(3, 12), others[7, :36].reshape(3, 12), 1)
+    heads = in_order(
+        core,
+        vectors[:, 7, :36].reshape(LAYERS, 3, 12),
+        others[:, 7, :36].reshape(LAYERS, 3, 12),
+        2,
+    )
     vectors = vectors + others
-    taps = part(vectors[:5, :28], core, 14, 1)
+    taps = part(vectors[:, :5, :28], core, 14, 2)
     return (
         dwin,
         dwout,
-        taps[:4],
-        taps[4],
-        part(vectors[5, :12], core, 6, 0),
-        part(vectors[6, :24], core, 12, 0),
+        taps[:, :4],
+        taps[:, 4],
+        part(vectors[:, 5, :12], core, 6, 1),
+        part(vectors[:, 6, :24], core, 12, 1),
         heads,
     )
 
@@ -624,8 +651,7 @@
 
 
 def layers_of(
-    hidden, cotangent, segments, head_values, weights, wouts, core, send_gate, send_rest,
-    interpret=False,
+    hidden, cotangent, segments, head_values, weights, wouts, core, interpret=False
 ):
     segr = segments
     segc = segments.reshape(TOKENS, 1)
@@ -648,6 +674,8 @@
         current = current + own_rho * branch
     upstream = cotangent.astype(F32)
     sent = [None] * LAYERS
+    arrived = None
+    after = [jnp.zeros((1, 1), F32)] * 2
     for layer in reversed(range(LAYERS)):
         before, sigma, xhat, gate, rest, y, rho, own_rho, branch, taps, norm, gain = saved[layer]
         seed = upstream.astype(BF16)
@@ -657,19 +685,24 @@
         seed = jnp.concatenate([seed, padded(means, (HALF, 128))], axis=1)
         seed = lax.all_gather(seed, "seq", axis=0, tiled=True)
         dgate, dy, dwin_gate, dwout, dgain = gate_back(
-            seed, rho, xhat, norm, wouts[layer], gate, y, gain, interpret=interpret
+            seed, rho, xhat, norm, wouts[layer], gate, y, gain, after[0], interpret=interpret
         )
-        early = send_gate(dwin_gate, dwout)
+        early, arrived = reduced_gate(dwin_gate, dwout, core, arrived)
+        after_early = arrived
         dscaled, dwin_rest = backward_mix(
             layer, dgate, dy, xhat, norm, weights, rest, segc, segr, taps, heads_all[layer],
-            dgain, maps, interpret=interpret,
+            dgain, maps, after[1], interpret=interpret,
         )
-        sent[layer] = early + (send_rest(dwin_rest),)
+        late, arrived = reduced_rest(dwin_rest, arrived)
+        sent[layer] = (early, late)
+        after = [after_early, arrived]
+        dscaled, after_early = lax.optimization_barrier((dscaled, after_early))
         scaled = over_positions(dscaled, core)
         upstream = upstream + sigma * (
             scaled
             - before * (sigma * sigma) * jnp.mean(scaled * before, axis=1, keepdims=True)
         )
+        upstream = jnp.where(jnp.isnan(after_early), after_early, upstream)
     return current.astype(BF16), upstream.astype(BF16), sent
 
 
@@ -692,16 +725,11 @@
     weights = lax.all_gather(block, DP, axis=0, tiled=True)
     wouts = output_weights(weights, core)
 
-    def send_gate(dwin, dwout):
-        return reduced_input(dwin), reduced_output(dwout, core)
-
     hidden_out, input_gradient, totals = layers_of(
-        hidden_in[0], cotangent[0], segments, head_values, weights, wouts, core, send_gate,
-        reduced_input,
-    )
-    pieces = [unpacked_gradients(*total, core) for total in totals]
-    stacked = tuple(jnp.stack([piece[slot] for piece in pieces]) for slot in range(7))
-    return (hidden_out[None], input_gradient[None]) + stacked
+        hidden_in[0], cotangent[0], segments, head_values, weights, wouts, core
+    )
+    totals = [jnp.stack(layers) for layers in zip(*totals)]
+    return (hidden_out[None], input_gradient[None]) + unpacked_gradients(*totals, core)
 
 
 def solution(mesh):

time: 401 us -> 350 us (0.87)
  waiting for transfers between devices: 148 us -> 110 us
  starting transfers between devices: 63.2 us -> 43.5 us
  other arithmetic: 27.6 us -> 33.1 us
    all_to_all x6 -> x4, waiting for transfers between devices: 62.2 us -> 23.8 us  [reduced(): arrived = lax.all_to_all(packed, DP, 0, 0, tiled=True)]
    ppermute x18 -> x15, starting transfers between devices: 21.5 us -> 10.6 us  [swapped(): return lax.ppermute(v, 'seq', [(0, 1), (1, 0)])]
    all_to_all x6 -> x4, starting transfers between devices: 41.7 us -> 32.8 us  [reduced(): arrived = lax.all_to_all(packed, DP, 0, 0, tiled=True)]
    unnamed x59 -> x53, local copies, waits for them, and re-layouts: 9.54 us -> 6.23 us
    dynamic_slice x20 -> x14, local copies, waits for them, and re-layouts: 10.1 us -> 10.7 us  [part(): return lax.dynamic_slice_in_dim(v, index * size, size, axis)]
  transfers between devices with their start and end apart: 25 -> 20, of which waited for: 14 -> 10; matrix products, arithmetic and copies ran while one was open for 9% -> 10% of each run, Pallas kernels for 9% -> 19%
where the time goes in v4:
time: 350 us; the launch traced here: 345 us
  waiting for transfers between devices  110 us (31%)
  Pallas kernels  105 us (30%)
  starting transfers between devices  43.5 us (12%)
  other arithmetic  33.1 us (9%)
  local copies, waits for them, and re-layouts  26.2 us (7%)
  between operations  17 us (5%)
  blocking collectives  10.4 us (3%)
    all_gather x1, waiting for transfers between devices, per_device(): weights = lax.all_gather(block, DP, axis=0, tiled=True)  81 us
    pallas_call x2, Pallas kernels, backward_mix(): pl.pallas_call(functools.partial(backward_kernel, layer), in_specs=vmem(4...  58.7 us
    all_to_all x4, starting transfers between devices, reduced(): arrived = lax.all_to_all(packed, DP, 0, 0, tiled=True)  32.8 us
    pallas_call x2, Pallas kernels, forward_mix(): pl.pallas_call(functools.partial(forward_kernel, layer), in_specs=vmem(1)...  30 us
    all_to_all x4, waiting for transfers between devices, reduced(): arrived = lax.all_to_all(packed, DP, 0, 0, tiled=True)  23.8 us
    pallas_call x2, Pallas kernels, gate_back(): pl.pallas_call(gate_kernel, out_shape=(jax.ShapeDtypeStruct((TOKENS, OWN)...  16.6 us
    dynamic_slice x14, local copies, waits for them, and re-layouts, part(): return lax.dynamic_slice_in_dim(v, index * size, size, axis)  10.7 us
    ppermute x15, starting transfers between devices, swapped(): return lax.ppermute(v, 'seq', [(0, 1), (1, 0)])  10.6 us
  transfers between devices with their start and end apart: 20, of which 10 were waited for; matrix products, arithmetic and copies ran while one was open for 10% of the time, Pallas kernels for 19%

profile of v4, /device:TPU:1, one launch (start us, length us, event | category | flops | bytes accessed | tf_op | source)
XLA Modules:
  0.0 345.3 jit_solution(7942667480100431783)
XLA Ops:
  17.6 81.0 %all-gather.2.cloned.1.call-done.weights_ref = bf16[512,8192]{1,0:T(8,128)(2,1)} async-done(((bf16[8,8192]{1,0:T(8,128)(2,1)}), bf16[512,8192]{1,0:T(8,128)(2,1)}) %all-gather.2.cloned.1.call-update) | async-done | bytes 8388624 | tf_op jit(solution)/shard_map/all_gather | solution.py:725
  98.6 1.8 slice.224
  105.2 2.7 all_gather.15.xhat_ref
  107.8 1.7 broadcast_select_fusion
  109.6 1.6 fusion.2
  111.2 15.0 %shard_map.169 = (f32[512,768]{1,0:T(8,128)}, f32[512,1152]{1,0:T(8,128)}, f32[512,768]{1,0:T(8,128)}, bf16[512,768]{1,0:T(8,128)(2,1)}, f32[512,128]{1,0:T(8,12...) custom-call(bf16[512,768]{1,0:T(8,128)(2,1)} %all_gather.15.xhat_ref, ...), custom_call_target="tpu_custom_call" | custom-call | flops 16499999744 | bytes 54000000 | tf_op jit(solution)/shard_map/pallas_call | solution.py:246
  131.0 2.5 all_gather.17.xhat_ref
  133.5 15.0 %shard_map.170 = (f32[512,768]{1,0:T(8,128)}, f32[512,1152]{1,0:T(8,128)}, f32[512,768]{1,0:T(8,128)}, bf16[512,768]{1,0:T(8,128)(2,1)}, f32[512,128]{1,0:T(8,12...) custom-call(bf16[512,768]{1,0:T(8,128)(2,1)} %all_gather.17.xhat_ref, ...), custom_call_target="tpu_custom_call" | custom-call | flops 16499999744 | bytes 54000000 | tf_op jit(solution)/shard_map/pallas_call | solution.py:246
  153.1 2.6 all_gather.18.seed_ref
  155.7 8.3 %shard_map.171 = (bf16[512,768]{1,0:T(8,128)(2,1)}, f32[512,768]{1,0:T(8,128)}, bf16[512,1152]{1,0:T(8,128)(2,1)}, bf16[768,768]{1,0:T(8,128)(2,1)}, f32[8,768]{1,0:T(8,128)}) custom-call(bf16[512,896]{1,0:T(8,128)(2,1)} %all_gather.18.seed_ref, f32[512,1]{1,0:T(8,128)} %copy-done.17, bf16[512,768]{1,0:T(8,128)(2,1)} %all_gather.17.xhat_ref, ...), custom_call_target="tpu_custom_call" | custom-call | flops 8800000000 | bytes 28800000 | tf_op jit(solution)/shard_map/pallas_call | solution.py:300
  165.4 1.8 collective-permute-done.8
  168.7 1.5 pad_maximum_fusion
  170.2 8.5 %all-to-all-start = ((bf16[64,8,2304]{2,1,0:T(8,128)(2,1)}), bf16[64,8,2304]{2,1,0:T(8,128)(2,1)S(1)}, u32[]{:S(2)}, u32[]{:S(2)}) async-start(bf16[64,8,2304]{2,1,0:T(8,128)(2,1)} %pad_maximum_fusion), calls=%async_computation | async-start | bytes 4718592 | tf_op jit(solution)/shard_map/all_to_all | solution.py:570
  178.7 29.4 %shard_map.172 = (bf16[512,768]{1,0:T(8,128)(2,1)}, bf16[512,1792]{1,0:T(8,128)(2,1)}) custom-call(bf16[512,768]{1,0:T(8,128)(2,1)} %get-tuple-element.57.dgate_ref, f32[512,768]{1,0:T(8,128)} %get-tuple-element.58.dy_ref, bf16[512,768]{1,0:T(8,128)(2,1)} %all_gather.17.xhat_ref, f32[8,768]{1,0:T(8,128)} %get-tuple-element.53.norm_ref, ...), custom_call_target="tpu_custom_call" | custom-call | flops 32999999488 | bytes 108000000 | tf_op jit(solution)/shard_map/pallas_call | solution.py:451
  208.1 1.7 all-to-all-done
  211.0 1.8 constant_dynamic-slice_fusion.9
  212.8 2.0 collective-permute-start.9
  214.8 7.1 %all-to-all-start.1 = ((bf16[64,8,1792]{2,1,0:T(8,128)(2,1)}), bf16[64,8,1792]{2,1,0:T(8,128)(2,1)}, u32[]{:S(2)}, u32[]{:S(2)}) async-start(bf16[64,8,1792]{2,1,0:T(8,128)(2,1)} %bitcast.106), calls=%async_computation.1 | async-start | bytes 3670016 | tf_op jit(solution)/shard_map/all_to_all | solution.py:570
  223.4 2.6 multiply_reduce_fusion
  228.3 2.6 all_gather.19.seed_ref
  230.9 8.3 %shard_map.173 = (bf16[512,768]{1,0:T(8,128)(2,1)}, f32[512,768]{1,0:T(8,128)}, bf16[512,1152]{1,0:T(8,128)(2,1)}, bf16[768,768]{1,0:T(8,128)(2,1)}, f32[8,768]{1,0:T(8,128)}) custom-call(bf16[512,896]{1,0:T(8,128)(2,1)} %all_gather.19.seed_ref, f32[512,1]{1,0:T(8,128)} %copy-done.16, bf16[512,768]{1,0:T(8,128)(2,1)} %all_gather.15.xhat_ref, ...), custom_call_target="tpu_custom_call" | custom-call | flops 8800000000 | bytes 28800000 | tf_op jit(solution)/shard_map/pallas_call | solution.py:300
  243.9 1.7 pad_maximum_fusion.1
  245.6 2.3 all-to-all-done.1
  249.8 7.7 %all-to-all-start.2 = ((bf16[64,8,2304]{2,1,0:T(8,128)(2,1)}), bf16[64,8,2304]{2,1,0:T(8,128)(2,1)S(1)}, u32[]{:S(2)}, u32[]{:S(2)}) async-start(bf16[64,8,2304]{2,1,0:T(8,128)(2,1)} %pad_maximum_fusion.1), calls=%async_computation.2 | async-start | bytes 4718592 | tf_op jit(solution)/shard_map/all_to_all | solution.py:570
  257.5 1.8 convert_reduce_fusion.2
  259.9 29.3 %shard_map.174 = (bf16[512,768]{1,0:T(8,128)(2,1)}, bf16[512,1792]{1,0:T(8,128)(2,1)}) custom-call(bf16[512,768]{1,0:T(8,128)(2,1)} %get-tuple-element.71.dgate_ref, f32[512,768]{1,0:T(8,128)} %get-tuple-element.72.dy_ref, bf16[512,768]{1,0:T(8,128)(2,1)} %all_gather.15.xhat_ref, f32[8,768]{1,0:T(8,128)} %get-tuple-element.67.norm_ref, ...), custom_call_target="tpu_custom_call" | custom-call | flops 32999999488 | bytes 108000000 | tf_op jit(solution)/shard_map/pallas_call | solution.py:451
  290.4 1.8 constant_dynamic-slice_fusion.7
  293.6 9.5 %all-to-all-start.3 = ((bf16[64,8,1792]{2,1,0:T(8,128)(2,1)}), bf16[64,8,1792]{2,1,0:T(8,128)(2,1)}, u32[]{:S(2)}, u32[]{:S(2)}) async-start(bf16[64,8,1792]{2,1,0:T(8,128)(2,1)} %bitcast.107), calls=%async_computation.3 | async-start | bytes 3670016 | tf_op jit(solution)/shard_map/all_to_all | solution.py:570
  307.4 2.2 fusion.15
  309.5 19.7 %all-to-all-done.3 = bf16[64,8,1792]{2,1,0:T(8,128)(2,1)} async-done(((bf16[64,8,1792]{2,1,0:T(8,128)(2,1)}), bf16[64,8,1792]{2,1,0:T(8,128)(2,1)}, u32[]{:S(2)}, u32[]{:S(2)}) %all-to-all-start.3) | async-done | bytes 1835040 | tf_op jit(solution)/shard_map/all_to_all | solution.py:570
  329.2 1.8 convert_reduce_fusion.3
  331.2 1.7 collective-permute-start.14
  (197 shorter events, 49.3 us)
Async XLA Ops:
  7.2 95.4 %copy-start = (f32[2,3,24]{2,0,1:T(2,128)S(1)}, f32[2,3,24]{2,0,1:T(2,128)}, u32[]{:S(2)}) copy-start(f32[2,3,24]{2,0,1:T(2,128)} %param.18) | copy-start | bytes 1732
  7.2 91.4 %all-gather.2.cloned.1.call-start = ((), (), s32[]{:S(2)}) async-start(), calls=%async_computation.4 | async-start | bytes 8519680 | tf_op jit(solution)/shard_map/all_gather | solution.py:725
  8.1 7.3 %collective-permute-start = (bf16[2,6,3352]{2,1,0:T(8,128)(2,1)S(1)}, bf16[2,6,3352]{2,1,0:T(8,128)(2,1)S(1)}, u32[]{:S(2)}, u32[]{:S(2)}) collective-permute-start(bf16[2,6,3352]{2,1,0:T(8,128)(2,1)S(1)} %copy.113), channel_id=1, source_target_pairs={{0,1},{1,0},{2,3},{3,2},{4,5},{5,4},{6,7},{7,6},{8,9},{9,8},{10,11... | collective-permute-start | bytes 241352 | tf_op jit(solution)/shard_map/ppermute | solution.py:483
  12.3 1.4 collective-permute-start.1
  13.2 1.4 collective-permute-start.2
  100.7 4.1 %copy-start.2 = (bf16[1,256,768]{2,1,0:T(8,128)(2,1)S(1)}, bf16[1,256,768]{2,1,0:T(8,128)(2,1)}, u32[]{:S(2)}) copy-start(bf16[1,256,768]{2,1,0:T(8,128)(2,1)} %param.10) | copy-start | bytes 1179652
  101.9 5.9 %collective-permute-start.3 = (bf16[2,768,384]{2,1,0:T(8,128)(2,1)}, bf16[2,768,384]{2,1,0:T(8,128)(2,1)}, u32[]{:S(2)}, u32[]{:S(2)}) collective-permute-start(bf16[2,768,384]{2,1,0:T(8,128)(2,1)} %constant_dynamic-slice_fusion.14), channel_id=1, source_target_pairs={{0,1},{1,0},{2,3},{3,2},{4,5},{5,4},{6,7},{7,6},{8,9},{9,8},{10,11... | collective-permute-start | bytes 3538952 | tf_op jit(solution)/shard_map/ppermute | solution.py:483
  126.2 3.8 %copy-start.7 = (bf16[512,768]{1,0:T(8,128)(2,1)S(1)}, bf16[512,768]{1,0:T(8,128)(2,1)}, u32[]{:S(2)}) copy-start(bf16[512,768]{1,0:T(8,128)(2,1)} %get-tuple-element.50) | copy-start | bytes 2359300
  126.2 2.1 collective-permute-start.4
  127.4 2.5 collective-permute-start.5
  130.0 3.5 %copy-start.9 = (bf16[256,768]{1,0:T(8,128)(2,1)}, bf16[256,768]{1,0:T(8,128)(2,1)S(1)}, u32[]{:S(2)}) copy-start(bf16[256,768]{1,0:T(8,128)(2,1)S(1)} %collective-permute-done.5) | copy-start | bytes 1179652
  148.5 3.2 copy-start.3
  148.5 3.2 copy-start.18
  148.5 2.0 collective-permute-start.6
  149.9 1.8 collective-permute-start.7
  165.1 3.5 %copy-start.15 = (bf16[512,1152]{1,0:T(8,128)(2,1)S(1)}, bf16[512,1152]{1,0:T(8,128)(2,1)}, u32[]{:S(2)}) copy-start(bf16[512,1152]{1,0:T(8,128)(2,1)} %get-tuple-element.63) | copy-start | bytes 3538948
  165.1 2.1 collective-permute-start.8
  170.2 39.6 %all-to-all-start = ((bf16[64,8,2304]{2,1,0:T(8,128)(2,1)}), bf16[64,8,2304]{2,1,0:T(8,128)(2,1)S(1)}, u32[]{:S(2)}, u32[]{:S(2)}) async-start(bf16[64,8,2304]{2,1,0:T(8,128)(2,1)} %pad_maximum_fusion), calls=%async_computation | async-start | bytes 4718592 | tf_op jit(solution)/shard_map/all_to_all | solution.py:570
  212.8 9.1 %collective-permute-start.9 = (bf16[256,768]{1,0:T(8,128)(2,1)}, bf16[256,768]{1,0:T(8,128)(2,1)}, u32[]{:S(2)}, u32[]{:S(2)}) collective-permute-start(bf16[256,768]{1,0:T(8,128)(2,1)} %constant_dynamic-slice_fusion.9), channel_id=1, source_target_pairs={{0,1},{1,0},{2,3},{3,2},{4,5},{5,4},{6,7},{7,6},{8,9},{9,8},{10,11... | collective-permute-start | bytes 1179656 | tf_op jit(solution)/shard_map/ppermute | solution.py:483
  214.8 33.2 %all-to-all-start.1 = ((bf16[64,8,1792]{2,1,0:T(8,128)(2,1)}), bf16[64,8,1792]{2,1,0:T(8,128)(2,1)}, u32[]{:S(2)}, u32[]{:S(2)}) async-start(bf16[64,8,1792]{2,1,0:T(8,128)(2,1)} %bitcast.106), calls=%async_computation.1 | async-start | bytes 3670016 | tf_op jit(solution)/shard_map/all_to_all | solution.py:570
  240.3 2.2 collective-permute-start.10
  241.6 2.3 copy-start.14
  249.8 39.5 %all-to-all-start.2 = ((bf16[64,8,2304]{2,1,0:T(8,128)(2,1)}), bf16[64,8,2304]{2,1,0:T(8,128)(2,1)S(1)}, u32[]{:S(2)}, u32[]{:S(2)}) async-start(bf16[64,8,2304]{2,1,0:T(8,128)(2,1)} %pad_maximum_fusion.1), calls=%async_computation.2 | async-start | bytes 4718592 | tf_op jit(solution)/shard_map/all_to_all | solution.py:570
  292.2 13.9 %collective-permute-start.11 = (bf16[256,768]{1,0:T(8,128)(2,1)}, bf16[256,768]{1,0:T(8,128)(2,1)}, u32[]{:S(2)}, u32[]{:S(2)}) collective-permute-start(bf16[256,768]{1,0:T(8,128)(2,1)} %constant_dynamic-slice_fusion.7), channel_id=1, source_target_pairs={{0,1},{1,0},{2,3},{3,2},{4,5},{5,4},{6,7},{7,6},{8,9},{9,8},{10,11... | collective-permute-start | bytes 1179656 | tf_op jit(solution)/shard_map/ppermute | solution.py:483
  293.6 35.6 %all-to-all-start.3 = ((bf16[64,8,1792]{2,1,0:T(8,128)(2,1)}), bf16[64,8,1792]{2,1,0:T(8,128)(2,1)}, u32[]{:S(2)}, u32[]{:S(2)}) async-start(bf16[64,8,1792]{2,1,0:T(8,128)(2,1)} %bitcast.107), calls=%async_computation.3 | async-start | bytes 3670016 | tf_op jit(solution)/shard_map/all_to_all | solution.py:570
  303.1 3.0 copy-start.6
  303.5 3.8 %copy-start.5 = (f32[256,768]{1,0:T(8,128)S(1)}, f32[256,768]{1,0:T(8,128)}, u32[]{:S(2)}) copy-start(f32[256,768]{1,0:T(8,128)} %get-tuple-element.138) | copy-start | bytes 2359300
  304.1 1.3 collective-permute-start.13
  307.3 23.7 %copy-start.11 = (f32[1,8,1792]{2,1,0:T(8,128)S(1)}, f32[1,8,1792]{2,1,0:T(8,128)}, u32[]{:S(2)}) copy-start(f32[1,8,1792]{2,1,0:T(8,128)} %select_bitcast_fusion.1) | copy-start | bytes 172036
  329.2 8.9 %copy-start.1 = (f32[2,3,24]{2,0,1:T(2,128)S(1)}, f32[2,3,24]{2,0,1:T(2,128)}, u32[]{:S(2)}) copy-start(f32[2,3,24]{2,0,1:T(2,128)} %param.18) | copy-start | bytes 1732
  331.2 2.5 collective-permute-start.14
  332.9 4.3 %collective-permute-start.12 = (f32[2,6,1920]{2,1,0:T(8,128)S(1)}, f32[2,6,1920]{2,1,0:T(8,128)S(1)}, u32[]{:S(2)}, u32[]{:S(2)}) collective-permute-start(f32[2,6,1920]{2,1,0:T(8,128)S(1)} %constant_dynamic-slice_fusion.6), channel_id=1, source_target_pairs={{0,1},{1,0},{2,3},{3,2},{4,5},{5,4},{6,7},{7,6},{8,9},{9,8},{10,11... | collective-permute-start | bytes 276488 | tf_op jit(solution)/shard_map/ppermute | solution.py:483
  (9 other events, 12.1 us)
Sparse Core Ops, SparseCore 0:
  17.7 80.8 all-gather.1

commit v5 on v4

--- a/solution.py
+++ b/solution.py
@@ -55,16 +55,17 @@
 
 
 def padded_orders():
-    column = iota((WIDTH, 512), 1)
+    column = iota((1, 512), 1)
     row = iota((WIDTH, 512), 0)
     start = 12 * (column >> 3)
     place = column & 7
-    features = (
-        start + place,
-        jnp.where(place < 4, start + place + 8, -1),
-        jnp.where(place < 4, -1, start + place + 4),
-    )
+    features = (start + place, start + 8 + (place & 3))
     return [jnp.where(feature == row, 1.0, 0.0).astype(BF16) for feature in features]
+
+
+def half_places():
+    low = (iota((1, 512), 1) & 7) < 4
+    return jnp.where(low, 1.0, 0.0).astype(BF16), jnp.where(low, 0.0, 1.0).astype(BF16)
 
 
 def head_spread():
@@ -106,8 +107,10 @@
     return (jnp.where(low, 1.0, 0.0).astype(BF16), jnp.where(low, 0.0, 1.0).astype(BF16))
 
 
-def reordered(scaled):
-    return [dot(scaled, order).astype(BF16) for order in padded_orders()]
+def reordered(scaled, orders=None):
+    once, twice = [dot(scaled, order).astype(BF16) for order in orders or padded_orders()]
+    low, high = half_places()
+    return once, twice * low, twice * high
 
 
 def projected(parts, full, folded, fold):
@@ -166,6 +169,13 @@
 def fetched(source, target, semaphore, layer, columns):
     start = layer * LAYER_COLS
     return pltpu.make_async_copy(source.at[:, start : start + columns], target, semaphore)
+
+
+def spread_steps(step, spread):
+    spread = spread.astype(BF16)
+    high = step.astype(BF16)
+    low = (step - high.astype(F32)).astype(BF16)
+    return dot(high, spread) + dot(low, spread)
 
 
 def forward_kernel(
@@ -204,7 +214,7 @@
     _, step, cumul = steps_of(rest_ref[:, OWN_CONV:], heads)
     cumul_rows = cumul.T
     spread = head_spread()
-    dtx_ref[...] = (dot(step, spread, precision=HIGHEST) * inputs).astype(BF16)
+    dtx_ref[...] = (spread_steps(step, spread) * inputs).astype(BF16)
     y_ref[...] = dot(heads, spread, precision=HIGHEST)[2:3] * inputs
     affinity_ref[...] = dot_nt(readers, writers)
     halves = lane_masks()
@@ -335,7 +345,7 @@
     shifted, step, cumul = steps_of(rest_ref[:, OWN_CONV:], heads)
     cumul_rows = cumul.T
     spread = head_spread()
-    step_wide = dot(step, spread, precision=HIGHEST)
+    step_wide = spread_steps(step, spread)
     skip_wide = dot(heads, spread, precision=HIGHEST)[2:3]
     dtx_ref[...] = (step_wide * inputs).astype(BF16)
     allowed = (iota((TOKENS, TOKENS), 0) <= iota((TOKENS, TOKENS), 1)) & (segc == segr_ref[...])
@@ -409,7 +419,7 @@
     xhat = xhat_ref[...].astype(F32)
     orders = padded_orders()
     u = (xhat * norm).astype(BF16)
-    parts = [dot(u, order).astype(BF16) for order in orders]
+    parts = reordered(u, orders)
     drest = drest_ref[...]
     copy.wait()
     from_rest = input_gradients(
@@ -418,9 +428,9 @@
     from_gate = input_gradients(
         dgate_ref[...], win_ref[:, :OWN], win_ref[:, OWN:GATE_COLS], GATE_FOLD
     )
-    du = jnp.zeros((TOKENS, WIDTH), F32)
-    for one, other, order in zip(from_rest, from_gate, orders):
-        du = du + dot_nt((one + other).astype(BF16), order)
+    once, low, high = [(one + other).astype(BF16) for one, other in zip(from_rest, from_gate)]
+    low_places, high_places = half_places()
+    du = dot_nt(once, orders[0]) + dot_nt(low * low_places + high * high_places, orders[1])
     dscaled_ref[...] = (du * norm).astype(BF16)
 
     full, folded = weight_gradient(parts, drest, REST_FOLD)
@@ -651,7 +661,7 @@
 
 
 def layers_of(
-    hidden, cotangent, segments, head_values, weights, wouts, core, interpret=False
+    hidden, cotangent, segments, head_values, weights, core, interpret=False
 ):
     segr = segments
     segc = segments.reshape(TOKENS, 1)
@@ -662,6 +672,11 @@
     for layer in range(LAYERS):
         sigma = mean_square_scale(current)
         xhat = lax.all_gather((current * sigma).astype(BF16), "seq", axis=0, tiled=True)
+        if layer == 0:
+            weights, xhat, segc, heads_all, maps = lax.optimization_barrier(
+                (weights, xhat, segc, heads_all, maps)
+            )
+            wouts = output_weights(weights, core)
         gate, rest, y, out, square, taps, norm, gain = forward_mix(
             layer, xhat, weights, wouts[layer], segc, segr, heads_all[layer], maps,
             interpret=interpret,
@@ -723,10 +738,8 @@
         projection_in, projection_out, kernel_weight, kernel_bias, norm_gain, gate_gain, core
     )
     weights = lax.all_gather(block, DP, axis=0, tiled=True)
-    wouts = output_weights(weights, core)
-
     hidden_out, input_gradient, totals = layers_of(
-        hidden_in[0], cotangent[0], segments, head_values, weights, wouts, core
+        hidden_in[0], cotangent[0], segments, head_values, weights, core
     )
     totals = [jnp.stack(layers) for layers in zip(*totals)]
     return (hidden_out[None], input_gradient[None]) + unpacked_gradients(*totals, core)

time: 350 us -> 343 us (0.980)
  Pallas kernels: 105 us -> 98.9 us
    pallas_call x2, Pallas kernels: 58.7 us -> 54.6 us  [backward_mix(): pl.pallas_call(functools.partial(backward_kernel, layer), in_specs=vmem(4...]
    all_gather x1, waiting for transfers between devices: 81 us -> 77.3 us  [per_device(): weights = lax.all_gather(block, DP, axis=0, tiled=True)]
  transfers between devices with their start and end apart: 20 -> 20, of which waited for: 10 -> 14; matrix products, arithmetic and copies ran while one was open for 10% -> 10% of each run, Pallas kernels for 19% -> 18%
where the time goes in v5:
time: 343 us; the launch traced here: 339 us
  waiting for transfers between devices  110 us (32%)
  Pallas kernels  98.9 us (29%)
  starting transfers between devices  42.6 us (12%)
  other arithmetic  33.1 us (10%)
  local copies, waits for them, and re-layouts  26.1 us (8%)
  between operations  17 us (5%)
  blocking collectives  10.6 us (3%)
    all_gather x1, waiting for transfers between devices, per_device(): weights = lax.all_gather(block, DP, axis=0, tiled=True)  77.3 us
    pallas_call x2, Pallas kernels, backward_mix(): pl.pallas_call(functools.partial(backward_kernel, layer), in_specs=vmem(4...  54.6 us
    all_to_all x4, starting transfers between devices, reduced(): arrived = lax.all_to_all(packed, DP, 0, 0, tiled=True)  30.6 us
    pallas_call x2, Pallas kernels, forward_mix(): pl.pallas_call(functools.partial(forward_kernel, layer), in_specs=vmem(1)...  28.5 us
    all_to_all x4, waiting for transfers between devices, reduced(): arrived = lax.all_to_all(packed, DP, 0, 0, tiled=True)  26.7 us
    pallas_call x2, Pallas kernels, gate_back(): pl.pallas_call(gate_kernel, out_shape=(jax.ShapeDtypeStruct((TOKENS, OWN)...  15.8 us
    ppermute x15, starting transfers between devices, swapped(): return lax.ppermute(v, 'seq', [(0, 1), (1, 0)])  12 us
    dynamic_slice x14, local copies, waits for them, and re-layouts, part(): return lax.dynamic_slice_in_dim(v, index * size, size, axis)  10.6 us
  transfers between devices with their start and end apart: 20, of which 14 were waited for; matrix products, arithmetic and copies ran while one was open for 10% of the time, Pallas kernels for 18%

profile of v5, /device:TPU:1, one launch (start us, length us, event | category | flops | bytes accessed | tf_op | source)
XLA Modules:
  0.0 338.8 jit_solution(9676815477505528492)
XLA Ops:
  18.8 2.5 all_gather.16.xhat_ref
  21.3 77.3 %all-gather.2.cloned.1.call-done.weights_ref = bf16[512,8192]{1,0:T(8,128)(2,1)} async-done(((bf16[8,8192]{1,0:T(8,128)(2,1)}), bf16[512,8192]{1,0:T(8,128)(2,1)}) %all-gather.2.cloned.1.call-update) | async-done | bytes 8388624 | tf_op jit(solution)/shard_map/all_gather | solution.py:740
  98.7 1.8 slice.224
  105.6 1.7 broadcast_select_fusion
  107.3 1.6 fusion.2
  108.9 14.3 %shard_map.169 = (f32[512,768]{1,0:T(8,128)}, f32[512,1152]{1,0:T(8,128)}, f32[512,768]{1,0:T(8,128)}, bf16[512,768]{1,0:T(8,128)(2,1)}, f32[512,128]{1,0:T(8,12...) custom-call(bf16[512,768]{1,0:T(8,128)(2,1)} %all_gather.16.xhat_ref, ...), custom_call_target="tpu_custom_call" | custom-call | flops 16499999744 | bytes 54000000 | tf_op jit(solution)/shard_map/pallas_call | solution.py:256
  127.7 2.9 all_gather.17.xhat_ref
  130.7 14.2 %shard_map.170 = (f32[512,768]{1,0:T(8,128)}, f32[512,1152]{1,0:T(8,128)}, f32[512,768]{1,0:T(8,128)}, bf16[512,768]{1,0:T(8,128)(2,1)}, f32[512,128]{1,0:T(8,12...) custom-call(bf16[512,768]{1,0:T(8,128)(2,1)} %all_gather.17.xhat_ref, ...), custom_call_target="tpu_custom_call" | custom-call | flops 16499999744 | bytes 54000000 | tf_op jit(solution)/shard_map/pallas_call | solution.py:256
  149.5 2.6 all_gather.18.seed_ref
  152.1 7.9 %shard_map.171 = (bf16[512,768]{1,0:T(8,128)(2,1)}, f32[512,768]{1,0:T(8,128)}, bf16[512,1152]{1,0:T(8,128)(2,1)}, bf16[768,768]{1,0:T(8,128)(2,1)}, f32[8,768]{1,0:T(8,128)}) custom-call(bf16[512,896]{1,0:T(8,128)(2,1)} %all_gather.18.seed_ref, f32[512,1]{1,0:T(8,128)} %copy-done.17, bf16[512,768]{1,0:T(8,128)(2,1)} %all_gather.17.xhat_ref, ...), custom_call_target="tpu_custom_call" | custom-call | flops 8800000000 | bytes 28800000 | tf_op jit(solution)/shard_map/pallas_call | solution.py:310
  161.6 1.7 collective-permute-done.8
  166.3 8.5 %all-to-all-start = ((bf16[64,8,2304]{2,1,0:T(8,128)(2,1)}), bf16[64,8,2304]{2,1,0:T(8,128)(2,1)S(1)}, u32[]{:S(2)}, u32[]{:S(2)}) async-start(bf16[64,8,2304]{2,1,0:T(8,128)(2,1)} %pad_maximum_fusion), calls=%async_computation | async-start | bytes 4718592 | tf_op jit(solution)/shard_map/all_to_all | solution.py:580
  174.8 27.3 %shard_map.172 = (bf16[512,768]{1,0:T(8,128)(2,1)}, bf16[512,1792]{1,0:T(8,128)(2,1)}) custom-call(bf16[512,768]{1,0:T(8,128)(2,1)} %get-tuple-element.67.dgate_ref, f32[512,768]{1,0:T(8,128)} %get-tuple-element.68.dy_ref, bf16[512,768]{1,0:T(8,128)(2,1)} %all_gather.17.xhat_ref, f32[8,768]{1,0:T(8,128)} %get-tuple-element.63.norm_ref, ...), custom_call_target="tpu_custom_call" | custom-call | flops 32999999488 | bytes 108000000 | tf_op jit(solution)/shard_map/pallas_call | solution.py:461
  202.1 3.6 %all-to-all-done = bf16[64,8,2304]{2,1,0:T(8,128)(2,1)S(1)} async-done(((bf16[64,8,2304]{2,1,0:T(8,128)(2,1)}), bf16[64,8,2304]{2,1,0:T(8,128)(2,1)S(1)}, u32[]{:S(2)}, u32[]{:S(2)}) %all-to-all-start) | async-done | bytes 2359328 | tf_op jit(solution)/shard_map/all_to_all | solution.py:580
  206.8 1.8 constant_dynamic-slice_fusion.9
  208.6 2.2 collective-permute-start.9
  210.8 6.8 %all-to-all-start.1 = ((bf16[64,8,1792]{2,1,0:T(8,128)(2,1)}), bf16[64,8,1792]{2,1,0:T(8,128)(2,1)}, u32[]{:S(2)}, u32[]{:S(2)}) async-start(bf16[64,8,1792]{2,1,0:T(8,128)(2,1)} %bitcast.106), calls=%async_computation.1 | async-start | bytes 3670016 | tf_op jit(solution)/shard_map/all_to_all | solution.py:580
  219.2 2.6 multiply_reduce_fusion
  224.1 2.6 all_gather.19.seed_ref
  226.6 7.8 %shard_map.173 = (bf16[512,768]{1,0:T(8,128)(2,1)}, f32[512,768]{1,0:T(8,128)}, bf16[512,1152]{1,0:T(8,128)(2,1)}, bf16[768,768]{1,0:T(8,128)(2,1)}, f32[8,768]{1,0:T(8,128)}) custom-call(bf16[512,896]{1,0:T(8,128)(2,1)} %all_gather.19.seed_ref, f32[512,1]{1,0:T(8,128)} %copy-done.16, bf16[512,768]{1,0:T(8,128)(2,1)} %all_gather.16.xhat_ref, ...), custom_call_target="tpu_custom_call" | custom-call | flops 8800000000 | bytes 28800000 | tf_op jit(solution)/shard_map/pallas_call | solution.py:310
  239.3 1.7 pad_maximum_fusion.1
  241.0 2.7 all-to-all-done.1
  245.5 7.5 %all-to-all-start.2 = ((bf16[64,8,2304]{2,1,0:T(8,128)(2,1)}), bf16[64,8,2304]{2,1,0:T(8,128)(2,1)S(1)}, u32[]{:S(2)}, u32[]{:S(2)}) async-start(bf16[64,8,2304]{2,1,0:T(8,128)(2,1)} %pad_maximum_fusion.1), calls=%async_computation.2 | async-start | bytes 4718592 | tf_op jit(solution)/shard_map/all_to_all | solution.py:580
  253.1 1.8 convert_reduce_fusion.2
  255.5 27.3 %shard_map.174 = (bf16[512,768]{1,0:T(8,128)(2,1)}, bf16[512,1792]{1,0:T(8,128)(2,1)}) custom-call(bf16[512,768]{1,0:T(8,128)(2,1)} %get-tuple-element.81.dgate_ref, f32[512,768]{1,0:T(8,128)} %get-tuple-element.82.dy_ref, bf16[512,768]{1,0:T(8,128)(2,1)} %all_gather.16.xhat_ref, f32[8,768]{1,0:T(8,128)} %get-tuple-element.77.norm_ref, ...), custom_call_target="tpu_custom_call" | custom-call | flops 32999999488 | bytes 108000000 | tf_op jit(solution)/shard_map/pallas_call | solution.py:461
  284.9 1.8 constant_dynamic-slice_fusion.7
  286.6 2.5 collective-permute-start.11
  289.1 7.8 %all-to-all-start.3 = ((bf16[64,8,1792]{2,1,0:T(8,128)(2,1)}), bf16[64,8,1792]{2,1,0:T(8,128)(2,1)}, u32[]{:S(2)}, u32[]{:S(2)}) async-start(bf16[64,8,1792]{2,1,0:T(8,128)(2,1)} %bitcast.107), calls=%async_computation.3 | async-start | bytes 3670016 | tf_op jit(solution)/shard_map/all_to_all | solution.py:580
  301.2 2.2 fusion.15
  303.3 19.5 %all-to-all-done.3 = bf16[64,8,1792]{2,1,0:T(8,128)(2,1)} async-done(((bf16[64,8,1792]{2,1,0:T(8,128)(2,1)}), bf16[64,8,1792]{2,1,0:T(8,128)(2,1)}, u32[]{:S(2)}, u32[]{:S(2)}) %all-to-all-start.3) | async-done | bytes 1835040 | tf_op jit(solution)/shard_map/all_to_all | solution.py:580
  322.8 1.8 convert_reduce_fusion.3
  324.7 1.7 collective-permute-start.14
  (198 shorter events, 51.8 us)
Async XLA Ops:
  7.2 10.5 %copy-start = (f32[2,3,24]{2,0,1:T(2,128)S(1)}, f32[2,3,24]{2,0,1:T(2,128)}, u32[]{:S(2)}) copy-start(f32[2,3,24]{2,0,1:T(2,128)} %param.18) | copy-start | bytes 1732
  7.2 11.3 %copy-start.2 = (bf16[1,256,768]{2,1,0:T(8,128)(2,1)S(1)}, bf16[1,256,768]{2,1,0:T(8,128)(2,1)}, u32[]{:S(2)}) copy-start(bf16[1,256,768]{2,1,0:T(8,128)(2,1)} %param.10) | copy-start | bytes 1179652
  7.2 91.5 %all-gather.2.cloned.1.call-start = ((), (), s32[]{:S(2)}) async-start(), calls=%async_computation.4 | async-start | bytes 8519680 | tf_op jit(solution)/shard_map/all_gather | solution.py:740
  8.2 7.3 %collective-permute-start = (bf16[2,6,3352]{2,1,0:T(8,128)(2,1)S(1)}, bf16[2,6,3352]{2,1,0:T(8,128)(2,1)S(1)}, u32[]{:S(2)}, u32[]{:S(2)}) collective-permute-start(bf16[2,6,3352]{2,1,0:T(8,128)(2,1)S(1)} %copy.113), channel_id=1, source_target_pairs={{0,1},{1,0},{2,3},{3,2},{4,5},{5,4},{6,7},{7,6},{8,9},{9,8},{10,11... | collective-permute-start | bytes 241352 | tf_op jit(solution)/shard_map/ppermute | solution.py:493
  12.4 1.4 collective-permute-start.1
  13.3 1.4 collective-permute-start.2
  101.9 3.6 %collective-permute-start.3 = (bf16[2,768,384]{2,1,0:T(8,128)(2,1)}, bf16[2,768,384]{2,1,0:T(8,128)(2,1)}, u32[]{:S(2)}, u32[]{:S(2)}) collective-permute-start(bf16[2,768,384]{2,1,0:T(8,128)(2,1)} %constant_dynamic-slice_fusion.13), channel_id=1, source_target_pairs={{0,1},{1,0},{2,3},{3,2},{4,5},{5,4},{6,7},{7,6},{8,9},{9,8},{10,11... | collective-permute-start | bytes 3538952 | tf_op jit(solution)/shard_map/ppermute | solution.py:493
  123.2 3.6 %copy-start.7 = (bf16[512,768]{1,0:T(8,128)(2,1)S(1)}, bf16[512,768]{1,0:T(8,128)(2,1)}, u32[]{:S(2)}) copy-start(bf16[512,768]{1,0:T(8,128)(2,1)} %get-tuple-element.60) | copy-start | bytes 2359300
  123.2 1.8 collective-permute-start.4
  124.6 2.1 collective-permute-start.5
  126.7 3.9 %copy-start.9 = (bf16[256,768]{1,0:T(8,128)(2,1)}, bf16[256,768]{1,0:T(8,128)(2,1)S(1)}, u32[]{:S(2)}) copy-start(bf16[256,768]{1,0:T(8,128)(2,1)S(1)} %collective-permute-done.5) | copy-start | bytes 1179652
  144.9 3.3 copy-start.3
  144.9 3.3 copy-start.18
  144.9 2.0 collective-permute-start.6
  146.4 1.8 collective-permute-start.7
  161.2 3.5 %copy-start.15 = (bf16[512,1152]{1,0:T(8,128)(2,1)S(1)}, bf16[512,1152]{1,0:T(8,128)(2,1)}, u32[]{:S(2)}) copy-start(bf16[512,1152]{1,0:T(8,128)(2,1)} %get-tuple-element.73) | copy-start | bytes 3538948
  161.2 2.1 collective-permute-start.8
  166.3 39.4 %all-to-all-start = ((bf16[64,8,2304]{2,1,0:T(8,128)(2,1)}), bf16[64,8,2304]{2,1,0:T(8,128)(2,1)S(1)}, u32[]{:S(2)}, u32[]{:S(2)}) async-start(bf16[64,8,2304]{2,1,0:T(8,128)(2,1)} %pad_maximum_fusion), calls=%async_computation | async-start | bytes 4718592 | tf_op jit(solution)/shard_map/all_to_all | solution.py:580
  208.6 9.1 %collective-permute-start.9 = (bf16[256,768]{1,0:T(8,128)(2,1)}, bf16[256,768]{1,0:T(8,128)(2,1)}, u32[]{:S(2)}, u32[]{:S(2)}) collective-permute-start(bf16[256,768]{1,0:T(8,128)(2,1)} %constant_dynamic-slice_fusion.9), channel_id=1, source_target_pairs={{0,1},{1,0},{2,3},{3,2},{4,5},{5,4},{6,7},{7,6},{8,9},{9,8},{10,11... | collective-permute-start | bytes 1179656 | tf_op jit(solution)/shard_map/ppermute | solution.py:493
  210.8 32.9 %all-to-all-start.1 = ((bf16[64,8,1792]{2,1,0:T(8,128)(2,1)}), bf16[64,8,1792]{2,1,0:T(8,128)(2,1)}, u32[]{:S(2)}, u32[]{:S(2)}) async-start(bf16[64,8,1792]{2,1,0:T(8,128)(2,1)} %bitcast.106), calls=%async_computation.1 | async-start | bytes 3670016 | tf_op jit(solution)/shard_map/all_to_all | solution.py:580
  235.6 2.2 collective-permute-start.10
  237.0 2.3 copy-start.14
  245.5 38.2 %all-to-all-start.2 = ((bf16[64,8,2304]{2,1,0:T(8,128)(2,1)}), bf16[64,8,2304]{2,1,0:T(8,128)(2,1)S(1)}, u32[]{:S(2)}, u32[]{:S(2)}) async-start(bf16[64,8,2304]{2,1,0:T(8,128)(2,1)} %pad_maximum_fusion.1), calls=%async_computation.2 | async-start | bytes 4718592 | tf_op jit(solution)/shard_map/all_to_all | solution.py:580
  286.6 13.3 %collective-permute-start.11 = (bf16[256,768]{1,0:T(8,128)(2,1)}, bf16[256,768]{1,0:T(8,128)(2,1)}, u32[]{:S(2)}, u32[]{:S(2)}) collective-permute-start(bf16[256,768]{1,0:T(8,128)(2,1)} %constant_dynamic-slice_fusion.7), channel_id=1, source_target_pairs={{0,1},{1,0},{2,3},{3,2},{4,5},{5,4},{6,7},{7,6},{8,9},{9,8},{10,11... | collective-permute-start | bytes 1179656 | tf_op jit(solution)/shard_map/ppermute | solution.py:493
  289.1 33.7 %all-to-all-start.3 = ((bf16[64,8,1792]{2,1,0:T(8,128)(2,1)}), bf16[64,8,1792]{2,1,0:T(8,128)(2,1)}, u32[]{:S(2)}, u32[]{:S(2)}) async-start(bf16[64,8,1792]{2,1,0:T(8,128)(2,1)} %bitcast.107), calls=%async_computation.3 | async-start | bytes 3670016 | tf_op jit(solution)/shard_map/all_to_all | solution.py:580
  297.0 3.0 copy-start.6
  297.3 3.8 %copy-start.5 = (f32[256,768]{1,0:T(8,128)S(1)}, f32[256,768]{1,0:T(8,128)}, u32[]{:S(2)}) copy-start(f32[256,768]{1,0:T(8,128)} %get-tuple-element.148) | copy-start | bytes 2359300
  297.9 1.3 collective-permute-start.13
  301.2 23.4 %copy-start.11 = (f32[1,8,1792]{2,1,0:T(8,128)S(1)}, f32[1,8,1792]{2,1,0:T(8,128)}, u32[]{:S(2)}) copy-start(f32[1,8,1792]{2,1,0:T(8,128)} %select_bitcast_fusion.1) | copy-start | bytes 172036
  322.8 8.9 %copy-start.1 = (f32[2,3,24]{2,0,1:T(2,128)S(1)}, f32[2,3,24]{2,0,1:T(2,128)}, u32[]{:S(2)}) copy-start(f32[2,3,24]{2,0,1:T(2,128)} %param.18) | copy-start | bytes 1732
  324.7 2.5 collective-permute-start.14
  326.5 4.3 %collective-permute-start.12 = (f32[2,6,1920]{2,1,0:T(8,128)S(1)}, f32[2,6,1920]{2,1,0:T(8,128)S(1)}, u32[]{:S(2)}, u32[]{:S(2)}) collective-permute-start(f32[2,6,1920]{2,1,0:T(8,128)S(1)} %constant_dynamic-slice_fusion.6), channel_id=1, source_target_pairs={{0,1},{1,0},{2,3},{3,2},{4,5},{5,4},{6,7},{7,6},{8,9},{9,8},{10,11... | collective-permute-start | bytes 276488 | tf_op jit(solution)/shard_map/ppermute | solution.py:493
  (9 other events, 12.3 us)
Sparse Core Ops, SparseCore 0:
  17.8 80.8 all-gather.1

commit v6 on v5

--- a/solution.py
+++ b/solution.py
@@ -166,6 +166,15 @@
     return jnp.where(iota((8, 1), 0) == row, values, 0.0)
 
 
+def column_halves(core_ref):
+    half = WIDTH // 2
+    core = core_ref[0]
+    return (
+        pl.ds(pl.multiple_of(core * half, 128), half),
+        pl.ds(pl.multiple_of((1 - core) * half, 128), half),
+    )
+
+
 def fetched(source, target, semaphore, layer, columns):
     start = layer * LAYER_COLS
     return pltpu.make_async_copy(source.at[:, start : start + columns], target, semaphore)
@@ -179,7 +188,7 @@
 
 
 def forward_kernel(
-    layer, xhat_ref, weights_ref, wout_ref, segc_ref, segr_ref, heads_ref, maps_ref,
+    layer, core_ref, xhat_ref, weights_ref, wout_ref, wother_ref, segc_ref, segr_ref, heads_ref, maps_ref,
     gate_ref, rest_ref, y_ref, out_ref, square_ref, taps_ref, norm_ref, gain_ref,
     win_ref, dtx_ref, affinity_ref, bias_ref, semaphore,
 ):
@@ -237,7 +246,10 @@
             y_ref[rows, lanes] = total
     gate = gate_ref[...]
     gated = y_ref[...] * (gate * jax.nn.sigmoid(gate))
-    out_ref[...] = dot((gated * gain).astype(BF16), wout_ref[...]).astype(out_ref.dtype)
+    outgoing = (gated * gain).astype(BF16)
+    own, other = column_halves(core_ref)
+    out_ref[:, own] = dot(outgoing, wout_ref[...]).astype(BF16)
+    out_ref[:, other] = dot(outgoing, wother_ref[...]).astype(BF16)
     square_ref[...] = jnp.broadcast_to(
         jnp.sum(gated * gated, axis=1, keepdims=True), square_ref.shape
     )
@@ -248,14 +260,17 @@
     return pl.CostEstimate(flops=flops, bytes_accessed=bytes_accessed, transcendentals=0)
 
 
+SCALAR = pl.BlockSpec(memory_space=pltpu.SMEM)
+
+
 def vmem(count):
     return [pl.BlockSpec(memory_space=pltpu.VMEM)] * count
 
 
-def forward_mix(layer, xhat, weights, wout, segc, segr, heads, maps, interpret=False):
+def forward_mix(layer, core, xhat, weights, wout, segc, segr, heads, maps, interpret=False):
     return pl.pallas_call(
         functools.partial(forward_kernel, layer),
-        in_specs=vmem(1) + [pl.BlockSpec(memory_space=pl.ANY)] + vmem(5),
+        in_specs=[SCALAR] + vmem(1) + [pl.BlockSpec(memory_space=pl.ANY)] + vmem(6),
         out_shape=(
             jax.ShapeDtypeStruct((TOKENS, OWN), F32),
             jax.ShapeDtypeStruct((TOKENS, REST), F32),
@@ -276,14 +291,16 @@
         compiler_params=pltpu.CompilerParams(vmem_limit_bytes=58 * 2**20),
         cost_estimate=cost(15),
         interpret=interpret,
-    )(xhat, weights, wout, segc, segr, heads, maps)
+    )(core, xhat, weights, *wout, segc, segr, heads, maps)
 
 
 def gate_kernel(
-    seed_ref, rho_ref, xhat_ref, norm_ref, wout_ref, gate_ref, y_ref, gain_ref, after_ref,
-    dgate_ref, dy_ref, dwin_ref, dwout_ref, dgain_ref,
+    core_ref, seed_ref, rho_ref, xhat_ref, norm_ref, wout_ref, wother_ref, gate_ref, y_ref,
+    gain_ref, after_ref, dgate_ref, dy_ref, dwin_ref, dwout_ref, dwother_ref, dgain_ref,
 ):
-    seed = seed_ref[:, :WIDTH]
+    own, other = column_halves(core_ref)
+    seed_own = seed_ref[:, own]
+    seed_other = seed_ref[:, other]
     mean = seed_ref[:, WIDTH : WIDTH + 128].astype(F32)
     mean = mean[:, 0:1] + mean[:, 1:2]
     gain = gain_ref[0:1]
@@ -293,8 +310,10 @@
     open_gate = jax.nn.sigmoid(gate)
     passed = gate * open_gate
     scaled = y * passed * rho
-    dyn = dot_nt(seed, wout_ref[...])
-    dwout_ref[...] = dot_tn((scaled * gain).astype(BF16), seed).astype(BF16)
+    dyn = dot_nt(seed_own, wout_ref[...]) + dot_nt(seed_other, wother_ref[...])
+    outgoing = (scaled * gain).astype(BF16)
+    dwout_ref[...] = dot_tn(outgoing, seed_own).astype(BF16)
+    dwother_ref[...] = dot_tn(outgoing, seed_other).astype(BF16)
     dgain_ref[...] = jnp.broadcast_to(jnp.sum(dyn * scaled, axis=0, keepdims=True), dgain_ref.shape)
     dgated = rho * (dyn * gain - scaled * mean)
     dy_ref[...] = dgated * passed
@@ -306,20 +325,22 @@
     dwin_ref[:, OWN:] = folded.astype(BF16)
 
 
-def gate_back(seed, rho, xhat, norm, wout, gate, y, gain, after, interpret=False):
+def gate_back(core, seed, rho, xhat, norm, wout, gate, y, gain, after, interpret=False):
     return pl.pallas_call(
         gate_kernel,
+        in_specs=[SCALAR] + vmem(10),
         out_shape=(
             jax.ShapeDtypeStruct((TOKENS, OWN), BF16),
             jax.ShapeDtypeStruct((TOKENS, OWN), F32),
             jax.ShapeDtypeStruct((512, GATE_COLS), BF16),
-            jax.ShapeDtypeStruct((OWN, WIDTH), BF16),
+            jax.ShapeDtypeStruct((OWN, WIDTH // 2), BF16),
+            jax.ShapeDtypeStruct((OWN, WIDTH // 2), BF16),
             jax.ShapeDtypeStruct((8, OWN), F32),
         ),
         compiler_params=pltpu.CompilerParams(vmem_limit_bytes=58 * 2**20),
         cost_estimate=cost(8),
         interpret=interpret,
-    )(seed, rho, xhat, norm, wout, gate, y, gain, after)
+    )(core, seed, rho, xhat, norm, *wout, gate, y, gain, after)
 
 
 def backward_kernel(
@@ -558,7 +579,8 @@
     wout = gathered.reshape(CHIPS, 8, LAYERS, LAYER_COLS)[:, :, :, WIN_COLS:]
     wout = wout.reshape(CHIPS, 8, LAYERS, 3, WIDTH // 2).transpose(2, 0, 3, 1, 4)
     wout = wout.reshape(LAYERS, INNER, WIDTH // 2)
-    return in_order(core, part(wout, core, OWN, 1), swapped(part(wout, 1 - core, OWN, 1)), 2)
+    own, other = part(wout, core, OWN, 1), swapped(part(wout, 1 - core, OWN, 1))
+    return [(own[layer], other[layer]) for layer in range(LAYERS)]
 
 
 def vector_maps(core):
@@ -584,10 +606,9 @@
     return total, arrived[0, :1, :1].astype(F32)
 
 
-def reduced_gate(dwin, dwout, core, earlier):
+def reduced_gate(dwin, dwout, dwother, core, earlier):
     half = WIDTH // 2
-    dwout = in_order(core, part(dwout, core, half, 1), swapped(part(dwout, 1 - core, half, 1)), 0)
-    dwout = dwout.reshape(CHIPS, 3, 8, half).transpose(0, 2, 1, 3)
+    dwout = in_order(core, dwout, swapped(dwother), 0).reshape(CHIPS, 3, 8, half).transpose(0, 2, 1, 3)
     dwin = dwin.reshape(CHIPS, 8, GATE_COLS)
     packed = jnp.concatenate([dwin, dwout.reshape(CHIPS, 8, OUT_COLS)], axis=2)
     return reduced(packed, earlier)
@@ -667,6 +688,7 @@
     segc = segments.reshape(TOKENS, 1)
     heads_all = padded(part(head_values, core, OWN_HEADS, 2), (LAYERS, 8, 128))
     maps = vector_maps(core)
+    place = core.astype(jnp.int32).reshape(1)
     current = hidden.astype(F32)
     saved = []
     for layer in range(LAYERS):
@@ -678,7 +700,7 @@
             )
             wouts = output_weights(weights, core)
         gate, rest, y, out, square, taps, norm, gain = forward_mix(
-            layer, xhat, weights, wouts[layer], segc, segr, heads_all[layer], maps,
+            layer, place, xhat, weights, wouts[layer], segc, segr, heads_all[layer], maps,
             interpret=interpret,
         )
         square = square + swapped(square)
@@ -699,10 +721,10 @@
         means = jnp.concatenate([high, mean - high], axis=1).astype(BF16)
         seed = jnp.concatenate([seed, padded(means, (HALF, 128))], axis=1)
         seed = lax.all_gather(seed, "seq", axis=0, tiled=True)
-        dgate, dy, dwin_gate, dwout, dgain = gate_back(
-            seed, rho, xhat, norm, wouts[layer], gate, y, gain, after[0], interpret=interpret
+        dgate, dy, dwin_gate, dwout, dwother, dgain = gate_back(
+            place, seed, rho, xhat, norm, wouts[layer], gate, y, gain, after[0], interpret=interpret
         )
-        early, arrived = reduced_gate(dwin_gate, dwout, core, arrived)
+        early, arrived = reduced_gate(dwin_gate, dwout, dwother, core, arrived)
         after_early = arrived
         dscaled, dwin_rest = backward_mix(
             layer, dgate, dy, xhat, norm, weights, rest, segc, segr, taps, heads_all[layer],

time: 343 us -> 344 us (level)
    squeeze x0 -> x2, local copies, waits for them, and re-layouts: none -> 3.6 us  [output_weights(): return [(own[layer], other[layer]) for layer in range(LAYERS)]]
    dynamic_slice x14 -> x12, local copies, waits for them, and re-layouts: 10.6 us -> 8.36 us  [part(): return lax.dynamic_slice_in_dim(v, index * size, size, axis)]
  transfers between devices with their start and end apart: 20 -> 20, of which waited for: 14 -> 14; matrix products, arithmetic and copies ran while one was open for 10% -> 10% of each run, Pallas kernels for 18% -> 19%
where the time goes in v6:
time: 344 us; the launch traced here: 340 us
  waiting for transfers between devices  110 us (32%)
  Pallas kernels  101 us (29%)
  starting transfers between devices  42 us (12%)
  other arithmetic  32.1 us (9%)
  local copies, waits for them, and re-layouts  27.4 us (8%)
  between operations  16.9 us (5%)
  blocking collectives  10.6 us (3%)
    all_gather x1, waiting for transfers between devices, per_device(): weights = lax.all_gather(block, DP, axis=0, tiled=True)  77.3 us
    pallas_call x2, Pallas kernels, backward_mix(): pl.pallas_call(functools.partial(backward_kernel, layer), in_specs=vmem(4...  54.6 us
    all_to_all x4, starting transfers between devices, reduced(): arrived = lax.all_to_all(packed, DP, 0, 0, tiled=True)  30.6 us
    pallas_call x2, Pallas kernels, forward_mix(): pl.pallas_call(functools.partial(forward_kernel, layer), in_specs=[SCALAR...  28.4 us
    all_to_all x4, waiting for transfers between devices, reduced(): arrived = lax.all_to_all(packed, DP, 0, 0, tiled=True)  26.8 us
    pallas_call x2, Pallas kernels, gate_back(): pl.pallas_call(gate_kernel, in_specs=[SCALAR] + vmem(10), out_shape=(jax....  17.6 us
    ppermute x15, starting transfers between devices, swapped(): return lax.ppermute(v, 'seq', [(0, 1), (1, 0)])  11.3 us
    dynamic_slice x12, local copies, waits for them, and re-layouts, part(): return lax.dynamic_slice_in_dim(v, index * size, size, axis)  8.36 us
  transfers between devices with their start and end apart: 20, of which 14 were waited for; matrix products, arithmetic and copies ran while one was open for 10% of the time, Pallas kernels for 19%

profile of v6, /device:TPU:1, one launch (start us, length us, event | category | flops | bytes accessed | tf_op | source)
XLA Modules:
  0.0 339.8 jit_solution(1925825903340589192)
XLA Ops:
  18.9 2.5 all_gather.16.xhat_ref
  21.4 77.3 %all-gather.2.cloned.1.call-done.weights_ref = bf16[512,8192]{1,0:T(8,128)(2,1)} async-done(((bf16[8,8192]{1,0:T(8,128)(2,1)}), bf16[512,8192]{1,0:T(8,128)(2,1)}) %all-gather.2.cloned.1.call-update) | async-done | bytes 8388624 | tf_op jit(solution)/shard_map/all_gather | solution.py:762
  98.7 1.8 slice.230
  105.6 2.4 slice_bitcast_fusion
  108.0 14.2 %shard_map.169 = (f32[512,768]{1,0:T(8,128)}, f32[512,1152]{1,0:T(8,128)}, f32[512,768]{1,0:T(8,128)}, bf16[512,768]{1,0:T(8,128)(2,1)}, f32[512,128]{1,0:T(8,12...) custom-call(s32[1]{0:T(128)} %bitcast.1.core_ref, bf16[512,768]{1,0:T(8,128)(2,1)} %all_gather.16.xhat_ref, ...), custom_call_target="tpu_custom_call" | custom-call | flops 16499999744 | bytes 54000000 | tf_op jit(solution)/shard_map/pallas_call | solution.py:271
  127.9 2.9 all_gather.17.xhat_ref
  130.8 14.2 %shard_map.170 = (f32[512,768]{1,0:T(8,128)}, f32[512,1152]{1,0:T(8,128)}, f32[512,768]{1,0:T(8,128)}, bf16[512,768]{1,0:T(8,128)(2,1)}, f32[512,128]{1,0:T(8,12...) custom-call(s32[1]{0:T(128)} %bitcast.1.core_ref, bf16[512,768]{1,0:T(8,128)(2,1)} %all_gather.17.xhat_ref, ...), custom_call_target="tpu_custom_call" | custom-call | flops 16499999744 | bytes 54000000 | tf_op jit(solution)/shard_map/pallas_call | solution.py:271
  148.3 2.0 fusion
  150.7 2.6 all_gather.18.seed_ref
  153.3 8.8 %shard_map.171 = (bf16[512,768]{1,0:T(8,128)(2,1)}, f32[512,768]{1,0:T(8,128)}, bf16[512,1152]{1,0:T(8,128)(2,1)}, bf16[768,384]{1,0:T(8,128)(2,1)}, bf16[768,384]{1,0:T(8,128)(2,1)}, /*index=5*/f32[8,768]{1,0:T(8,128)}) custom-call(s32[1]{0:T(128)} %bitcast.1.core_ref, bf16[512,896]{1,0:T(8,128)(2,1)} %all_gather.18.seed_ref, f32[512,1]{1,0:T(8,128)} %copy-done.12, ...), custom_call_target="tpu_custom_call" | custom-call | flops 8800000000 | bytes 28800000 | tf_op jit(solution)/shard_map/pallas_call | solution.py:329
  162.2 2.1 collective-permute-done.8
  167.3 8.5 %all-to-all-start = ((bf16[64,8,2304]{2,1,0:T(8,128)(2,1)}), bf16[64,8,2304]{2,1,0:T(8,128)(2,1)S(1)}, u32[]{:S(2)}, u32[]{:S(2)}) async-start(bf16[64,8,2304]{2,1,0:T(8,128)(2,1)} %pad_maximum_fusion), calls=%async_computation | async-start | bytes 4718592 | tf_op jit(solution)/shard_map/all_to_all | solution.py:602
  175.8 27.3 %shard_map.172 = (bf16[512,768]{1,0:T(8,128)(2,1)}, bf16[512,1792]{1,0:T(8,128)(2,1)}) custom-call(bf16[512,768]{1,0:T(8,128)(2,1)} %get-tuple-element.69.dgate_ref, f32[512,768]{1,0:T(8,128)} %get-tuple-element.70.dy_ref, bf16[512,768]{1,0:T(8,128)(2,1)} %all_gather.17.xhat_ref, f32[8,768]{1,0:T(8,128)} %get-tuple-element.65.norm_ref, ...), custom_call_target="tpu_custom_call" | custom-call | flops 32999999488 | bytes 108000000 | tf_op jit(solution)/shard_map/pallas_call | solution.py:482
  203.1 3.9 %all-to-all-done = bf16[64,8,2304]{2,1,0:T(8,128)(2,1)S(1)} async-done(((bf16[64,8,2304]{2,1,0:T(8,128)(2,1)}), bf16[64,8,2304]{2,1,0:T(8,128)(2,1)S(1)}, u32[]{:S(2)}, u32[]{:S(2)}) %all-to-all-start) | async-done | bytes 2359328 | tf_op jit(solution)/shard_map/all_to_all | solution.py:602
  208.2 1.8 constant_dynamic-slice_fusion.7
  209.9 1.9 collective-permute-start.9
  211.9 6.7 %all-to-all-start.1 = ((bf16[64,8,1792]{2,1,0:T(8,128)(2,1)}), bf16[64,8,1792]{2,1,0:T(8,128)(2,1)}, u32[]{:S(2)}, u32[]{:S(2)}) async-start(bf16[64,8,1792]{2,1,0:T(8,128)(2,1)} %bitcast.111), calls=%async_computation.1 | async-start | bytes 3670016 | tf_op jit(solution)/shard_map/all_to_all | solution.py:602
  219.9 3.0 multiply_reduce_fusion
  225.1 2.6 all_gather.19.seed_ref
  227.7 8.8 %shard_map.173 = (bf16[512,768]{1,0:T(8,128)(2,1)}, f32[512,768]{1,0:T(8,128)}, bf16[512,1152]{1,0:T(8,128)(2,1)}, bf16[768,384]{1,0:T(8,128)(2,1)}, bf16[768,384]{1,0:T(8,128)(2,1)}, /*index=5*/f32[8,768]{1,0:T(8,128)}) custom-call(s32[1]{0:T(128)} %bitcast.1.core_ref, bf16[512,896]{1,0:T(8,128)(2,1)} %all_gather.19.seed_ref, f32[512,1]{1,0:T(8,128)} %copy-done.11, ...), custom_call_target="tpu_custom_call" | custom-call | flops 8800000000 | bytes 28800000 | tf_op jit(solution)/shard_map/pallas_call | solution.py:329
  240.4 1.6 pad_maximum_fusion.1
  242.0 2.7 all-to-all-done.1
  246.5 7.6 %all-to-all-start.2 = ((bf16[64,8,2304]{2,1,0:T(8,128)(2,1)}), bf16[64,8,2304]{2,1,0:T(8,128)(2,1)S(1)}, u32[]{:S(2)}, u32[]{:S(2)}) async-start(bf16[64,8,2304]{2,1,0:T(8,128)(2,1)} %pad_maximum_fusion.1), calls=%async_computation.2 | async-start | bytes 4718592 | tf_op jit(solution)/shard_map/all_to_all | solution.py:602
  254.1 1.8 convert_reduce_fusion.2
  256.5 27.3 %shard_map.174 = (bf16[512,768]{1,0:T(8,128)(2,1)}, bf16[512,1792]{1,0:T(8,128)(2,1)}) custom-call(bf16[512,768]{1,0:T(8,128)(2,1)} %get-tuple-element.84.dgate_ref, f32[512,768]{1,0:T(8,128)} %get-tuple-element.85.dy_ref, bf16[512,768]{1,0:T(8,128)(2,1)} %all_gather.16.xhat_ref, f32[8,768]{1,0:T(8,128)} %get-tuple-element.80.norm_ref, ...), custom_call_target="tpu_custom_call" | custom-call | flops 32999999488 | bytes 108000000 | tf_op jit(solution)/shard_map/pallas_call | solution.py:482
  285.8 1.8 constant_dynamic-slice_fusion.6
  287.6 2.5 collective-permute-start.11
  290.1 7.8 %all-to-all-start.3 = ((bf16[64,8,1792]{2,1,0:T(8,128)(2,1)}), bf16[64,8,1792]{2,1,0:T(8,128)(2,1)}, u32[]{:S(2)}, u32[]{:S(2)}) async-start(bf16[64,8,1792]{2,1,0:T(8,128)(2,1)} %bitcast.112), calls=%async_computation.3 | async-start | bytes 3670016 | tf_op jit(solution)/shard_map/all_to_all | solution.py:602
  302.3 2.1 fusion.12
  304.5 19.3 %all-to-all-done.3 = bf16[64,8,1792]{2,1,0:T(8,128)(2,1)} async-done(((bf16[64,8,1792]{2,1,0:T(8,128)(2,1)}), bf16[64,8,1792]{2,1,0:T(8,128)(2,1)}, u32[]{:S(2)}, u32[]{:S(2)}) %all-to-all-start.3) | async-done | bytes 1835040 | tf_op jit(solution)/shard_map/all_to_all | solution.py:602
  323.8 1.8 convert_reduce_fusion.3
  325.7 1.7 collective-permute-start.14
  (186 shorter events, 49.6 us)
Async XLA Ops:
  7.2 10.5 %copy-start = (f32[2,3,24]{2,0,1:T(2,128)S(1)}, f32[2,3,24]{2,0,1:T(2,128)}, u32[]{:S(2)}) copy-start(f32[2,3,24]{2,0,1:T(2,128)} %param.18) | copy-start | bytes 1732
  7.2 11.3 %copy-start.2 = (bf16[1,256,768]{2,1,0:T(8,128)(2,1)S(1)}, bf16[1,256,768]{2,1,0:T(8,128)(2,1)}, u32[]{:S(2)}) copy-start(bf16[1,256,768]{2,1,0:T(8,128)(2,1)} %param.10) | copy-start | bytes 1179652
  7.2 91.5 %all-gather.2.cloned.1.call-start = ((), (), s32[]{:S(2)}) async-start(), calls=%async_computation.4 | async-start | bytes 8519680 | tf_op jit(solution)/shard_map/all_gather | solution.py:762
  8.2 7.3 %collective-permute-start = (bf16[2,6,3352]{2,1,0:T(8,128)(2,1)S(1)}, bf16[2,6,3352]{2,1,0:T(8,128)(2,1)S(1)}, u32[]{:S(2)}, u32[]{:S(2)}) collective-permute-start(bf16[2,6,3352]{2,1,0:T(8,128)(2,1)S(1)} %copy.113), channel_id=1, source_target_pairs={{0,1},{1,0},{2,3},{3,2},{4,5},{5,4},{6,7},{7,6},{8,9},{9,8},{10,11... | collective-permute-start | bytes 241352 | tf_op jit(solution)/shard_map/ppermute | solution.py:514
  12.4 1.4 collective-permute-start.1
  13.3 1.4 collective-permute-start.2
  100.8 2.0 copy-start.15
  101.9 3.6 %collective-permute-start.3 = (bf16[2,768,384]{2,1,0:T(8,128)(2,1)}, bf16[2,768,384]{2,1,0:T(8,128)(2,1)}, u32[]{:S(2)}, u32[]{:S(2)}) collective-permute-start(bf16[2,768,384]{2,1,0:T(8,128)(2,1)} %constant_dynamic-slice_fusion.10), channel_id=1, source_target_pairs={{0,1},{1,0},{2,3},{3,2},{4,5},{5,4},{6,7},{7,6},{8,9},{9,8},{10,11... | collective-permute-start | bytes 3538952 | tf_op jit(solution)/shard_map/ppermute | solution.py:514
  122.2 1.8 collective-permute-start.4
  123.7 2.1 collective-permute-start.5
  125.7 5.1 %copy-start.6 = (bf16[256,768]{1,0:T(8,128)(2,1)}, bf16[256,768]{1,0:T(8,128)(2,1)S(1)}, u32[]{:S(2)}) copy-start(bf16[256,768]{1,0:T(8,128)(2,1)S(1)} %collective-permute-done.5) | copy-start | bytes 1179652
  130.8 17.5 %copy-start.3 = (bf16[1,256,768]{2,1,0:T(8,128)(2,1)S(1)}, bf16[1,256,768]{2,1,0:T(8,128)(2,1)}, u32[]{:S(2)}) copy-start(bf16[1,256,768]{2,1,0:T(8,128)(2,1)} %param.19) | copy-start | bytes 1179652
  145.0 1.8 collective-permute-start.6
  146.5 1.8 collective-permute-start.7
  147.9 5.4 %copy-start.12 = (f32[512,1]{1,0:T(8,128)}, f32[512,1]{1,0:T(8,128)S(1)}, u32[]{:S(2)}) copy-start(f32[512,1]{1,0:T(8,128)S(1)} %fusion.15.rho_ref) | copy-start | bytes 6148
  162.1 2.2 collective-permute-start.8
  167.3 39.7 %all-to-all-start = ((bf16[64,8,2304]{2,1,0:T(8,128)(2,1)}), bf16[64,8,2304]{2,1,0:T(8,128)(2,1)S(1)}, u32[]{:S(2)}, u32[]{:S(2)}) async-start(bf16[64,8,2304]{2,1,0:T(8,128)(2,1)} %pad_maximum_fusion), calls=%async_computation | async-start | bytes 4718592 | tf_op jit(solution)/shard_map/all_to_all | solution.py:602
  209.9 8.6 %collective-permute-start.9 = (bf16[256,768]{1,0:T(8,128)(2,1)}, bf16[256,768]{1,0:T(8,128)(2,1)}, u32[]{:S(2)}, u32[]{:S(2)}) collective-permute-start(bf16[256,768]{1,0:T(8,128)(2,1)} %constant_dynamic-slice_fusion.7), channel_id=1, source_target_pairs={{0,1},{1,0},{2,3},{3,2},{4,5},{5,4},{6,7},{7,6},{8,9},{9,8},{10,11... | collective-permute-start | bytes 1179656 | tf_op jit(solution)/shard_map/ppermute | solution.py:514
  211.9 32.8 %all-to-all-start.1 = ((bf16[64,8,1792]{2,1,0:T(8,128)(2,1)}), bf16[64,8,1792]{2,1,0:T(8,128)(2,1)}, u32[]{:S(2)}, u32[]{:S(2)}) async-start(bf16[64,8,1792]{2,1,0:T(8,128)(2,1)} %bitcast.111), calls=%async_computation.1 | async-start | bytes 3670016 | tf_op jit(solution)/shard_map/all_to_all | solution.py:602
  236.5 2.4 copy-start.13
  236.5 2.4 collective-permute-start.10
  238.9 1.5 copy-start.9
  246.5 38.2 %all-to-all-start.2 = ((bf16[64,8,2304]{2,1,0:T(8,128)(2,1)}), bf16[64,8,2304]{2,1,0:T(8,128)(2,1)S(1)}, u32[]{:S(2)}, u32[]{:S(2)}) async-start(bf16[64,8,2304]{2,1,0:T(8,128)(2,1)} %pad_maximum_fusion.1), calls=%async_computation.2 | async-start | bytes 4718592 | tf_op jit(solution)/shard_map/all_to_all | solution.py:602
  287.6 13.3 %collective-permute-start.11 = (bf16[256,768]{1,0:T(8,128)(2,1)}, bf16[256,768]{1,0:T(8,128)(2,1)}, u32[]{:S(2)}, u32[]{:S(2)}) collective-permute-start(bf16[256,768]{1,0:T(8,128)(2,1)} %constant_dynamic-slice_fusion.6), channel_id=1, source_target_pairs={{0,1},{1,0},{2,3},{3,2},{4,5},{5,4},{6,7},{7,6},{8,9},{9,8},{10,11... | collective-permute-start | bytes 1179656 | tf_op jit(solution)/shard_map/ppermute | solution.py:514
  290.1 33.7 %all-to-all-start.3 = ((bf16[64,8,1792]{2,1,0:T(8,128)(2,1)}), bf16[64,8,1792]{2,1,0:T(8,128)(2,1)}, u32[]{:S(2)}, u32[]{:S(2)}) async-start(bf16[64,8,1792]{2,1,0:T(8,128)(2,1)} %bitcast.112), calls=%async_computation.3 | async-start | bytes 3670016 | tf_op jit(solution)/shard_map/all_to_all | solution.py:602
  298.0 4.3 %copy-start.4 = (f32[256,768]{1,0:T(8,128)S(1)}, f32[256,768]{1,0:T(8,128)}, u32[]{:S(2)}) copy-start(f32[256,768]{1,0:T(8,128)} %get-tuple-element.152) | copy-start | bytes 2359300
  298.3 4.0 %copy-start.5 = (bf16[512,768]{1,0:T(8,128)(2,1)S(1)}, bf16[512,768]{1,0:T(8,128)(2,1)}, u32[]{:S(2)}) copy-start(bf16[512,768]{1,0:T(8,128)(2,1)} %get-tuple-element.97) | copy-start | bytes 2359300
  298.9 1.3 collective-permute-start.13
  302.3 23.3 %copy-start.7 = (f32[1,8,1792]{2,1,0:T(8,128)S(1)}, f32[1,8,1792]{2,1,0:T(8,128)}, u32[]{:S(2)}) copy-start(f32[1,8,1792]{2,1,0:T(8,128)} %select_bitcast_fusion.1) | copy-start | bytes 172036
  302.3 30.4 %copy-start.1 = (f32[2,3,24]{2,0,1:T(2,128)S(1)}, f32[2,3,24]{2,0,1:T(2,128)}, u32[]{:S(2)}) copy-start(f32[2,3,24]{2,0,1:T(2,128)} %param.18) | copy-start | bytes 1732
  325.7 2.5 collective-permute-start.14
  327.5 4.3 %collective-permute-start.12 = (f32[2,6,1920]{2,1,0:T(8,128)S(1)}, f32[2,6,1920]{2,1,0:T(8,128)S(1)}, u32[]{:S(2)}, u32[]{:S(2)}) collective-permute-start(f32[2,6,1920]{2,1,0:T(8,128)S(1)} %constant_dynamic-slice_fusion.5), channel_id=1, source_target_pairs={{0,1},{1,0},{2,3},{3,2},{4,5},{5,4},{6,7},{7,6},{8,9},{9,8},{10,11... | collective-permute-start | bytes 276488 | tf_op jit(solution)/shard_map/ppermute | solution.py:514
  (4 other events, 3.7 us)
Sparse Core Ops, SparseCore 0:
  17.8 80.8 all-gather.1
